TPU v7x, 32 devices: a whole 2x2x4 slice. The times are simulated.
32 devices in a mesh: rep: 4 (over y, core), tp: 8 (over z, x).
Axes of the slice: x: 2, y: 2, z: 4, core: 2. Of those that a mesh axis runs over, the one named last changes fastest.
Arguments:
- tokens: bfloat16 [4096, 2048], P(('rep', 'tp')), may hold values from -6 to 6
- seg_ids: int32 [4096], replicated, may hold values from 0 to 15, never falling along the last dimension, each value on 1 to 1024 neighbouring positions
- expert_ids: int32 [4096, 8], P(('rep', 'tp')), may hold values from 0 to 31, all different within a row; in each aligned block of 128 rows (0 to 127, 128 to 255, ...) at most 48 rows name the same one
- gates: bfloat16 [4096, 8], P(('rep', 'tp')), may hold values from 0.099609375 to 0.59765625
- page_table: int32 [256], P(('rep', 'tp')), may hold values from 0 to 7, as said below
- attn_gain: float32 [2048], replicated, may hold values from 0.5 to 1.5
- q_gain: float32 [128], replicated, may hold values from 0.5 to 6, as said below
- key_norm_gain: float32 [128], replicated, may hold values from 0.5 to 6, as said below
- w_query: bfloat16 [2048, 4096], P(None, 'tp'), may hold values from -1 to 1
- w_keyval: bfloat16 [2048, 1024], replicated, may hold values from -1 to 1
- w_out: bfloat16 [4096, 2048], P('tp'), may hold values from -0.09375 to 0.09375
- moe_gain: float32 [2048], replicated, may hold values from 0.5 to 1.5
- w_gate_up: bfloat16 [32, 2048, 1536], P(('rep', 'tp')), may hold values from -0.125 to 0.125
- w_down: bfloat16 [32, 768, 2048], P(('rep', 'tp')), may hold values from -0.21875 to 0.21875
Outputs:
- hidden_out: bfloat16 [4096, 2048], P(('rep', 'tp'))
- cache: bfloat16 [256, 16, 1024], P(('rep', 'tp'))
Inputs may be any that keep to these rules, and one draw needn't show every extreme that they name: `seg_ids`: never falling; each request has at most 1024 tokens and some request has exactly 1024. `expert_ids`: a token's 8 experts differ; in the rows of one device no expert appears more than 48 times. `page_table`: the 8 entries of each device name each of its slots once. `q_gain`: positive. `key_norm_gain`: positive.
All inputs are finite; a program needn't handle non-finite values.
Results may differ from a plain program's by a relative error of at most 0.022.
Values may be sent and summed in bfloat16 or wider, within the bound.
No kernel may reach another device: no remote copies, remote signals or barrier semaphores. Data moves between devices by JAX's collectives and lax.ppermute only.
A program may use at most 128 MiB of HBM per device.

v0:
```python
import math

import jax
import jax.numpy as jnp
from jax import lax
from jax.sharding import PartitionSpec as P


def passed_along(block, axis, distance):
    devices = range(lax.axis_size(axis))
    route = [(i - distance, i) for i in devices if i - distance in devices]
    return lax.ppermute(block, axis, route)


def root_mean_norm(value_rows, gain):
    return (
        value_rows
        * lax.rsqrt(jnp.mean(value_rows * value_rows, axis=-1, keepdims=True) + 1e-06)
        * gain
    )


def apply_rotary(value_rows, token_positions):
    half_dim = value_rows.shape[-1] // 2
    frequency = jnp.exp(
        jnp.arange(half_dim, dtype=jnp.float32)
        * (-2.0 * math.log(1000000.0) / value_rows.shape[-1])
    )
    angles = token_positions[:, None] * frequency[None, :]
    cosine = jnp.cos(angles)[:, None, :]
    sine_part = jnp.sin(angles)[:, None, :]
    first = value_rows[..., :half_dim]
    second = value_rows[..., half_dim:]
    return jnp.concatenate(
        [first * cosine - second * sine_part, second * cosine + first * sine_part], axis=-1
    )


def body(
    tokens,
    seg_ids,
    expert_ids,
    gates,
    page_table,
    attn_gain,
    q_gain,
    key_norm_gain,
    w_query,
    w_keyval,
    w_out,
    moe_gain,
    w_gate_up,
    w_down,
):
    tok_rows, width = tokens.shape
    tp_count = lax.axis_size("tp")
    rep_count = lax.axis_size("rep")
    rep_index = lax.axis_index("rep")
    tp_index = lax.axis_index("tp")
    group_rows = tok_rows * tp_count
    head_dim = q_gain.shape[0]
    q_width = w_query.shape[1]
    heads_here = q_width // head_dim
    kv_heads = w_keyval.shape[1] // (2 * head_dim)
    kv_width = kv_heads * head_dim
    per_key_value = heads_here * tp_count // kv_heads
    own_head = tp_index * heads_here // per_key_value
    first_row = (rep_index * tp_count + tp_index) * tok_rows
    local_pos = (first_row + jnp.arange(tok_rows, dtype=jnp.int32)).astype(jnp.float32)
    normed = root_mean_norm(tokens.astype(jnp.float32), attn_gain).astype(jnp.bfloat16)
    key_value_rows = jnp.dot(normed, w_keyval, preferred_element_type=jnp.float32)
    rotary_output = apply_rotary(
        root_mean_norm(
            key_value_rows[:, :kv_width].reshape(tok_rows, kv_heads, head_dim), key_norm_gain
        ),
        local_pos,
    )
    stored_cache = jnp.concatenate(
        [rotary_output.reshape(tok_rows, kv_width), key_value_rows[:, kv_width:]], axis=1
    ).astype(jnp.bfloat16)
    page_count = page_table.shape[0]
    placement_matrix = (
        page_table[None, :] == jnp.arange(page_count, dtype=jnp.int32)[:, None]
    ).astype(jnp.bfloat16)
    cache = jnp.dot(
        placement_matrix, stored_cache.reshape(page_count, -1), preferred_element_type=jnp.float32
    )
    cache = cache.astype(jnp.bfloat16).reshape(page_count, tok_rows // page_count, 2 * kv_width)
    projected = jnp.dot(
        lax.all_gather(normed, "tp", axis=0, tiled=True),
        w_query,
        preferred_element_type=jnp.float32,
    )
    group_start = rep_index * group_rows
    group_pos = group_start + jnp.arange(group_rows, dtype=jnp.int32)
    group_posf = group_pos.astype(jnp.float32)
    query = root_mean_norm(projected.reshape(group_rows, heads_here, head_dim), q_gain)
    query = apply_rotary(query, group_posf).astype(jnp.bfloat16)
    gathered = lax.all_gather(stored_cache, "tp", axis=0, tiled=True)
    own_keys = lax.dynamic_slice_in_dim(gathered, own_head * head_dim, head_dim, 1)
    own_values = lax.dynamic_slice_in_dim(gathered, kv_width + own_head * head_dim, head_dim, 1)
    earlier_keys, earlier_values = passed_along((own_keys, own_values), "rep", 1)
    own_seg = lax.dynamic_slice_in_dim(seg_ids, group_start, group_rows, 0)
    earlier_seg = lax.dynamic_slice_in_dim(
        seg_ids, jnp.maximum(group_start - group_rows, 0), group_rows, 0
    )
    earlier_seg = jnp.where(rep_index > 0, earlier_seg, -1)
    keys_all = jnp.concatenate([earlier_keys, own_keys], axis=0)
    values_all = jnp.concatenate([earlier_values, own_values], axis=0)
    key_seg = jnp.concatenate([earlier_seg, own_seg], axis=0)
    key_pos = group_start - group_rows + jnp.arange(2 * group_rows, dtype=jnp.int32)
    block_rows = min(512, group_rows)
    block_count = group_rows // block_rows
    scale = head_dim ** (-0.5)

    def attend(inputs):
        block_query, block_pos, block_seg = inputs
        scores = (
            jnp.einsum("bhd,kd->hbk", block_query, keys_all, preferred_element_type=jnp.float32)
            * scale
        )
        allowed = (key_seg[None, :] == block_seg[:, None]) & (
            key_pos[None, :] <= block_pos[:, None]
        )
        scores = jnp.where(allowed[None], scores, -jnp.inf)
        largest = jnp.max(scores, axis=-1, keepdims=True)
        weights = jnp.exp(scores - largest)
        totals = jnp.sum(weights, axis=-1, keepdims=True)
        mixed = (
            jnp.einsum(
                "hbk,kd->hbd",
                weights.astype(jnp.bfloat16),
                values_all,
                preferred_element_type=jnp.float32,
            )
            / totals
        )
        return jnp.transpose(mixed.astype(jnp.bfloat16), (1, 0, 2)).reshape(
            block_rows, heads_here * head_dim
        )

    attended = lax.map(
        attend,
        (
            query.reshape(block_count, block_rows, heads_here, head_dim),
            group_pos.reshape(block_count, block_rows),
            own_seg.reshape(block_count, block_rows),
        ),
    )
    attended = attended.reshape(group_rows, heads_here * head_dim)
    rows = attended
    term = jnp.dot(rows, w_out, preferred_element_type=jnp.float32).astype(jnp.bfloat16)
    mixed_sum = lax.psum_scatter(
        lax.optimization_barrier(term).astype(jnp.float32).astype(jnp.bfloat16),
        "tp",
        scatter_dimension=0,
        tiled=True,
    ).astype(jnp.float32)
    residual = (tokens.astype(jnp.float32) + mixed_sum).astype(jnp.bfloat16)
    normed_moe = root_mean_norm(residual.astype(jnp.float32), moe_gain).astype(jnp.bfloat16)
    expert_count = rep_count * tp_count * w_gate_up.shape[0]
    top_count = expert_ids.shape[1]
    capacity = max(2, 3 * tok_rows * top_count // (2 * expert_count))
    hidden_units = w_down.shape[1]
    flat = expert_ids.reshape(-1)
    onehot = (flat[:, None] == jnp.arange(expert_count, dtype=jnp.int32)[None, :]).astype(jnp.int32)
    rank = jnp.sum((jnp.cumsum(onehot, axis=0) - 1) * onehot, axis=1)
    target = (flat * capacity + rank).reshape(tok_rows, top_count)
    match = (
        target[:, :, None] == jnp.arange(expert_count * capacity, dtype=jnp.int32)[None, None, :]
    )
    dispatch = jnp.any(match, axis=1).astype(jnp.bfloat16)
    combine = jnp.sum(jnp.where(match, gates[:, :, None].astype(jnp.float32), 0.0), axis=1).astype(
        jnp.bfloat16
    )
    outgoing = lax.dot_general(
        dispatch, normed_moe, (((0,), (0,)), ((), ())), preferred_element_type=jnp.float32
    )
    outgoing = outgoing.astype(jnp.bfloat16).reshape(expert_count, capacity, width)
    received = lax.all_to_all(outgoing, ("rep", "tp"), split_axis=0, concat_axis=0, tiled=True)
    rows = received.reshape(-1, width)
    gate_up = jnp.dot(rows, w_gate_up[0], preferred_element_type=jnp.float32)
    act = (jax.nn.silu(gate_up[:, :hidden_units]) * gate_up[:, hidden_units:]).astype(jnp.bfloat16)
    result = jnp.dot(act, w_down[0], preferred_element_type=jnp.float32).astype(jnp.bfloat16)
    returned = lax.all_to_all(
        result.reshape(received.shape), ("rep", "tp"), split_axis=0, concat_axis=0, tiled=True
    )
    combined = jnp.dot(
        combine,
        returned.reshape(expert_count * capacity, width),
        preferred_element_type=jnp.float32,
    )
    hidden_out = (residual.astype(jnp.float32) + combined).astype(jnp.bfloat16)
    return (hidden_out, cache)


def solution(mesh):
    in_specs = (
        P(("rep", "tp"), None),
        P(),
        P(("rep", "tp"), None),
        P(("rep", "tp"), None),
        P(("rep", "tp")),
        P(),
        P(),
        P(),
        P(None, "tp"),
        P(),
        P("tp", None),
        P(),
        P(("rep", "tp"), None, None),
        P(("rep", "tp"), None, None),
    )
    out_specs = (P(("rep", "tp"), None), P(("rep", "tp"), None, None))
    return jax.shard_map(body, mesh=mesh, in_specs=in_specs, out_specs=out_specs, check_vma=False)
```

profile of v0, /device:TPU:0, one launch (start us, length us, event | category | flops | bytes accessed | tf_op | source)
XLA Modules:
  0.0 618.4 jit_solution(2007581520442255707)
XLA Ops:
  7.8 1.5 fusion.29
  9.3 2.0 fusion.31
  11.3 3.1 fusion.46
  15.8 1.0 reshape.285
  17.0 1.0 multiply_cosine_fusion.1
  21.0 2.4 multiply_cosine_fusion
  23.4 48.9 %all-gather.5.cloned.1.call-done = bf16[1024,1024]{1,0:T(8,128)(2,1)} async-done(((bf16[128,1024]{1,0:T(8,128)(2,1)}), bf16[1024,1024]{1,0:T(8,128)(2,1)}) %all-gather.5.cloned.1.call-update) | async-done | bytes 2097168 | tf_op jit(solution)/shard_map/all_gather | solution.py:99
  72.3 1.9 constant_dynamic-slice_fusion.2
  74.2 2.0 collective-permute-start.1
  76.3 4.1 collective-permute-start
  80.4 1.9 pad_maximum_fusion.2
  82.3 2.1 copy.57
  84.4 1.9 pad_maximum_fusion.1
  86.3 60.6 %all-gather.3.cloned.1.call-done = bf16[1024,2048]{1,0:T(8,128)(2,1)} async-done(((bf16[128,2048]{1,0:T(8,128)(2,1)}), bf16[1024,2048]{1,0:T(8,128)(2,1)}) %all-gather.3.cloned.1.call-update) | async-done | bytes 4194320 | tf_op jit(solution)/shard_map/all_gather | solution.py:90
  146.9 5.3 multiply_reduce_fusion
  152.7 1.3 subtract_convert_fusion
  154.0 2.2 concatenate.25
  156.2 2.2 concatenate.26
  158.5 3.6 pad_maximum_fusion
  162.0 3.7 copy.56
  165.7 38.7 %while.11 = (s32[]{:T(128)}, bf16[2,512,512]{2,1,0:T(8,128)(2,1)}, s32[2048]{0:T(1024)S(1)}, s32[2,512]{1,0:T(2,128)S(1)}, s32[2,512]{1,0:T(2,128)S(1)}, /*index...) while((s32[]{:T(128)}, bf16[2,512,512]{2,1,0:T(8,128)(2,1)}, ...), condition=%wide.region_6.7_spmd.clone, body=%wide.region_3.6_spmd.clone.sunk | while | flops 2197288960 | bytes 60896392 | solution.py:142
  165.7 0.9 compare_and_fusion.2
  166.7 4.6 bitcast_reduce_fusion.2
  171.2 4.4 fusion.63
  175.7 5.5 divide_convert_fusion.2
  181.1 2.1 copy.76
  183.2 1.9 constant_dynamic-update-slice_fusion.2
  185.1 0.9 compare_and_fusion.2
  186.0 4.6 bitcast_reduce_fusion.2
  190.6 4.4 fusion.63
  195.0 5.5 divide_convert_fusion.2
  200.5 2.1 copy.76
  202.5 1.9 constant_dynamic-update-slice_fusion.2
  204.4 6.2 %convolution_convert_fusion.3 = bf16[1024,2048]{1,0:T(8,128)(2,1)} fusion(bf16[1024,512]{1,0:T(8,128)(2,1)} %bitcast.119, bf16[512,2048]{1,0:T(8,128)(2,1)} %param.26), kind=kOutput, calls=%fused_computation.34 | convolution fusion | flops 2149580800 | bytes 7340032 | tf_op jit(solution)/shard_map/dot_general | solution.py:152
  211.0 9.0 %reduce-window.6 = s32[32,8,128]{2,1,0:T(8,128)S(1)} reduce-window(s32[32,8,128]{2,1,0:T(8,128)S(1)} %fusion.42, s32[]{:T(128)} %constant.45.clone.1), window={size=1x1x128 pad=0_0x0_0x127_0}, to_apply=%region_8.9 | reduce-window | flops 4161536 | bytes 262148 | tf_op jit(solution)/shard_map/reduce-window
  220.8 3.1 fusion.23
  223.9 73.3 %reduce-scatter.2.cloned.1.call-done = bf16[128,2048]{1,0:T(8,128)(2,1)} async-done(((bf16[1024,2048]{1,0:T(8,128)(2,1)}), bf16[128,2048]{1,0:T(8,128)(2,1)}) %reduce-scatter.2.cloned.1.call-update) | async-done | bytes 524304 | tf_op jit(solution)/shard_map/reduce_scatter | solution.py:153
  297.2 1.5 fusion.33
  298.7 3.2 convolution_convert_fusion.2
  302.0 144.1 %all_to_all.10 = bf16[32,48,2048]{2,1,0:T(8,128)(2,1)S(1)} all-to-all(bf16[32,48,2048]{2,1,0:T(8,128)(2,1)S(1)} %bitcast.105), channel_id=1, replica_groups=mesh['rep'=4,'tp'=8] {'rep','tp'}, dimensions={0} | all-to-all | bytes 12582912 | tf_op jit(solution)/shard_map/all_to_all | solution.py:180
  446.1 10.0 %fusion.21 = f32[1536,1536]{1,0:T(8,128)S(1)} fusion(bf16[1536,2048]{1,0:T(8,128)(2,1)S(1)} %bitcast.108, bf16[1,2048,1536]{2,1,0:T(8,128)(2,1)S(1)} %bitcast.118), kind=kOutput, calls=%fused_computation.27 | convolution fusion | flops 9663676416 | bytes 22020096 | tf_op jit(solution)/shard_map/dot_general | solution.py:182
  456.1 7.0 %convolution_convert_fusion.1 = bf16[1536,2048]{1,0:T(8,128)(2,1)} fusion(bf16[1,768,2048]{2,1,0:T(8,128)(2,1)S(1)} %copy-done, f32[1536,1536]{1,0:T(8,128)S(1)} %fusion.21), kind=kOutput, calls=%fused_computation.25 | convolution fusion | flops 4842061824 | bytes 18874368 | tf_op jit(solution)/shard_map/dot_general | solution.py:184
  463.1 3.7 all-to-all-start.1
  468.4 1.2 convolution_convert_fusion
  469.6 0.9 copy.66
  470.4 2.8 select_reduce_fusion
  473.3 133.7 %all-to-all-done.1 = bf16[32,48,2048]{2,1,0:T(8,128)(2,1)} async-done(((bf16[32,48,2048]{2,1,0:T(8,128)(2,1)}), bf16[32,48,2048]{2,1,0:T(8,128)(2,1)}, u32[]{:S(2)}, u32[]{:S(2)}) %all-to-all-start.1) | async-done | bytes 6291488 | tf_op jit(solution)/shard_map/all_to_all | solution.py:185
  607.0 4.8 fusion.26
  (79 shorter events, 8.3 us)
Async XLA Ops:
  7.2 448.9 %copy-start = (bf16[1,768,2048]{2,1,0:T(8,128)(2,1)S(1)}, bf16[1,768,2048]{2,1,0:T(8,128)(2,1)}, u32[]{:S(2)}) copy-start(bf16[1,768,2048]{2,1,0:T(8,128)(2,1)} %param.29) | copy-start | bytes 9437188
  7.2 65.1 %all-gather.5.cloned.1.call-start = ((), (), s32[]{:S(2)}) async-start(), calls=%async_computation.4 | async-start | bytes 2359296 | tf_op jit(solution)/shard_map/all_gather | solution.py:99
  11.3 64.8 %copy-start.7 = (s32[4096]{0:T(1024)S(1)}, s32[4096]{0:T(1024)}, u32[]{:S(2)}) copy-start(s32[4096]{0:T(1024)} %param.17) | copy-start | bytes 49156
  20.2 126.8 %all-gather.3.cloned.1.call-start = ((), (), s32[]{:S(2)}) async-start(), calls=%async_computation.3 | async-start | bytes 4718592 | tf_op jit(solution)/shard_map/all_gather | solution.py:90
  20.9 276.3 %reduce-scatter.2.cloned.1.call-start = ((), (), s32[]{:S(2)}) async-start(), calls=%async_computation.5 | async-start | bytes 4718592 | tf_op jit(solution)/shard_map/reduce_scatter | solution.py:153
  74.2 6.2 %collective-permute-start.1 = (bf16[1024,128]{1,0:T(8,128)(2,1)}, bf16[1024,128]{1,0:T(8,128)(2,1)}, u32[]{:S(2)}, u32[]{:S(2)}) collective-permute-start(bf16[1024,128]{1,0:T(8,128)(2,1)} %get-tuple-element.150), channel_id=1, source_target_pairs={{0,8},{8,16},{16,24},{1,9},{9,17},{17,25},{2,10},{10,18},{18,26},{... | collective-permute-start | bytes 786440 | tf_op jit(solution)/shard_map/ppermute | solution.py:12
  76.3 8.2 %collective-permute-start = (bf16[1024,128]{1,0:T(8,128)(2,1)}, bf16[1024,128]{1,0:T(8,128)(2,1)}, u32[]{:S(2)}, u32[]{:S(2)}) collective-permute-start(bf16[1024,128]{1,0:T(8,128)(2,1)} %get-tuple-element.151), channel_id=1, source_target_pairs={{0,8},{8,16},{16,24},{1,9},{9,17},{17,25},{2,10},{10,18},{18,26},{... | collective-permute-start | bytes 786440 | tf_op jit(solution)/shard_map/ppermute | solution.py:12
  86.3 65.9 %copy-start.9 = (f32[128]{0:T(128)S(1)}, f32[128]{0:T(128)}, u32[]{:S(2)}) copy-start(f32[128]{0:T(128)} %param.22) | copy-start | bytes 1540
  146.9 5.8 copy-start.2
  171.2 4.4 copy-start.4
  190.6 4.4 copy-start.4
  204.4 6.2 %copy-start.5 = (s32[128,8]{0,1:T(8,128)S(1)}, s32[128,8]{0,1:T(8,128)}, u32[]{:S(2)}) copy-start(s32[128,8]{0,1:T(8,128)} %param.18) | copy-start | bytes 12292
  210.6 88.1 %copy-start.6 = (f32[2048]{0:T(1024)S(1)}, f32[2048]{0:T(1024)}, u32[]{:S(2)}) copy-start(f32[2048]{0:T(1024)} %param.27) | copy-start | bytes 24580
  220.8 225.3 %copy-start.3 = (s32[128,8]{1,0:T(8,128)}, s32[128,8]{1,0:T(8,128)S(1)}, u32[]{:S(2)}) copy-start(s32[128,8]{1,0:T(8,128)S(1)} %copy.64) | copy-start | bytes 12292
  298.7 147.3 %slice-start = ((s8[6291456]{0:T(1024)(128)(4,1)}), s8[4194304]{0:T(1024)(128)(4,1)S(1)}, s32[]{:S(2)}) async-start(s8[6291456]{0:T(1024)(128)(4,1)} %bitcast.117), calls=%async_computation.6 | async-start | bytes 8388608
  301.9 144.1 %slice-start.1 = ((s8[6291456]{0:T(1024)(128)(4,1)}), s8[2097152]{0:T(1024)(128)(4,1)S(1)}, s32[]{:S(2)}) async-start(s8[6291456]{0:T(1024)(128)(4,1)} %bitcast.117), calls=%async_computation.7 | async-start | bytes 4194304
  463.1 3.8 copy-start.1
  463.1 4.6 copy-start.8
  463.1 5.3 copy-start.10
  463.1 143.9 %all-to-all-start.1 = ((bf16[32,48,2048]{2,1,0:T(8,128)(2,1)}), bf16[32,48,2048]{2,1,0:T(8,128)(2,1)}, u32[]{:S(2)}, u32[]{:S(2)}) async-start(bf16[32,48,2048]{2,1,0:T(8,128)(2,1)} %bitcast.107), calls=%async_computation.2 | async-start | bytes 12582912 | tf_op jit(solution)/shard_map/all_to_all | solution.py:185
Sparse Core Ops, SparseCore 0:
  20.3 51.9 all-gather.4
  75.0 71.8 all-gather.2
  210.8 86.3 reduce-scatter.1
where the time goes:
time: 619 us; the launch traced here: 618 us
  waiting for transfers between devices  317 us (51%)
  blocking collectives  144 us (23%)
  matrix products  60.9 us (10%)
  other arithmetic  46.9 us (8%)
  local copies, waits for them, and re-layouts  25.1 us (4%)
  between operations  14.1 us (2%)
  starting transfers between devices  9.97 us (2%)
    all_to_all x1, blocking collectives, body(): lax.all_to_all(outgoing, ('rep', 'tp'), split_axis=0, concat_axis=0, tile...  144 us
    all_to_all x1, waiting for transfers between devices, body(): lax.all_to_all(result.reshape(received.shape), ('rep', 'tp'), split_axis=...  134 us
    reduce_scatter x1, waiting for transfers between devices, body(): lax.psum_scatter(lax.optimization_barrier(term).astype(jnp.float32).astyp...  73.3 us
    all_gather x1, waiting for transfers between devices, body(): lax.all_gather(normed, 'tp', axis=0, tiled=True)  60.6 us
    all_gather x1, waiting for transfers between devices, body(): gathered = lax.all_gather(stored_cache, 'tp', axis=0, tiled=True)  48.9 us
  transfers between devices with their start and end apart: 6, of which 4 were waited for; matrix products, arithmetic and copies ran while one was open for 5% of the time, Pallas kernels for 0%

commit v1 on v0

--- a/solution.py
+++ b/solution.py
@@ -1,8 +1,11 @@
+import functools
 import math
 
 import jax
 import jax.numpy as jnp
 from jax import lax
+from jax.experimental import pallas as pl
+from jax.experimental.pallas import tpu as pltpu
 from jax.sharding import PartitionSpec as P
 
 
@@ -36,7 +39,7 @@
     )
 
 
-def body(
+def general_body(
     tokens,
     seg_ids,
     expert_ids,
@@ -194,6 +197,312 @@
     return (hidden_out, cache)
 
 
+KEY_BLOCK = 256
+MASKED = -1e30
+
+
+def moved(block, change):
+    route = []
+    for y in range(2):
+        for core in range(2):
+            for z in range(4):
+                for x in range(2):
+                    to_y, to_core, to_z, to_x = change(y, core, z, x)
+                    route.append(
+                        ((y * 2 + core) * 8 + z * 2 + x, (to_y * 2 + to_core) * 8 + to_z * 2 + to_x)
+                    )
+    return lax.ppermute(block, ("rep", "tp"), route)
+
+
+def other_x(block):
+    return moved(block, lambda y, core, z, x: (y, core, z, 1 - x))
+
+
+def other_y(block):
+    return moved(block, lambda y, core, z, x: (1 - y, core, z, x))
+
+
+def other_core(block):
+    return moved(block, lambda y, core, z, x: (y, 1 - core, z, x))
+
+
+def other_z(block, k):
+    return moved(block, lambda y, core, z, x: (y, core, z ^ k, x))
+
+
+def after(value, earlier):
+    return lax.optimization_barrier((value, earlier))[0]
+
+
+def attention_kernel(
+    place, low, projected, gain, cosine, sine, start, kv_here, kv_side, kv_before, kv_before_side, out,
+    keys, values, acc, peak, total,
+):
+    slot = pl.program_id(0)
+    z, x = place[0], place[1]
+    rows = projected.shape[0]
+    head = gain.shape[0]
+    heads = projected.shape[1] // head
+    half = head // 2
+
+    @pl.when(slot == 0)
+    def _():
+        for first, near, far in ((0, kv_before, kv_before_side), (8, kv_here, kv_side)):
+            for k in range(4):
+                at = jnp.bitwise_xor(z, k) * 2
+                for source, shift in ((near, x), (far, 1 - x)):
+                    row = pl.multiple_of((first + at + shift) * rows, rows)
+                    keys[pl.ds(row, rows), :] = source[k, :, :head]
+                    values[:, pl.ds(row, rows)] = source[k, :, head:].astype(jnp.float32).T.astype(jnp.bfloat16)
+
+    turned = []
+    for h in range(heads):
+        q = projected[:, h * head : (h + 1) * head].T
+        q = q * lax.rsqrt(jnp.mean(q * q, axis=0, keepdims=True) + 1e-06) * gain[...]
+        first, second = q[:half], q[half:]
+        turned.append(
+            jnp.concatenate(
+                [first * cosine[0] - second * sine[0], second * cosine[0] + first * sine[0]], axis=0
+            )
+        )
+    query = (jnp.concatenate(turned, axis=1) * (head**-0.5 * math.log2(math.e))).astype(jnp.bfloat16)
+    acc[...] = jnp.zeros_like(acc)
+    total[...] = jnp.zeros_like(total)
+    peak[...] = jnp.full_like(peak, MASKED)
+    position = (8 + jnp.bitwise_xor(z, slot) * 2 + x) * rows
+    own_position = position + lax.broadcasted_iota(jnp.int32, (KEY_BLOCK, rows), 1)
+    own_start = start[0]
+
+    def step(j, _):
+        row = pl.multiple_of(j * KEY_BLOCK, KEY_BLOCK)
+        scores = jnp.dot(keys[pl.ds(row, KEY_BLOCK), :], query, preferred_element_type=jnp.float32)
+        key_position = row + lax.broadcasted_iota(jnp.int32, (KEY_BLOCK, rows), 0)
+        allowed = (key_position >= own_start) & (key_position <= own_position)
+        scores = jnp.concatenate(
+            [jnp.where(allowed, scores[:, h * rows : (h + 1) * rows], MASKED) for h in range(heads)], axis=1
+        )
+        largest = jnp.maximum(peak[...], jnp.max(scores, axis=0, keepdims=True))
+        fade = jnp.exp2(peak[...] - largest)
+        weights = jnp.exp2(scores - largest)
+        total[...] = total[...] * fade + jnp.sum(weights, axis=0, keepdims=True)
+        acc[...] = acc[...] * fade + jnp.dot(
+            values[:, pl.ds(row, KEY_BLOCK)], weights.astype(jnp.bfloat16), preferred_element_type=jnp.float32
+        )
+        peak[...] = largest
+        return 0
+
+    lax.fori_loop(low[slot], (position + rows - 1) // KEY_BLOCK + 1, step, 0)
+    mixed = acc[...] / total[...]
+    for h in range(heads):
+        out[:, h * head : (h + 1) * head] = mixed[:, h * rows : (h + 1) * rows].T.astype(out.dtype)
+
+
+def attend_slots(place, low, projected, q_gain, cosine, sine, start, kv):
+    slots, rows = start.shape[0], start.shape[2]
+    head = q_gain.shape[0]
+    width = projected.shape[1]
+    whole = lambda *shape: pl.BlockSpec(shape, lambda s, *_: (0,) * len(shape))
+    return pl.pallas_call(
+        attention_kernel,
+        grid_spec=pltpu.PrefetchScalarGridSpec(
+            num_scalar_prefetch=2,
+            grid=(slots,),
+            in_specs=[
+                pl.BlockSpec((rows, width), lambda s, *_: (s, 0)),
+                whole(head, 1),
+                pl.BlockSpec((1, head // 2, rows), lambda s, *_: (s, 0, 0)),
+                pl.BlockSpec((1, head // 2, rows), lambda s, *_: (s, 0, 0)),
+                pl.BlockSpec((1, 1, rows), lambda s, *_: (s, 0, 0)),
+            ]
+            + [whole(*part.shape) for part in kv],
+            out_specs=pl.BlockSpec((rows, width), lambda s, *_: (s, 0)),
+            scratch_shapes=[
+                pltpu.VMEM((16 * rows, head), jnp.bfloat16),
+                pltpu.VMEM((head, 16 * rows), jnp.bfloat16),
+                pltpu.VMEM((head, width // head * rows), jnp.float32),
+                pltpu.VMEM((1, width // head * rows), jnp.float32),
+                pltpu.VMEM((1, width // head * rows), jnp.float32),
+            ],
+        ),
+        out_shape=jax.ShapeDtypeStruct((slots * rows, width), jnp.bfloat16),
+        compiler_params=pltpu.CompilerParams(vmem_limit_bytes=40 * 2**20),
+        cost_estimate=pl.CostEstimate(
+            flops=4 * slots * rows * width * 4 * rows,
+            bytes_accessed=8 * 2**20,
+            transcendentals=slots * width * rows,
+        ),
+        name="attention",
+    )(place, low, projected, q_gain.reshape(head, 1), cosine, sine, start, *kv)
+
+
+def grid_body(
+    tokens,
+    seg_ids,
+    expert_ids,
+    gates,
+    page_table,
+    attn_gain,
+    q_gain,
+    key_norm_gain,
+    w_query,
+    w_keyval,
+    w_out,
+    moe_gain,
+    w_gate_up,
+    w_down,
+):
+    rows, width = tokens.shape
+    head = q_gain.shape[0]
+    kv_heads = w_keyval.shape[1] // (2 * head)
+    kv_width = kv_heads * head
+    rep, tp = lax.axis_index("rep"), lax.axis_index("tp")
+    y, core, z, x = rep // 2, rep % 2, tp // 2, tp % 2
+    group_rows = 8 * rows
+    group_start = rep * group_rows
+    slots = range(4)
+
+    raw = [tokens] + [other_z(tokens, k) for k in (1, 2, 3)]
+    half_heads = w_query.shape[1] // 2
+    query_half = other_x(lax.dynamic_slice_in_dim(w_query, core * half_heads, half_heads, 1))
+    query_rest = other_core(query_half)
+    out_half = other_x(
+        after(lax.dynamic_slice_in_dim(w_out, core * half_heads, half_heads, 0), query_half)
+    )
+    out_rest = other_core(out_half)
+
+    routes = jnp.concatenate([expert_ids.T.astype(jnp.bfloat16), gates.T], axis=0)
+    routes = lax.all_gather(routes, ("rep", "tp"), axis=0, tiled=True)
+
+    normed = root_mean_norm(tokens.astype(jnp.float32), attn_gain).astype(jnp.bfloat16)
+    own_position = (group_start + tp * rows + jnp.arange(rows, dtype=jnp.int32)).astype(jnp.float32)
+    keyval = jnp.dot(normed, w_keyval, preferred_element_type=jnp.float32)
+    rotated = apply_rotary(
+        root_mean_norm(keyval[:, :kv_width].reshape(rows, kv_heads, head), key_norm_gain), own_position
+    )
+    stored = jnp.concatenate([rotated.reshape(rows, kv_width), keyval[:, kv_width:]], axis=1).astype(
+        jnp.bfloat16
+    )
+    pages = page_table.shape[0]
+    placing = (page_table[None, :] == jnp.arange(pages, dtype=jnp.int32)[:, None]).astype(jnp.bfloat16)
+    cache = jnp.dot(placing, stored.reshape(pages, -1), preferred_element_type=jnp.float32)
+    cache = cache.astype(jnp.bfloat16).reshape(pages, rows // pages, 2 * kv_width)
+
+    by_head = jnp.transpose(stored.reshape(rows, 2, kv_heads, head), (2, 0, 1, 3))
+    by_head = by_head.reshape(kv_heads, rows, 2 * head)
+    pick = lambda h: lax.dynamic_index_in_dim(by_head, h, 0, keepdims=False)
+    kv_here = jnp.stack([pick(z)] + [other_z(pick(z ^ k), k) for k in (1, 2, 3)])
+    kv_before = passed_along(kv_here, "rep", 1)
+    kv_side = other_x(kv_here)
+    kv_before_side = other_x(kv_before)
+
+    slot_z = jnp.stack([z ^ k for k in slots])
+    slot_rows = ((slot_z * 2 + x) * rows)[:, None] + jnp.arange(rows, dtype=jnp.int32)[None, :]
+    slot_position = group_start + slot_rows
+    frequency = jnp.exp(
+        jnp.arange(head // 2, dtype=jnp.float32) * (-2.0 * math.log(1000000.0) / head)
+    )
+    angles = frequency[None, :, None] * slot_position.astype(jnp.float32)[:, None, :]
+    slot_seg = jnp.take(seg_ids, slot_position.reshape(-1), axis=0)
+    starts = jnp.sum((seg_ids[None, :] < slot_seg[:, None]).astype(jnp.int32), axis=1)
+    starts = (starts - (group_start - group_rows)).reshape(4, 1, rows)
+    low = starts[:, 0, 0] // KEY_BLOCK
+    lines = jnp.concatenate(raw, axis=0).astype(jnp.float32)
+    normed_lines = root_mean_norm(lines, attn_gain).astype(jnp.bfloat16)
+    w_query_wide = jnp.concatenate([w_query, query_half, query_rest], axis=1)
+    projected = jnp.dot(normed_lines, w_query_wide, preferred_element_type=jnp.float32)
+    attended = attend_slots(
+        jnp.stack([z, x]),
+        low,
+        projected,
+        q_gain,
+        jnp.cos(angles),
+        jnp.sin(angles),
+        starts,
+        (kv_here, kv_side, kv_before, kv_before_side),
+    )
+    w_out_wide = jnp.concatenate([w_out, out_half, out_rest], axis=0)
+    term = jnp.dot(attended, w_out_wide, preferred_element_type=jnp.float32).astype(jnp.bfloat16)
+    term = term.reshape(4, rows, width)
+    mixed_sum = term[0].astype(jnp.float32)
+    for k in (1, 2, 3):
+        mixed_sum = mixed_sum + other_z(term[k], k).astype(jnp.float32)
+    residual = (tokens.astype(jnp.float32) + mixed_sum).astype(jnp.bfloat16)
+    normed_moe = root_mean_norm(residual.astype(jnp.float32), moe_gain).astype(jnp.bfloat16)
+
+    top = expert_ids.shape[1]
+    capacity = max(2, 3 * rows * top // (2 * 32))
+    routes = routes.reshape(32, 2, top, rows)
+    block_of = jnp.stack(
+        [
+            ((y ^ dy) * 2 + core) * 8 + (z ^ k) * 2 + (x ^ dx)
+            for k in slots
+            for dy, dx in ((0, 0), (0, 1), (1, 0), (1, 1))
+        ]
+    )
+    routes = jnp.take(routes, block_of, axis=0)
+    experts = jnp.stack([rep * 8 + tp, (rep ^ 1) * 8 + tp])
+    hits = routes[:, 0][:, None] == experts.astype(jnp.bfloat16)[None, :, None, None]
+    weight = jnp.sum(jnp.where(hits, routes[:, 1][:, None].astype(jnp.float32), 0.0), axis=2)
+    hit = jnp.any(hits, axis=2)
+    earlier = jnp.arange(rows)[:, None] < jnp.arange(rows)[None, :]
+    place = jnp.dot(
+        hit.reshape(-1, rows).astype(jnp.bfloat16),
+        earlier.astype(jnp.bfloat16),
+        preferred_element_type=jnp.float32,
+    ).reshape(16, 2, rows)
+    chosen = (
+        place[:, :, None, :].astype(jnp.int32) == jnp.arange(capacity, dtype=jnp.int32)[None, None, :, None]
+    ) & hit[:, :, None, :]
+    weighted = jnp.where(chosen, weight[:, :, None, :], 0.0).astype(jnp.bfloat16)
+    weighted = weighted.reshape(4, 4, 2, capacity, rows)
+    chosen = chosen.astype(jnp.bfloat16).reshape(4, 4, 2 * capacity, rows)
+
+    def experts_of(slot_rows_in):
+        gate_up = jnp.dot(slot_rows_in, w_gate_up[0], preferred_element_type=jnp.float32)
+        hidden = w_down.shape[1]
+        act = (jax.nn.silu(gate_up[:, :hidden]) * gate_up[:, hidden:]).astype(jnp.bfloat16)
+        return jnp.dot(act, w_down[0], preferred_element_type=jnp.float32).astype(jnp.bfloat16)
+
+    half = rows // 2
+    arrived = [normed_moe]
+    for k in (1, 2, 3):
+        arrived.append(other_z(after(normed_moe, arrived[-1]) if k > 1 else normed_moe, k))
+    partial = []
+    for k in slots:
+        block = arrived[k]
+        side_x, side_y = other_x(block), other_y(block)
+        corner = jnp.concatenate([other_y(side_x[:half]), other_x(side_y[half:])], axis=0)
+        blocks = jnp.stack([block, side_x, side_y, corner])
+        picked = lax.dot_general(
+            chosen[k], blocks, (((2,), (1,)), ((0,), (0,))), preferred_element_type=jnp.float32
+        ).astype(jnp.bfloat16)
+        kept = picked[:, :capacity].reshape(-1, width)
+        traded = other_core(picked[:, capacity:].reshape(-1, width))
+        result = experts_of(jnp.concatenate([kept, traded], axis=0))
+        back = other_core(result[4 * capacity :])
+        both = jnp.stack([result[: 4 * capacity], back]).reshape(2, 4, capacity, width)
+        partial.append(
+            lax.dot_general(
+                weighted[k],
+                jnp.transpose(both, (1, 0, 2, 3)),
+                (((1, 2), (1, 2)), ((0,), (0,))),
+                preferred_element_type=jnp.float32,
+            ).astype(jnp.bfloat16)
+        )
+    combined = residual.astype(jnp.float32)
+    for k in (1, 2, 3, 0):
+        here, to_x, to_y, to_corner = (partial[k][v] for v in range(4))
+        by_y, by_x = other_y(to_corner[:half]), other_x(to_corner[half:])
+        add = lambda a, b: (a.astype(jnp.float32) + b.astype(jnp.float32)).astype(jnp.bfloat16)
+        from_x = other_x(jnp.concatenate([add(to_x[:half], by_y), to_x[half:]], axis=0))
+        from_y = other_y(jnp.concatenate([to_y[:half], add(to_y[half:], by_x)], axis=0))
+        total = here.astype(jnp.float32) + from_x.astype(jnp.float32) + from_y.astype(jnp.float32)
+        if k:
+            total = other_z(total.astype(jnp.bfloat16), k).astype(jnp.float32)
+        combined = combined + total
+    return (combined.astype(jnp.bfloat16), cache)
+
+
 def solution(mesh):
     in_specs = (
         P(("rep", "tp"), None),
@@ -212,4 +521,5 @@
         P(("rep", "tp"), None, None),
     )
     out_specs = (P(("rep", "tp"), None), P(("rep", "tp"), None, None))
+    body = grid_body if (mesh.shape["rep"], mesh.shape["tp"]) == (4, 8) else general_body
     return jax.shard_map(body, mesh=mesh, in_specs=in_specs, out_specs=out_specs, check_vma=False)

time: 619 us -> 447 us (0.72)
  the two profiles are of different devices: /device:TPU:0 before, /device:TPU:8 now
where the time goes in v1:
time: 447 us; the launch traced here: 440 us
  waiting for transfers between devices  202 us (45%)
  blocking collectives  82.9 us (19%)
  starting transfers between devices  58.8 us (13%)
  matrix products  35.5 us (8%)
  other arithmetic  26.2 us (6%)
  local copies, waits for them, and re-layouts  22.3 us (5%)
  Pallas kernels  9.56 us (2%)
    ppermute x61, waiting for transfers between devices, moved(): return lax.ppermute(block, ('rep', 'tp'), route)  202 us
    all_gather x1, blocking collectives, grid_body(): routes = lax.all_gather(routes, ('rep', 'tp'), axis=0, tiled=True)  82.9 us
    ppermute x61, starting transfers between devices, moved(): return lax.ppermute(block, ('rep', 'tp'), route)  56.8 us
    dot_general x4, matrix products, experts_of(): jnp.dot(slot_rows_in, w_gate_up[0], preferred_element_type=jnp.float32)  10.5 us
    pallas_call x1, Pallas kernels, attend_slots(): pl.pallas_call(attention_kernel, grid_spec=pltpu.PrefetchScalarGridSpec(n...  9.56 us
  transfers between devices with their start and end apart: 62, of which 32 were waited for; matrix products, arithmetic and copies ran while one was open for 17% of the time, Pallas kernels for 2%

profile of v1, /device:TPU:8, one launch (start us, length us, event | category | flops | bytes accessed | tf_op | source)
XLA Modules:
  0.0 439.8 jit_solution(9453119425123637401)
XLA Ops:
  2.2 3.1 fusion.128
  8.4 1.8 multiply_reduce_fusion
  17.0 1.8 collective-permute-start.5
  18.8 2.6 collective-permute-start.6
  21.4 2.3 constant_dynamic-slice_fusion.2
  26.0 3.1 gather_fusion
  31.8 2.3 constant_dynamic-slice_fusion
  34.2 3.1 collective-permute-start.1
  38.8 2.0 collective-permute-start.9
  40.8 7.3 %collective-permute-done.3 = bf16[2048,256]{1,0:T(8,128)(2,1)} collective-permute-done((bf16[2048,256]{1,0:T(8,128)(2,1)}, bf16[2048,256]{1,0:T(8,128)(2,1)}, u32[]{:S(2)}, u32[]{:S(2)}) %collective-permute-start.3) | collective-permute-done | bytes 1048608 | tf_op jit(solution)/shard_map/ppermute | solution.py:214
  50.1 82.9 %all_gather.3 = bf16[512,128]{1,0:T(8,128)(2,1)} all-gather(bf16[16,128]{1,0:T(8,128)(2,1)S(1)} %pad_maximum_fusion.12), channel_id=1, replica_groups=mesh['rep'=4,'tp'=8] {'rep','tp'}, dimensions={0}, use_global_device_ids=true | all-gather | bytes 135168 | tf_op jit(solution)/shard_map/all_gather | solution.py:374
  139.7 16.0 %collective-permute-done.2 = bf16[128,2048]{1,0:T(8,128)(2,1)S(1)} collective-permute-done((bf16[128,2048]{1,0:T(8,128)(2,1)}, bf16[128,2048]{1,0:T(8,128)(2,1)S(1)}, u32[]{:S(2)}, u32[]{:S(2)}) %collective-permute-start.2) | collective-permute-done | bytes 524320 | tf_op jit(solution)/shard_map/ppermute | solution.py:214
  155.7 1.8 fusion.8
  157.7 4.4 %fusion.11.projected = f32[512,1024]{1,0:T(8,128)S(1)} fusion(bf16[2048,256]{1,0:T(8,128)(2,1)} %collective-permute-done.4, bf16[2048,256]{1,0:T(8,128)(2,1)} %collective-permute-done.3, bf16[2048,512]{1,0:T(8,128)(2,1)S(1)} %copy-done.10, f32[2048]{0:T(1024)} %param.19, f32[512]{0:T(512)S(1)} %add_rsqrt_fusion.1, ...), kind=kOutput, calls=%fused_computation.17 | convolution fusion | flops 2171600896 | bytes 8398848 | tf_op jit(solution)/shard_map/dot_general | solution.py:412
  162.1 9.6 %attention.1 = bf16[512,1024]{1,0:T(8,128)(2,1)S(1)} custom-call(s32[2]{0:T(128)S(1)} %pad_add_fusion.place, s32[4]{0:T(128)S(1)} %and_select_fusion.low, f32[512,1024]{1,0:T(8,128)S(1)} %fusion.11.projected, f32[128,1]{1,0:T(8,128)S(1)} %copy.85.gain, f32[4,64,128]{2,1,0:T(8,128)S(1)} %get-tuple-element.78.cosine, ...), custom_call_target="tpu_custom_call" | custom-call | flops 1073741824 | bytes 8388608 | tf_op jit(solution)/shard_map/attention/pallas_call | solution.py:305
  171.7 3.6 fusion.31
  179.3 14.5 %collective-permute-done.13 = bf16[128,2048]{1,0:T(8,128)(2,1)S(1)} collective-permute-done((bf16[128,2048]{1,0:T(8,128)(2,1)S(1)}, bf16[128,2048]{1,0:T(8,128)(2,1)S(1)}, u32[]{:S(2)}, u32[]{:S(2)}) %collective-permute-start.13) | collective-permute-done | bytes 524320 | tf_op jit(solution)/shard_map/ppermute | solution.py:214
  193.9 4.6 %collective-permute-done.14 = bf16[128,2048]{1,0:T(8,128)(2,1)S(1)} collective-permute-done((bf16[128,2048]{1,0:T(8,128)(2,1)S(1)}, bf16[128,2048]{1,0:T(8,128)(2,1)S(1)}, u32[]{:S(2)}, u32[]{:S(2)}) %collective-permute-start.14) | collective-permute-done | bytes 524320 | tf_op jit(solution)/shard_map/ppermute | solution.py:214
  198.5 24.4 %collective-permute-done.15 = bf16[128,2048]{1,0:T(8,128)(2,1)S(1)} collective-permute-done((bf16[128,2048]{1,0:T(8,128)(2,1)S(1)}, bf16[128,2048]{1,0:T(8,128)(2,1)S(1)}, u32[]{:S(2)}, u32[]{:S(2)}) %collective-permute-start.15) | collective-permute-done | bytes 524320 | tf_op jit(solution)/shard_map/ppermute | solution.py:214
  224.6 2.3 collective-permute-start.52
  227.0 3.9 collective-permute-start.53
  231.3 7.5 %collective-permute-done.52 = bf16[128,2048]{1,0:T(8,128)(2,1)S(1)} collective-permute-done((bf16[128,2048]{1,0:T(8,128)(2,1)S(1)}, bf16[128,2048]{1,0:T(8,128)(2,1)S(1)}, u32[]{:S(2)}, u32[]{:S(2)}) %collective-permute-start.52) | collective-permute-done | bytes 524320 | tf_op jit(solution)/shard_map/ppermute | solution.py:214
  238.9 5.9 %collective-permute-start.54 = (bf16[64,2048]{1,0:T(8,128)(2,1)S(1)}, bf16[64,2048]{1,0:T(8,128)(2,1)S(1)}, u32[]{:S(2)}, u32[]{:S(2)}) collective-permute-start(bf16[64,2048]{1,0:T(8,128)(2,1)S(1)} %slice.500), channel_id=1, source_target_pairs={{0,16},{1,17},{2,18},{3,19},{4,20},{5,21},{6,22},{7,23},{8,24},{9,... | collective-permute-start | bytes 786440 | tf_op jit(solution)/shard_map/ppermute | solution.py:214
  245.4 1.8 collective-permute-start.17
  247.2 4.7 %collective-permute-done.54 = bf16[64,2048]{1,0:T(8,128)(2,1)S(1)} collective-permute-done((bf16[64,2048]{1,0:T(8,128)(2,1)S(1)}, bf16[64,2048]{1,0:T(8,128)(2,1)S(1)}, u32[]{:S(2)}, u32[]{:S(2)}) %collective-permute-start.54) | collective-permute-done | bytes 262176 | tf_op jit(solution)/shard_map/ppermute | solution.py:214
  252.0 2.1 collective-permute-done.55
  254.7 8.5 %collective-permute-done.17 = bf16[128,2048]{1,0:T(8,128)(2,1)S(1)} collective-permute-done((bf16[128,2048]{1,0:T(8,128)(2,1)S(1)}, bf16[128,2048]{1,0:T(8,128)(2,1)S(1)}, u32[]{:S(2)}, u32[]{:S(2)}) %collective-permute-start.17) | collective-permute-done | bytes 524320 | tf_op jit(solution)/shard_map/ppermute | solution.py:214
  265.2 2.4 collective-permute-done.28
  272.0 9.3 %collective-permute-done.29 = bf16[128,2048]{1,0:T(8,128)(2,1)S(1)} collective-permute-done((bf16[128,2048]{1,0:T(8,128)(2,1)S(1)}, bf16[128,2048]{1,0:T(8,128)(2,1)S(1)}, u32[]{:S(2)}, u32[]{:S(2)}) %collective-permute-start.29) | collective-permute-done | bytes 524320 | tf_op jit(solution)/shard_map/ppermute | solution.py:214
  283.8 7.5 %collective-permute-done.40 = bf16[128,2048]{1,0:T(8,128)(2,1)S(1)} collective-permute-done((bf16[128,2048]{1,0:T(8,128)(2,1)S(1)}, bf16[128,2048]{1,0:T(8,128)(2,1)S(1)}, u32[]{:S(2)}, u32[]{:S(2)}) %collective-permute-start.40) | collective-permute-done | bytes 524320 | tf_op jit(solution)/shard_map/ppermute | solution.py:214
  293.2 2.6 fusion
  298.8 4.0 collective-permute-done.41
  305.6 2.6 fusion.6
  310.2 1.8 collective-permute-done.44
  315.9 2.6 fusion.4
  320.2 2.8 collective-permute-done.58
  330.1 2.6 fusion.2
  334.6 9.1 %collective-permute-done.25 = bf16[64,2048]{1,0:T(8,128)(2,1)S(1)} collective-permute-done((bf16[64,2048]{1,0:T(8,128)(2,1)S(1)}, bf16[64,2048]{1,0:T(8,128)(2,1)S(1)}, u32[]{:S(2)}, u32[]{:S(2)}) %collective-permute-start.25) | collective-permute-done | bytes 262176 | tf_op jit(solution)/shard_map/ppermute | solution.py:214
  346.7 1.8 collective-permute-start.24
  348.5 3.4 collective-permute-done.35
  353.3 2.3 collective-permute-done.37
  358.5 10.6 %collective-permute-done.47 = bf16[64,2048]{1,0:T(8,128)(2,1)S(1)} collective-permute-done((bf16[64,2048]{1,0:T(8,128)(2,1)S(1)}, bf16[64,2048]{1,0:T(8,128)(2,1)S(1)}, u32[]{:S(2)}, u32[]{:S(2)}) %collective-permute-start.47) | collective-permute-done | bytes 262176 | tf_op jit(solution)/shard_map/ppermute | solution.py:214
  374.6 9.5 %collective-permute-done.36 = bf16[128,2048]{1,0:T(8,128)(2,1)S(1)} collective-permute-done((bf16[128,2048]{1,0:T(8,128)(2,1)S(1)}, bf16[128,2048]{1,0:T(8,128)(2,1)S(1)}, u32[]{:S(2)}, u32[]{:S(2)}) %collective-permute-start.36) | collective-permute-done | bytes 524320 | tf_op jit(solution)/shard_map/ppermute | solution.py:214
  386.7 5.4 %collective-permute-done.48 = bf16[128,2048]{1,0:T(8,128)(2,1)S(1)} collective-permute-done((bf16[128,2048]{1,0:T(8,128)(2,1)S(1)}, bf16[128,2048]{1,0:T(8,128)(2,1)S(1)}, u32[]{:S(2)}, u32[]{:S(2)}) %collective-permute-start.48) | collective-permute-done | bytes 524320 | tf_op jit(solution)/shard_map/ppermute | solution.py:214
  392.1 4.8 %collective-permute-done.50 = bf16[128,2048]{1,0:T(8,128)(2,1)S(1)} collective-permute-done((bf16[128,2048]{1,0:T(8,128)(2,1)S(1)}, bf16[128,2048]{1,0:T(8,128)(2,1)S(1)}, u32[]{:S(2)}, u32[]{:S(2)}) %collective-permute-start.50) | collective-permute-done | bytes 524320 | tf_op jit(solution)/shard_map/ppermute | solution.py:214
  403.3 22.9 %collective-permute-done.39 = bf16[128,2048]{1,0:T(8,128)(2,1)} collective-permute-done((bf16[128,2048]{1,0:T(8,128)(2,1)}, bf16[128,2048]{1,0:T(8,128)(2,1)}, u32[]{:S(2)}, u32[]{:S(2)}) %collective-permute-start.39) | collective-permute-done | bytes 524320 | tf_op jit(solution)/shard_map/ppermute | solution.py:214
  426.1 9.9 %collective-permute-done.51 = bf16[128,2048]{1,0:T(8,128)(2,1)} collective-permute-done((bf16[128,2048]{1,0:T(8,128)(2,1)}, bf16[128,2048]{1,0:T(8,128)(2,1)}, u32[]{:S(2)}, u32[]{:S(2)}) %collective-permute-start.51) | collective-permute-done | bytes 524320 | tf_op jit(solution)/shard_map/ppermute | solution.py:214
  436.0 3.4 fusion.111
  (245 shorter events, 88.1 us)
Async XLA Ops:
  0.6 137.0 %collective-permute-start = (bf16[128,2048]{1,0:T(8,128)(2,1)}, bf16[128,2048]{1,0:T(8,128)(2,1)}, u32[]{:S(2)}, u32[]{:S(2)}) collective-permute-start(bf16[128,2048]{1,0:T(8,128)(2,1)} %param.14), channel_id=1, source_target_pairs={{0,2},{1,3},{2,0},{3,1},{4,6},{5,7},{6,4},{7,5},{8,10},{9,11},{10,... | collective-permute-start | bytes 1572872 | tf_op jit(solution)/shard_map/ppermute | solution.py:214
  17.0 17.2 %collective-permute-start.5 = (bf16[128,256]{1,0:T(8,128)(2,1)}, bf16[128,256]{1,0:T(8,128)(2,1)S(1)}, u32[]{:S(2)}, u32[]{:S(2)}) collective-permute-start(bf16[128,256]{1,0:T(8,128)(2,1)} %get-tuple-element.70), channel_id=1, source_target_pairs={{0,2},{1,3},{2,0},{3,1},{4,6},{5,7},{6,4},{7,5},{8,10},{9,11},{10,... | collective-permute-start | bytes 196616 | tf_op jit(solution)/shard_map/ppermute | solution.py:214
  18.8 18.5 %collective-permute-start.6 = (bf16[128,256]{1,0:T(8,128)(2,1)S(1)}, bf16[128,256]{1,0:T(8,128)(2,1)S(1)}, u32[]{:S(2)}, u32[]{:S(2)}) collective-permute-start(bf16[128,256]{1,0:T(8,128)(2,1)S(1)} %get-tuple-element.69), channel_id=1, source_target_pairs={{0,4},{1,5},{2,6},{3,7},{4,0},{5,1},{6,2},{7,3},{8,12},{9,13},{10,... | collective-permute-start | bytes 196616 | tf_op jit(solution)/shard_map/ppermute | solution.py:214
  21.4 15.9 %collective-permute-start.7 = (bf16[128,256]{1,0:T(8,128)(2,1)S(1)}, bf16[128,256]{1,0:T(8,128)(2,1)}, u32[]{:S(2)}, u32[]{:S(2)}) collective-permute-start(bf16[128,256]{1,0:T(8,128)(2,1)S(1)} %get-tuple-element.68), channel_id=1, source_target_pairs={{0,6},{1,7},{2,4},{3,5},{4,2},{5,3},{6,0},{7,1},{8,14},{9,15},{10,... | collective-permute-start | bytes 196616 | tf_op jit(solution)/shard_map/ppermute | solution.py:214
  23.7 24.4 %collective-permute-start.3 = (bf16[2048,256]{1,0:T(8,128)(2,1)}, bf16[2048,256]{1,0:T(8,128)(2,1)}, u32[]{:S(2)}, u32[]{:S(2)}) collective-permute-start(bf16[2048,256]{1,0:T(8,128)(2,1)} %constant_dynamic-slice_fusion.2), channel_id=1, source_target_pairs={{0,1},{1,0},{2,3},{3,2},{4,5},{5,4},{6,7},{7,6},{8,9},{9,8},{10,11... | collective-permute-start | bytes 3145736 | tf_op jit(solution)/shard_map/ppermute | solution.py:214
  34.2 104.1 %collective-permute-start.1 = (bf16[128,2048]{1,0:T(8,128)(2,1)}, bf16[128,2048]{1,0:T(8,128)(2,1)}, u32[]{:S(2)}, u32[]{:S(2)}) collective-permute-start(bf16[128,2048]{1,0:T(8,128)(2,1)} %param.14), channel_id=1, source_target_pairs={{0,4},{1,5},{2,6},{3,7},{4,0},{5,1},{6,2},{7,3},{8,12},{9,13},{10,... | collective-permute-start | bytes 1572872 | tf_op jit(solution)/shard_map/ppermute | solution.py:214
  38.8 96.6 %collective-permute-start.9 = (bf16[4,128,256]{2,1,0:T(8,128)(2,1)S(1)}, bf16[4,128,256]{2,1,0:T(8,128)(2,1)}, u32[]{:S(2)}, u32[]{:S(2)}) collective-permute-start(bf16[4,128,256]{2,1,0:T(8,128)(2,1)S(1)} %pad_maximum_fusion.10.kv_here), channel_id=1, source_target_pairs={{0,8},{8,16},{16,24},{1,9},{9,17},{17,25},{2,10},{10,18},{18,26},{... | collective-permute-start | bytes 786440 | tf_op jit(solution)/shard_map/ppermute | solution.py:15
  48.1 109.5 %collective-permute-start.11 = (bf16[256,2048]{1,0:T(8,128)(2,1)}, bf16[256,2048]{1,0:T(8,128)(2,1)}, u32[]{:S(2)}, u32[]{:S(2)}) collective-permute-start(bf16[256,2048]{1,0:T(8,128)(2,1)} %constant_dynamic-slice_fusion), channel_id=1, source_target_pairs={{0,1},{1,0},{2,3},{3,2},{4,5},{5,4},{6,7},{7,6},{8,9},{9,8},{10,11... | collective-permute-start | bytes 3145736 | tf_op jit(solution)/shard_map/ppermute | solution.py:214
  50.1 107.6 %collective-permute-start.4 = (bf16[2048,256]{1,0:T(8,128)(2,1)}, bf16[2048,256]{1,0:T(8,128)(2,1)}, u32[]{:S(2)}, u32[]{:S(2)}) collective-permute-start(bf16[2048,256]{1,0:T(8,128)(2,1)} %collective-permute-done.3), channel_id=1, source_target_pairs={{0,8},{1,9},{2,10},{3,11},{4,12},{5,13},{6,14},{7,15},{8,0},{9,1},... | collective-permute-start | bytes 3145736 | tf_op jit(solution)/shard_map/ppermute | solution.py:214
  135.4 20.3 %collective-permute-start.2 = (bf16[128,2048]{1,0:T(8,128)(2,1)}, bf16[128,2048]{1,0:T(8,128)(2,1)S(1)}, u32[]{:S(2)}, u32[]{:S(2)}) collective-permute-start(bf16[128,2048]{1,0:T(8,128)(2,1)} %param.14), channel_id=1, source_target_pairs={{0,6},{1,7},{2,4},{3,5},{4,2},{5,3},{6,0},{7,1},{8,14},{9,15},{10,... | collective-permute-start | bytes 1572872 | tf_op jit(solution)/shard_map/ppermute | solution.py:214
  137.6 24.5 %collective-permute-start.8 = (bf16[4,128,256]{2,1,0:T(8,128)(2,1)S(1)}, bf16[4,128,256]{2,1,0:T(8,128)(2,1)S(1)}, u32[]{:S(2)}, u32[]{:S(2)}) collective-permute-start(bf16[4,128,256]{2,1,0:T(8,128)(2,1)S(1)} %pad_maximum_fusion.10.kv_here), channel_id=1, source_target_pairs={{0,1},{1,0},{2,3},{3,2},{4,5},{5,4},{6,7},{7,6},{8,9},{9,8},{10,11... | collective-permute-start | bytes 786440 | tf_op jit(solution)/shard_map/ppermute | solution.py:214
  138.2 23.8 %collective-permute-start.10 = (bf16[4,128,256]{2,1,0:T(8,128)(2,1)}, bf16[4,128,256]{2,1,0:T(8,128)(2,1)S(1)}, u32[]{:S(2)}, u32[]{:S(2)}) collective-permute-start(bf16[4,128,256]{2,1,0:T(8,128)(2,1)} %collective-permute-done.9.kv_before), channel_id=1, source_target_pairs={{0,1},{1,0},{2,3},{3,2},{4,5},{5,4},{6,7},{7,6},{8,9},{9,8},{10,11... | collective-permute-start | bytes 786440 | tf_op jit(solution)/shard_map/ppermute | solution.py:214
  157.6 14.1 %collective-permute-start.12 = (bf16[256,2048]{1,0:T(8,128)(2,1)}, bf16[256,2048]{1,0:T(8,128)(2,1)S(1)}, u32[]{:S(2)}, u32[]{:S(2)}) collective-permute-start(bf16[256,2048]{1,0:T(8,128)(2,1)} %collective-permute-done.11), channel_id=1, source_target_pairs={{0,8},{1,9},{2,10},{3,11},{4,12},{5,13},{6,14},{7,15},{8,0},{9,1},... | collective-permute-start | bytes 3145736 | tf_op jit(solution)/shard_map/ppermute | solution.py:214
  175.5 18.4 %collective-permute-start.13 = (bf16[128,2048]{1,0:T(8,128)(2,1)S(1)}, bf16[128,2048]{1,0:T(8,128)(2,1)S(1)}, u32[]{:S(2)}, u32[]{:S(2)}) collective-permute-start(bf16[128,2048]{1,0:T(8,128)(2,1)S(1)} %get-tuple-element.44), channel_id=1, source_target_pairs={{0,2},{1,3},{2,0},{3,1},{4,6},{5,7},{6,4},{7,5},{8,10},{9,11},{10,... | collective-permute-start | bytes 1572872 | tf_op jit(solution)/shard_map/ppermute | solution.py:214
  175.5 22.9 %collective-permute-start.14 = (bf16[128,2048]{1,0:T(8,128)(2,1)S(1)}, bf16[128,2048]{1,0:T(8,128)(2,1)S(1)}, u32[]{:S(2)}, u32[]{:S(2)}) collective-permute-start(bf16[128,2048]{1,0:T(8,128)(2,1)S(1)} %get-tuple-element.46), channel_id=1, source_target_pairs={{0,4},{1,5},{2,6},{3,7},{4,0},{5,1},{6,2},{7,3},{8,12},{9,13},{10,... | collective-permute-start | bytes 1572872 | tf_op jit(solution)/shard_map/ppermute | solution.py:214
  177.3 45.5 %collective-permute-start.15 = (bf16[128,2048]{1,0:T(8,128)(2,1)S(1)}, bf16[128,2048]{1,0:T(8,128)(2,1)S(1)}, u32[]{:S(2)}, u32[]{:S(2)}) collective-permute-start(bf16[128,2048]{1,0:T(8,128)(2,1)S(1)} %get-tuple-element.45), channel_id=1, source_target_pairs={{0,6},{1,7},{2,4},{3,5},{4,2},{5,3},{6,0},{7,1},{8,14},{9,15},{10,... | collective-permute-start | bytes 1572872 | tf_op jit(solution)/shard_map/ppermute | solution.py:214
  224.6 14.2 %collective-permute-start.52 = (bf16[128,2048]{1,0:T(8,128)(2,1)S(1)}, bf16[128,2048]{1,0:T(8,128)(2,1)S(1)}, u32[]{:S(2)}, u32[]{:S(2)}) collective-permute-start(bf16[128,2048]{1,0:T(8,128)(2,1)S(1)} %fusion.107), channel_id=1, source_target_pairs={{0,1},{1,0},{2,3},{3,2},{4,5},{5,4},{6,7},{7,6},{8,9},{9,8},{10,11... | collective-permute-start | bytes 1572872 | tf_op jit(solution)/shard_map/ppermute | solution.py:214
  227.0 17.8 %collective-permute-start.53 = (bf16[128,2048]{1,0:T(8,128)(2,1)S(1)}, bf16[128,2048]{1,0:T(8,128)(2,1)S(1)}, u32[]{:S(2)}, u32[]{:S(2)}) collective-permute-start(bf16[128,2048]{1,0:T(8,128)(2,1)S(1)} %fusion.107), channel_id=1, source_target_pairs={{0,16},{1,17},{2,18},{3,19},{4,20},{5,21},{6,22},{7,23},{8,24},{9,... | collective-permute-start | bytes 1572872 | tf_op jit(solution)/shard_map/ppermute | solution.py:214
  231.1 14.2 %collective-permute-start.16 = (bf16[128,2048]{1,0:T(8,128)(2,1)S(1)}, bf16[128,2048]{1,0:T(8,128)(2,1)S(1)}, u32[]{:S(2)}, u32[]{:S(2)}) collective-permute-start(bf16[128,2048]{1,0:T(8,128)(2,1)S(1)} %fusion.107), channel_id=1, source_target_pairs={{0,2},{1,3},{2,0},{3,1},{4,6},{5,7},{6,4},{7,5},{8,10},{9,11},{10,... | collective-permute-start | bytes 1572872 | tf_op jit(solution)/shard_map/ppermute | solution.py:214
  238.9 13.1 %collective-permute-start.54 = (bf16[64,2048]{1,0:T(8,128)(2,1)S(1)}, bf16[64,2048]{1,0:T(8,128)(2,1)S(1)}, u32[]{:S(2)}, u32[]{:S(2)}) collective-permute-start(bf16[64,2048]{1,0:T(8,128)(2,1)S(1)} %slice.500), channel_id=1, source_target_pairs={{0,16},{1,17},{2,18},{3,19},{4,20},{5,21},{6,22},{7,23},{8,24},{9,... | collective-permute-start | bytes 786440 | tf_op jit(solution)/shard_map/ppermute | solution.py:214
  245.3 22.3 %collective-permute-start.28 = (bf16[128,2048]{1,0:T(8,128)(2,1)S(1)}, bf16[128,2048]{1,0:T(8,128)(2,1)S(1)}, u32[]{:S(2)}, u32[]{:S(2)}) collective-permute-start(bf16[128,2048]{1,0:T(8,128)(2,1)S(1)} %fusion.107), channel_id=1, source_target_pairs={{0,4},{1,5},{2,6},{3,7},{4,0},{5,1},{6,2},{7,3},{8,12},{9,13},{10,... | collective-permute-start | bytes 1572872 | tf_op jit(solution)/shard_map/ppermute | solution.py:214
  245.4 17.8 %collective-permute-start.17 = (bf16[128,2048]{1,0:T(8,128)(2,1)S(1)}, bf16[128,2048]{1,0:T(8,128)(2,1)S(1)}, u32[]{:S(2)}, u32[]{:S(2)}) collective-permute-start(bf16[128,2048]{1,0:T(8,128)(2,1)S(1)} %collective-permute-done.16), channel_id=1, source_target_pairs={{0,1},{1,0},{2,3},{3,2},{4,5},{5,4},{6,7},{7,6},{8,9},{9,8},{10,11... | collective-permute-start | bytes 1572872 | tf_op jit(solution)/shard_map/ppermute | solution.py:214
  247.2 16.4 %collective-permute-start.18 = (bf16[128,2048]{1,0:T(8,128)(2,1)S(1)}, bf16[128,2048]{1,0:T(8,128)(2,1)S(1)}, u32[]{:S(2)}, u32[]{:S(2)}) collective-permute-start(bf16[128,2048]{1,0:T(8,128)(2,1)S(1)} %collective-permute-done.16), channel_id=1, source_target_pairs={{0,16},{1,17},{2,18},{3,19},{4,20},{5,21},{6,22},{7,23},{8,24},{9,... | collective-permute-start | bytes 1572872 | tf_op jit(solution)/shard_map/ppermute | solution.py:214
  265.1 27.6 %collective-permute-start.56 = (bf16[192,2048]{1,0:T(8,128)(2,1)S(1)}, bf16[192,2048]{1,0:T(8,128)(2,1)S(1)}, u32[]{:S(2)}, u32[]{:S(2)}) collective-permute-start(bf16[192,2048]{1,0:T(8,128)(2,1)S(1)} %bitcast.312), channel_id=1, source_target_pairs={{0,8},{1,9},{2,10},{3,11},{4,12},{5,13},{6,14},{7,15},{8,0},{9,1},... | collective-permute-start | bytes 2359304 | tf_op jit(solution)/shard_map/ppermute | solution.py:214
  267.6 23.7 %collective-permute-start.40 = (bf16[128,2048]{1,0:T(8,128)(2,1)S(1)}, bf16[128,2048]{1,0:T(8,128)(2,1)S(1)}, u32[]{:S(2)}, u32[]{:S(2)}) collective-permute-start(bf16[128,2048]{1,0:T(8,128)(2,1)S(1)} %fusion.107), channel_id=1, source_target_pairs={{0,6},{1,7},{2,4},{3,5},{4,2},{5,3},{6,0},{7,1},{8,14},{9,15},{10,... | collective-permute-start | bytes 1572872 | tf_op jit(solution)/shard_map/ppermute | solution.py:214
  268.2 13.0 %collective-permute-start.29 = (bf16[128,2048]{1,0:T(8,128)(2,1)S(1)}, bf16[128,2048]{1,0:T(8,128)(2,1)S(1)}, u32[]{:S(2)}, u32[]{:S(2)}) collective-permute-start(bf16[128,2048]{1,0:T(8,128)(2,1)S(1)} %collective-permute-done.28), channel_id=1, source_target_pairs={{0,1},{1,0},{2,3},{3,2},{4,5},{5,4},{6,7},{7,6},{8,9},{9,8},{10,11... | collective-permute-start | bytes 1572872 | tf_op jit(solution)/shard_map/ppermute | solution.py:214
  269.7 13.4 %collective-permute-start.30 = (bf16[128,2048]{1,0:T(8,128)(2,1)S(1)}, bf16[128,2048]{1,0:T(8,128)(2,1)S(1)}, u32[]{:S(2)}, u32[]{:S(2)}) collective-permute-start(bf16[128,2048]{1,0:T(8,128)(2,1)S(1)} %collective-permute-done.28), channel_id=1, source_target_pairs={{0,16},{1,17},{2,18},{3,19},{4,20},{5,21},{6,22},{7,23},{8,24},{9,... | collective-permute-start | bytes 1572872 | tf_op jit(solution)/shard_map/ppermute | solution.py:214
  271.9 33.7 %collective-permute-start.21 = (bf16[192,2048]{1,0:T(8,128)(2,1)S(1)}, bf16[192,2048]{1,0:T(8,128)(2,1)S(1)}, u32[]{:S(2)}, u32[]{:S(2)}) collective-permute-start(bf16[192,2048]{1,0:T(8,128)(2,1)S(1)} %bitcast.305), channel_id=1, source_target_pairs={{0,8},{1,9},{2,10},{3,11},{4,12},{5,13},{6,14},{7,15},{8,0},{9,1},... | collective-permute-start | bytes 2359304 | tf_op jit(solution)/shard_map/ppermute | solution.py:214
  281.3 16.1 %collective-permute-start.31 = (bf16[64,2048]{1,0:T(8,128)(2,1)S(1)}, bf16[64,2048]{1,0:T(8,128)(2,1)S(1)}, u32[]{:S(2)}, u32[]{:S(2)}) collective-permute-start(bf16[64,2048]{1,0:T(8,128)(2,1)S(1)} %slice.468), channel_id=1, source_target_pairs={{0,16},{1,17},{2,18},{3,19},{4,20},{5,21},{6,22},{7,23},{8,24},{9,... | collective-permute-start | bytes 786440 | tf_op jit(solution)/shard_map/ppermute | solution.py:214
  283.1 14.4 %collective-permute-start.32 = (bf16[64,2048]{1,0:T(8,128)(2,1)S(1)}, bf16[64,2048]{1,0:T(8,128)(2,1)S(1)}, u32[]{:S(2)}, u32[]{:S(2)}) collective-permute-start(bf16[64,2048]{1,0:T(8,128)(2,1)S(1)} %slice.469), channel_id=1, source_target_pairs={{0,1},{1,0},{2,3},{3,2},{4,5},{5,4},{6,7},{7,6},{8,9},{9,8},{10,11... | collective-permute-start | bytes 786440 | tf_op jit(solution)/shard_map/ppermute | solution.py:214
  297.4 15.4 %collective-permute-start.57 = (bf16[192,2048]{1,0:T(8,128)(2,1)S(1)}, bf16[192,2048]{1,0:T(8,128)(2,1)S(1)}, u32[]{:S(2)}, u32[]{:S(2)}) collective-permute-start(bf16[192,2048]{1,0:T(8,128)(2,1)S(1)} %get-tuple-element.60), channel_id=1, source_target_pairs={{0,8},{1,9},{2,10},{3,11},{4,12},{5,13},{6,14},{7,15},{8,0},{9,1},... | collective-permute-start | bytes 2359304 | tf_op jit(solution)/shard_map/ppermute | solution.py:214
  298.3 17.6 %collective-permute-start.33 = (bf16[192,2048]{1,0:T(8,128)(2,1)S(1)}, bf16[192,2048]{1,0:T(8,128)(2,1)S(1)}, u32[]{:S(2)}, u32[]{:S(2)}) collective-permute-start(bf16[192,2048]{1,0:T(8,128)(2,1)S(1)} %bitcast.308), channel_id=1, source_target_pairs={{0,8},{1,9},{2,10},{3,11},{4,12},{5,13},{6,14},{7,15},{8,0},{9,1},... | collective-permute-start | bytes 2359304 | tf_op jit(solution)/shard_map/ppermute | solution.py:214
  310.1 15.7 %collective-permute-start.22 = (bf16[192,2048]{1,0:T(8,128)(2,1)S(1)}, bf16[192,2048]{1,0:T(8,128)(2,1)S(1)}, u32[]{:S(2)}, u32[]{:S(2)}) collective-permute-start(bf16[192,2048]{1,0:T(8,128)(2,1)S(1)} %get-tuple-element.48), channel_id=1, source_target_pairs={{0,8},{1,9},{2,10},{3,11},{4,12},{5,13},{6,14},{7,15},{8,0},{9,1},... | collective-permute-start | bytes 2359304 | tf_op jit(solution)/shard_map/ppermute | solution.py:214
  312.7 17.4 %collective-permute-start.45 = (bf16[192,2048]{1,0:T(8,128)(2,1)S(1)}, bf16[192,2048]{1,0:T(8,128)(2,1)S(1)}, u32[]{:S(2)}, u32[]{:S(2)}) collective-permute-start(bf16[192,2048]{1,0:T(8,128)(2,1)S(1)} %bitcast.307), channel_id=1, source_target_pairs={{0,8},{1,9},{2,10},{3,11},{4,12},{5,13},{6,14},{7,15},{8,0},{9,1},... | collective-permute-start | bytes 2359304 | tf_op jit(solution)/shard_map/ppermute | solution.py:214
  320.1 23.7 %collective-permute-start.34 = (bf16[192,2048]{1,0:T(8,128)(2,1)S(1)}, bf16[192,2048]{1,0:T(8,128)(2,1)S(1)}, u32[]{:S(2)}, u32[]{:S(2)}) collective-permute-start(bf16[192,2048]{1,0:T(8,128)(2,1)S(1)} %get-tuple-element.52), channel_id=1, source_target_pairs={{0,8},{1,9},{2,10},{3,11},{4,12},{5,13},{6,14},{7,15},{8,0},{9,1},... | collective-permute-start | bytes 2359304 | tf_op jit(solution)/shard_map/ppermute | solution.py:214
  324.7 76.9 %collective-permute-start.59 = (bf16[128,2048]{1,0:T(8,128)(2,1)}, bf16[128,2048]{1,0:T(8,128)(2,1)}, u32[]{:S(2)}, u32[]{:S(2)}) collective-permute-start(bf16[128,2048]{1,0:T(8,128)(2,1)} %pad_maximum_fusion.7), channel_id=1, source_target_pairs={{0,1},{1,0},{2,3},{3,2},{4,5},{5,4},{6,7},{7,6},{8,9},{9,8},{10,11... | collective-permute-start | bytes 1572872 | tf_op jit(solution)/shard_map/ppermute | solution.py:214
  328.3 15.3 %collective-permute-start.25 = (bf16[64,2048]{1,0:T(8,128)(2,1)S(1)}, bf16[64,2048]{1,0:T(8,128)(2,1)S(1)}, u32[]{:S(2)}, u32[]{:S(2)}) collective-permute-start(bf16[64,2048]{1,0:T(8,128)(2,1)S(1)} %get-tuple-element.23), channel_id=1, source_target_pairs={{0,1},{1,0},{2,3},{3,2},{4,5},{5,4},{6,7},{7,6},{8,9},{9,8},{10,11... | collective-permute-start | bytes 786440 | tf_op jit(solution)/shard_map/ppermute | solution.py:214
  334.3 21.5 %collective-permute-start.46 = (bf16[192,2048]{1,0:T(8,128)(2,1)S(1)}, bf16[192,2048]{1,0:T(8,128)(2,1)S(1)}, u32[]{:S(2)}, u32[]{:S(2)}) collective-permute-start(bf16[192,2048]{1,0:T(8,128)(2,1)S(1)} %get-tuple-element.56), channel_id=1, source_target_pairs={{0,8},{1,9},{2,10},{3,11},{4,12},{5,13},{6,14},{7,15},{8,0},{9,1},... | collective-permute-start | bytes 2359304 | tf_op jit(solution)/shard_map/ppermute | solution.py:214
  346.7 25.1 %collective-permute-start.24 = (bf16[128,2048]{1,0:T(8,128)(2,1)S(1)}, bf16[128,2048]{1,0:T(8,128)(2,1)S(1)}, u32[]{:S(2)}, u32[]{:S(2)}) collective-permute-start(bf16[128,2048]{1,0:T(8,128)(2,1)S(1)} %pad_maximum_fusion.1), channel_id=1, source_target_pairs={{0,1},{1,0},{2,3},{3,2},{4,5},{5,4},{6,7},{7,6},{8,9},{9,8},{10,11... | collective-permute-start | bytes 1572872 | tf_op jit(solution)/shard_map/ppermute | solution.py:214
  352.0 20.6 %collective-permute-start.26 = (bf16[128,2048]{1,0:T(8,128)(2,1)S(1)}, bf16[128,2048]{1,0:T(8,128)(2,1)S(1)}, u32[]{:S(2)}, u32[]{:S(2)}) collective-permute-start(bf16[128,2048]{1,0:T(8,128)(2,1)S(1)} %pad_maximum_fusion.2), channel_id=1, source_target_pairs={{0,16},{1,17},{2,18},{3,19},{4,20},{5,21},{6,22},{7,23},{8,24},{9,... | collective-permute-start | bytes 1572872 | tf_op jit(solution)/shard_map/ppermute | solution.py:214
  369.2 14.9 %collective-permute-start.36 = (bf16[128,2048]{1,0:T(8,128)(2,1)S(1)}, bf16[128,2048]{1,0:T(8,128)(2,1)S(1)}, u32[]{:S(2)}, u32[]{:S(2)}) collective-permute-start(bf16[128,2048]{1,0:T(8,128)(2,1)S(1)} %pad_maximum_fusion.3), channel_id=1, source_target_pairs={{0,1},{1,0},{2,3},{3,2},{4,5},{5,4},{6,7},{7,6},{8,9},{9,8},{10,11... | collective-permute-start | bytes 1572872 | tf_op jit(solution)/shard_map/ppermute | solution.py:214
  370.8 14.9 %collective-permute-start.38 = (bf16[128,2048]{1,0:T(8,128)(2,1)S(1)}, bf16[128,2048]{1,0:T(8,128)(2,1)S(1)}, u32[]{:S(2)}, u32[]{:S(2)}) collective-permute-start(bf16[128,2048]{1,0:T(8,128)(2,1)S(1)} %pad_maximum_fusion.4), channel_id=1, source_target_pairs={{0,16},{1,17},{2,18},{3,19},{4,20},{5,21},{6,22},{7,23},{8,24},{9,... | collective-permute-start | bytes 1572872 | tf_op jit(solution)/shard_map/ppermute | solution.py:214
  371.8 20.2 %collective-permute-start.48 = (bf16[128,2048]{1,0:T(8,128)(2,1)S(1)}, bf16[128,2048]{1,0:T(8,128)(2,1)S(1)}, u32[]{:S(2)}, u32[]{:S(2)}) collective-permute-start(bf16[128,2048]{1,0:T(8,128)(2,1)S(1)} %pad_maximum_fusion.5), channel_id=1, source_target_pairs={{0,1},{1,0},{2,3},{3,2},{4,5},{5,4},{6,7},{7,6},{8,9},{9,8},{10,11... | collective-permute-start | bytes 1572872 | tf_op jit(solution)/shard_map/ppermute | solution.py:214
  372.6 24.3 %collective-permute-start.50 = (bf16[128,2048]{1,0:T(8,128)(2,1)S(1)}, bf16[128,2048]{1,0:T(8,128)(2,1)S(1)}, u32[]{:S(2)}, u32[]{:S(2)}) collective-permute-start(bf16[128,2048]{1,0:T(8,128)(2,1)S(1)} %pad_maximum_fusion.6), channel_id=1, source_target_pairs={{0,16},{1,17},{2,18},{3,19},{4,20},{5,21},{6,22},{7,23},{8,24},{9,... | collective-permute-start | bytes 1572872 | tf_op jit(solution)/shard_map/ppermute | solution.py:214
  384.0 19.2 %collective-permute-start.61 = (bf16[128,2048]{1,0:T(8,128)(2,1)}, bf16[128,2048]{1,0:T(8,128)(2,1)}, u32[]{:S(2)}, u32[]{:S(2)}) collective-permute-start(bf16[128,2048]{1,0:T(8,128)(2,1)} %pad_maximum_fusion.8), channel_id=1, source_target_pairs={{0,16},{1,17},{2,18},{3,19},{4,20},{5,21},{6,22},{7,23},{8,24},{9,... | collective-permute-start | bytes 1572872 | tf_op jit(solution)/shard_map/ppermute | solution.py:214
  385.6 17.6 %collective-permute-start.27 = (bf16[128,2048]{1,0:T(8,128)(2,1)}, bf16[128,2048]{1,0:T(8,128)(2,1)}, u32[]{:S(2)}, u32[]{:S(2)}) collective-permute-start(bf16[128,2048]{1,0:T(8,128)(2,1)} %fusion.118), channel_id=1, source_target_pairs={{0,2},{1,3},{2,0},{3,1},{4,6},{5,7},{6,4},{7,5},{8,10},{9,11},{10,... | collective-permute-start | bytes 1572872 | tf_op jit(solution)/shard_map/ppermute | solution.py:214
  392.1 34.0 %collective-permute-start.39 = (bf16[128,2048]{1,0:T(8,128)(2,1)}, bf16[128,2048]{1,0:T(8,128)(2,1)}, u32[]{:S(2)}, u32[]{:S(2)}) collective-permute-start(bf16[128,2048]{1,0:T(8,128)(2,1)} %fusion.116), channel_id=1, source_target_pairs={{0,4},{1,5},{2,6},{3,7},{4,0},{5,1},{6,2},{7,3},{8,12},{9,13},{10,... | collective-permute-start | bytes 1572872 | tf_op jit(solution)/shard_map/ppermute | solution.py:214
  398.0 38.0 %collective-permute-start.51 = (bf16[128,2048]{1,0:T(8,128)(2,1)}, bf16[128,2048]{1,0:T(8,128)(2,1)}, u32[]{:S(2)}, u32[]{:S(2)}) collective-permute-start(bf16[128,2048]{1,0:T(8,128)(2,1)} %fusion.114), channel_id=1, source_target_pairs={{0,6},{1,7},{2,4},{3,5},{4,2},{5,3},{6,0},{7,1},{8,14},{9,15},{10,... | collective-permute-start | bytes 1572872 | tf_op jit(solution)/shard_map/ppermute | solution.py:214
  (36 other events, 758.4 us)

commit v2 on v1

--- a/solution.py
+++ b/solution.py
@@ -238,14 +238,13 @@
     place, low, projected, gain, cosine, sine, start, kv_here, kv_side, kv_before, kv_before_side, out,
     keys, values, acc, peak, total,
 ):
-    slot = pl.program_id(0)
-    z, x = place[0], place[1]
+    z, x, slot = place[0], place[1], place[2] + pl.program_id(0)
     rows = projected.shape[0]
     head = gain.shape[0]
     heads = projected.shape[1] // head
     half = head // 2
 
-    @pl.when(slot == 0)
+    @pl.when(pl.program_id(0) == 0)
     def _():
         for first, near, far in ((0, kv_before, kv_before_side), (8, kv_here, kv_side)):
             for k in range(4):
@@ -291,7 +290,7 @@
         peak[...] = largest
         return 0
 
-    lax.fori_loop(low[slot], (position + rows - 1) // KEY_BLOCK + 1, step, 0)
+    lax.fori_loop(low[pl.program_id(0)], (position + rows - 1) // KEY_BLOCK + 1, step, 0)
     mixed = acc[...] / total[...]
     for h in range(heads):
         out[:, h * head : (h + 1) * head] = mixed[:, h * rows : (h + 1) * rows].T.astype(out.dtype)
@@ -335,6 +334,52 @@
     )(place, low, projected, q_gain.reshape(head, 1), cosine, sine, start, *kv)
 
 
+def keyval_kernel(tokens, gain, key_gain, cosine, sine, w_key, w_value, out, normed):
+    @pl.when(pl.program_id(0) == 0)
+    def _():
+        normed[...] = root_mean_norm(tokens[...].astype(jnp.float32), gain[...]).astype(jnp.bfloat16)
+
+    head = key_gain.shape[0]
+    half = head // 2
+    k = jnp.dot(normed[...], w_key[...], preferred_element_type=jnp.float32).T
+    k = k * lax.rsqrt(jnp.mean(k * k, axis=0, keepdims=True) + 1e-06) * key_gain[...]
+    first, second = k[:half], k[half:]
+    k = jnp.concatenate(
+        [first * cosine[0] - second * sine[0], second * cosine[0] + first * sine[0]], axis=0
+    )
+    out[0, :, :head] = k.T.astype(out.dtype)
+    v = jnp.dot(normed[...], w_value[...], preferred_element_type=jnp.float32)
+    out[0, :, head:] = v.astype(out.dtype)
+
+
+def keyval_by_head(tokens, attn_gain, key_norm_gain, cosine, sine, w_keyval):
+    rows, width = tokens.shape
+    head = key_norm_gain.shape[0]
+    heads = w_keyval.shape[1] // (2 * head)
+    whole = lambda *shape: pl.BlockSpec(shape, lambda h: (0,) * len(shape))
+    return pl.pallas_call(
+        keyval_kernel,
+        grid=(heads,),
+        in_specs=[
+            whole(rows, width),
+            whole(1, width),
+            whole(head, 1),
+            whole(1, head // 2, rows),
+            whole(1, head // 2, rows),
+            pl.BlockSpec((width, head), lambda h: (0, h)),
+            pl.BlockSpec((width, head), lambda h: (0, heads + h)),
+        ],
+        out_specs=pl.BlockSpec((1, rows, 2 * head), lambda h: (h, 0, 0)),
+        out_shape=jax.ShapeDtypeStruct((heads, rows, 2 * head), jnp.bfloat16),
+        scratch_shapes=[pltpu.VMEM((rows, width), jnp.bfloat16)],
+        compiler_params=pltpu.CompilerParams(vmem_limit_bytes=32 * 2**20),
+        cost_estimate=pl.CostEstimate(
+            flops=2 * rows * width * w_keyval.shape[1], bytes_accessed=5 * 2**20, transcendentals=0
+        ),
+        name="keyval",
+    )(tokens, attn_gain.reshape(1, width), key_norm_gain.reshape(head, 1), cosine, sine, w_keyval, w_keyval)
+
+
 def grid_body(
     tokens,
     seg_ids,
@@ -362,84 +407,83 @@
     slots = range(4)
 
     raw = [tokens] + [other_z(tokens, k) for k in (1, 2, 3)]
-    half_heads = w_query.shape[1] // 2
-    query_half = other_x(lax.dynamic_slice_in_dim(w_query, core * half_heads, half_heads, 1))
-    query_rest = other_core(query_half)
-    out_half = other_x(
-        after(lax.dynamic_slice_in_dim(w_out, core * half_heads, half_heads, 0), query_half)
-    )
-    out_rest = other_core(out_half)
-
-    routes = jnp.concatenate([expert_ids.T.astype(jnp.bfloat16), gates.T], axis=0)
-    routes = lax.all_gather(routes, ("rep", "tp"), axis=0, tiled=True)
-
-    normed = root_mean_norm(tokens.astype(jnp.float32), attn_gain).astype(jnp.bfloat16)
-    own_position = (group_start + tp * rows + jnp.arange(rows, dtype=jnp.int32)).astype(jnp.float32)
-    keyval = jnp.dot(normed, w_keyval, preferred_element_type=jnp.float32)
-    rotated = apply_rotary(
-        root_mean_norm(keyval[:, :kv_width].reshape(rows, kv_heads, head), key_norm_gain), own_position
-    )
-    stored = jnp.concatenate([rotated.reshape(rows, kv_width), keyval[:, kv_width:]], axis=1).astype(
-        jnp.bfloat16
-    )
-    pages = page_table.shape[0]
-    placing = (page_table[None, :] == jnp.arange(pages, dtype=jnp.int32)[:, None]).astype(jnp.bfloat16)
-    cache = jnp.dot(placing, stored.reshape(pages, -1), preferred_element_type=jnp.float32)
-    cache = cache.astype(jnp.bfloat16).reshape(pages, rows // pages, 2 * kv_width)
-
-    by_head = jnp.transpose(stored.reshape(rows, 2, kv_heads, head), (2, 0, 1, 3))
-    by_head = by_head.reshape(kv_heads, rows, 2 * head)
+
+    slot_z = jnp.stack([z ^ k for k in slots])
+    slot_position = group_start + ((slot_z * 2 + x) * rows)[:, None] + jnp.arange(rows, dtype=jnp.int32)
+    frequency = jnp.exp(
+        jnp.arange(head // 2, dtype=jnp.float32) * (-2.0 * math.log(1000000.0) / head)
+    )
+    angles = frequency[None, :, None] * slot_position.astype(jnp.float32)[:, None, :]
+    cosine, sine = jnp.cos(angles), jnp.sin(angles)
+
+    by_head = keyval_by_head(tokens, attn_gain, key_norm_gain, cosine[:1], sine[:1], w_keyval)
     pick = lambda h: lax.dynamic_index_in_dim(by_head, h, 0, keepdims=False)
     kv_here = jnp.stack([pick(z)] + [other_z(pick(z ^ k), k) for k in (1, 2, 3)])
     kv_before = passed_along(kv_here, "rep", 1)
     kv_side = other_x(kv_here)
     kv_before_side = other_x(kv_before)
 
-    slot_z = jnp.stack([z ^ k for k in slots])
-    slot_rows = ((slot_z * 2 + x) * rows)[:, None] + jnp.arange(rows, dtype=jnp.int32)[None, :]
-    slot_position = group_start + slot_rows
-    frequency = jnp.exp(
-        jnp.arange(head // 2, dtype=jnp.float32) * (-2.0 * math.log(1000000.0) / head)
-    )
-    angles = frequency[None, :, None] * slot_position.astype(jnp.float32)[:, None, :]
+    half_heads = w_query.shape[1] // 2
+    query_half = other_x(
+        lax.dynamic_slice_in_dim(after(w_query, by_head), core * half_heads, half_heads, 1)
+    )
+    query_rest = other_core(query_half)
+    out_half = other_x(
+        lax.dynamic_slice_in_dim(after(w_out, query_half), core * half_heads, half_heads, 0)
+    )
+    out_rest = other_core(out_half)
+
+    top = expert_ids.shape[1]
+    routes = jnp.concatenate([expert_ids.T.astype(jnp.bfloat16), gates.T], axis=0)
+    routes = after(routes, by_head)
+    routes = jnp.stack([routes] + [other_z(routes, k) for k in (1, 2, 3)])
+    routes = jnp.stack([routes, other_x(routes)], axis=1)
+    routes = jnp.concatenate([routes, other_y(routes)], axis=1).reshape(16, 2, top, rows)
+
+    pages = page_table.shape[0]
+    stored = jnp.transpose(by_head.reshape(kv_heads, rows, 2, head), (1, 2, 0, 3))
+    placing = (page_table[None, :] == jnp.arange(pages, dtype=jnp.int32)[:, None]).astype(jnp.bfloat16)
+    cache = jnp.dot(placing, stored.reshape(pages, -1), preferred_element_type=jnp.float32)
+    cache = cache.astype(jnp.bfloat16).reshape(pages, rows // pages, 2 * kv_width)
+
     slot_seg = jnp.take(seg_ids, slot_position.reshape(-1), axis=0)
     starts = jnp.sum((seg_ids[None, :] < slot_seg[:, None]).astype(jnp.int32), axis=1)
     starts = (starts - (group_start - group_rows)).reshape(4, 1, rows)
     low = starts[:, 0, 0] // KEY_BLOCK
-    lines = jnp.concatenate(raw, axis=0).astype(jnp.float32)
-    normed_lines = root_mean_norm(lines, attn_gain).astype(jnp.bfloat16)
     w_query_wide = jnp.concatenate([w_query, query_half, query_rest], axis=1)
-    projected = jnp.dot(normed_lines, w_query_wide, preferred_element_type=jnp.float32)
-    attended = attend_slots(
-        jnp.stack([z, x]),
-        low,
-        projected,
-        q_gain,
-        jnp.cos(angles),
-        jnp.sin(angles),
-        starts,
-        (kv_here, kv_side, kv_before, kv_before_side),
-    )
     w_out_wide = jnp.concatenate([w_out, out_half, out_rest], axis=0)
-    term = jnp.dot(attended, w_out_wide, preferred_element_type=jnp.float32).astype(jnp.bfloat16)
-    term = term.reshape(4, rows, width)
-    mixed_sum = term[0].astype(jnp.float32)
-    for k in (1, 2, 3):
-        mixed_sum = mixed_sum + other_z(term[k], k).astype(jnp.float32)
+
+    def attended(first):
+        two = slice(first, first + 2)
+        lines = jnp.concatenate(raw[two], axis=0).astype(jnp.float32)
+        lines = root_mean_norm(lines, attn_gain).astype(jnp.bfloat16)
+        projected = jnp.dot(lines, w_query_wide, preferred_element_type=jnp.float32)
+        return attend_slots(
+            jnp.stack([z, x, jnp.int32(first)]),
+            low[two],
+            projected,
+            q_gain,
+            cosine[two],
+            sine[two],
+            starts[two],
+            (kv_here, kv_side, kv_before, kv_before_side),
+        )
+
+    def term_of(part):
+        term = jnp.dot(part, w_out_wide, preferred_element_type=jnp.float32).astype(jnp.bfloat16)
+        return term[:rows], term[rows:]
+
+    early = attended(0)
+    term_2, term_3 = term_of(attended(2))
+    far = [other_z(term_2, 2), other_z(term_3, 3)]
+    term_0, term_1 = term_of(after(early, term_3))
+    mixed_sum = term_0.astype(jnp.float32)
+    for part in [other_z(term_1, 1)] + far:
+        mixed_sum = mixed_sum + part.astype(jnp.float32)
     residual = (tokens.astype(jnp.float32) + mixed_sum).astype(jnp.bfloat16)
     normed_moe = root_mean_norm(residual.astype(jnp.float32), moe_gain).astype(jnp.bfloat16)
 
-    top = expert_ids.shape[1]
     capacity = max(2, 3 * rows * top // (2 * 32))
-    routes = routes.reshape(32, 2, top, rows)
-    block_of = jnp.stack(
-        [
-            ((y ^ dy) * 2 + core) * 8 + (z ^ k) * 2 + (x ^ dx)
-            for k in slots
-            for dy, dx in ((0, 0), (0, 1), (1, 0), (1, 1))
-        ]
-    )
-    routes = jnp.take(routes, block_of, axis=0)
     experts = jnp.stack([rep * 8 + tp, (rep ^ 1) * 8 + tp])
     hits = routes[:, 0][:, None] == experts.astype(jnp.bfloat16)[None, :, None, None]
     weight = jnp.sum(jnp.where(hits, routes[:, 1][:, None].astype(jnp.float32), 0.0), axis=2)
@@ -464,13 +508,15 @@
         return jnp.dot(act, w_down[0], preferred_element_type=jnp.float32).astype(jnp.bfloat16)
 
     half = rows // 2
-    arrived = [normed_moe]
-    for k in (1, 2, 3):
-        arrived.append(other_z(after(normed_moe, arrived[-1]) if k > 1 else normed_moe, k))
+    arrived = [normed_moe, other_z(normed_moe, 1)]
+    arrived.append(other_z(after(normed_moe, arrived[1]), 2))
+    arrived.append(other_z(after(normed_moe, arrived[2]), 3))
     partial = []
+    turn = normed_moe
     for k in slots:
-        block = arrived[k]
+        block, turn = lax.optimization_barrier((arrived[k], turn))
         side_x, side_y = other_x(block), other_y(block)
+        turn = side_x
         corner = jnp.concatenate([other_y(side_x[:half]), other_x(side_y[half:])], axis=0)
         blocks = jnp.stack([block, side_x, side_y, corner])
         picked = lax.dot_general(
@@ -490,10 +536,13 @@
             ).astype(jnp.bfloat16)
         )
     combined = residual.astype(jnp.float32)
-    for k in (1, 2, 3, 0):
-        here, to_x, to_y, to_corner = (partial[k][v] for v in range(4))
+    add = lambda a, b: (a.astype(jnp.float32) + b.astype(jnp.float32)).astype(jnp.bfloat16)
+    turn = partial[2]
+    for k in (2, 3, 1, 0):
+        partial_k, turn = lax.optimization_barrier((partial[k], turn))
+        here, to_x, to_y, to_corner = (partial_k[v] for v in range(4))
         by_y, by_x = other_y(to_corner[:half]), other_x(to_corner[half:])
-        add = lambda a, b: (a.astype(jnp.float32) + b.astype(jnp.float32)).astype(jnp.bfloat16)
+        turn = by_x
         from_x = other_x(jnp.concatenate([add(to_x[:half], by_y), to_x[half:]], axis=0))
         from_y = other_y(jnp.concatenate([to_y[:half], add(to_y[half:], by_x)], axis=0))
         total = here.astype(jnp.float32) + from_x.astype(jnp.float32) + from_y.astype(jnp.float32)

time: 447 us -> 382 us (0.85)
  the two profiles are of different devices: /device:TPU:8 before, /device:TPU:0 now
where the time goes in v2:
time: 382 us; the launch traced here: 374 us
  waiting for transfers between devices  202 us (53%)
  starting transfers between devices  82.2 us (22%)
  matrix products  30.8 us (8%)
  local copies, waits for them, and re-layouts  28.3 us (7%)
  other arithmetic  15.5 us (4%)
  Pallas kernels  12.8 us (3%)
    ppermute x66, waiting for transfers between devices, moved(): return lax.ppermute(block, ('rep', 'tp'), route)  202 us
    ppermute x66, starting transfers between devices, moved(): return lax.ppermute(block, ('rep', 'tp'), route)  80.9 us
    unnamed x53, local copies, waits for them, and re-layouts  11.8 us
    dot_general x4, matrix products, experts_of(): jnp.dot(slot_rows_in, w_gate_up[0], preferred_element_type=jnp.float32)  10.7 us
    pallas_call x2, Pallas kernels, attend_slots(): pl.pallas_call(attention_kernel, grid_spec=pltpu.PrefetchScalarGridSpec(n...  9.46 us
  transfers between devices with their start and end apart: 67, of which 30 were waited for; matrix products, arithmetic and copies ran while one was open for 17% of the time, Pallas kernels for 3%

profile of v2, /device:TPU:0, one launch (start us, length us, event | category | flops | bytes accessed | tf_op | source)
XLA Modules:
  0.0 374.2 jit_solution(17409575869432634280)
XLA Ops:
  0.6 3.1 collective-permute-start
  5.3 2.2 copy-done.1
  9.2 3.3 keyval.1
  12.6 2.3 constant_dynamic-slice_fusion.2
  17.5 2.6 collective-permute-start.4
  23.1 3.1 gather_fusion
  27.6 3.3 constant_dynamic-update-slice_fusion.2
  33.8 2.5 collective-permute-start.10
  36.3 1.9 collective-permute-start.16
  39.8 2.6 collective-permute-start.17
  42.4 15.4 %collective-permute-done.16 = bf16[16,128]{1,0:T(8,128)(2,1)S(1)} collective-permute-done((bf16[16,128]{1,0:T(8,128)(2,1)}, bf16[16,128]{1,0:T(8,128)(2,1)S(1)}, u32[]{:S(2)}, u32[]{:S(2)}) %collective-permute-start.16) | collective-permute-done | bytes 4128 | tf_op jit(solution)/shard_map/ppermute | solution.py:214
  60.4 19.8 %collective-permute-done.17 = bf16[16,128]{1,0:T(8,128)(2,1)S(1)} collective-permute-done((bf16[16,128]{1,0:T(8,128)(2,1)}, bf16[16,128]{1,0:T(8,128)(2,1)S(1)}, u32[]{:S(2)}, u32[]{:S(2)}) %collective-permute-start.17) | collective-permute-done | bytes 4128 | tf_op jit(solution)/shard_map/ppermute | solution.py:214
  82.1 2.0 collective-permute-start.2
  90.8 15.5 %collective-permute-done.11 = bf16[256,2048]{1,0:T(8,128)(2,1)S(1)} collective-permute-done((bf16[256,2048]{1,0:T(8,128)(2,1)S(1)}, bf16[256,2048]{1,0:T(8,128)(2,1)S(1)}, u32[]{:S(2)}, u32[]{:S(2)}) %collective-permute-start.11) | collective-permute-done | bytes 1048608 | tf_op jit(solution)/shard_map/ppermute | solution.py:214
  106.3 2.7 collective-permute-start.12
  109.2 2.4 fusion.95.projected
  112.3 5.6 %collective-permute-done.8.kv_before_side = bf16[4,128,256]{2,1,0:T(8,128)(2,1)S(1)} collective-permute-done((bf16[4,128,256]{2,1,0:T(8,128)(2,1)S(1)}, bf16[4,128,256]{2,1,0:T(8,128)(2,1)S(1)}, u32[]{:S(2)}, u32[]{:S(2)}) %collective-permute-start.8) | collective-permute-done | bytes 262176 | tf_op jit(solution)/shard_map/ppermute | solution.py:214
  117.9 4.0 %attention.2 = bf16[256,1024]{1,0:T(8,128)(2,1)S(1)} custom-call(s32[3]{0:T(128)S(1)} %pad_add_fusion.place, s32[2]{0:T(128)S(1)} %get-tuple-element.100.low, f32[256,1024]{1,0:T(8,128)S(1)} %fusion.95.projected, f32[128,1]{1,0:T(8,128)S(1)} %copy.65.gain, f32[2,64,128]{2,1,0:T(8,128)S(1)} %copy-done.6, f32[2,64,128]{2,1,0:T(8,128)S(1)} %copy-done.5, ...), custom_call_target="tpu_custom_call" | custom-call | flops 536870912 | bytes 8388608 | tf_op jit(solution)/shard_map/attention/pallas_call | solution.py:304
  123.2 5.5 %attention.3 = bf16[256,1024]{1,0:T(8,128)(2,1)S(1)} custom-call(s32[3]{0:T(128)S(1)} %pad_add_fusion.2.place, s32[2]{0:T(128)S(1)} %get-tuple-element.101.low, f32[256,1024]{1,0:T(8,128)S(1)} %fusion.93.projected, f32[128,1]{1,0:T(8,128)S(1)} %copy.65.gain, f32[2,64,128]{2,1,0:T(8,128)S(1)} %copy-done.4, f32[2,64,128]{2,1,0:T(8,128)S(1)} %get-tuple-element.89.sine, ...), custom_call_target="tpu_custom_call" | custom-call | flops 536870912 | bytes 8388608 | tf_op jit(solution)/shard_map/attention/pallas_call | solution.py:304
  130.3 2.7 collective-permute-start.15
  136.1 4.1 %collective-permute-start.20 = (bf16[4,2,16,128]{3,2,1,0:T(8,128)(2,1)S(1)}, bf16[4,2,16,128]{3,2,1,0:T(8,128)(2,1)S(1)}, u32[]{:S(2)}, u32[]{:S(2)}) collective-permute-start(bf16[4,2,16,128]{3,2,1,0:T(8,128)(2,1)S(1)} %pad_maximum_fusion.14), channel_id=1, source_target_pairs={{0,16},{1,17},{2,18},{3,19},{4,20},{5,21},{6,22},{7,23},{8,24},{9,... | collective-permute-start | bytes 98312 | tf_op jit(solution)/shard_map/ppermute | solution.py:214
  140.3 1.8 collective-permute-done.20
  142.2 18.8 %collective-permute-done.13 = bf16[128,2048]{1,0:T(8,128)(2,1)S(1)} collective-permute-done((bf16[128,2048]{1,0:T(8,128)(2,1)S(1)}, bf16[128,2048]{1,0:T(8,128)(2,1)S(1)}, u32[]{:S(2)}, u32[]{:S(2)}) %collective-permute-start.13) | collective-permute-done | bytes 524320 | tf_op jit(solution)/shard_map/ppermute | solution.py:214
  160.9 17.1 %collective-permute-done.14 = bf16[128,2048]{1,0:T(8,128)(2,1)S(1)} collective-permute-done((bf16[128,2048]{1,0:T(8,128)(2,1)S(1)}, bf16[128,2048]{1,0:T(8,128)(2,1)S(1)}, u32[]{:S(2)}, u32[]{:S(2)}) %collective-permute-start.14) | collective-permute-done | bytes 524320 | tf_op jit(solution)/shard_map/ppermute | solution.py:214
  180.3 13.3 %collective-permute-done.23 = bf16[128,2048]{1,0:T(8,128)(2,1)S(1)} collective-permute-done((bf16[128,2048]{1,0:T(8,128)(2,1)S(1)}, bf16[128,2048]{1,0:T(8,128)(2,1)S(1)}, u32[]{:S(2)}, u32[]{:S(2)}) %collective-permute-start.23) | collective-permute-done | bytes 524320 | tf_op jit(solution)/shard_map/ppermute | solution.py:214
  196.1 2.0 collective-permute-start.48
  198.1 4.9 %collective-permute-done.59 = bf16[64,2048]{1,0:T(8,128)(2,1)S(1)} collective-permute-done((bf16[64,2048]{1,0:T(8,128)(2,1)S(1)}, bf16[64,2048]{1,0:T(8,128)(2,1)S(1)}, u32[]{:S(2)}, u32[]{:S(2)}) %collective-permute-start.59) | collective-permute-done | bytes 262176 | tf_op jit(solution)/shard_map/ppermute | solution.py:214
  203.7 8.9 %collective-permute-done.24 = bf16[128,2048]{1,0:T(8,128)(2,1)S(1)} collective-permute-done((bf16[128,2048]{1,0:T(8,128)(2,1)S(1)}, bf16[128,2048]{1,0:T(8,128)(2,1)S(1)}, u32[]{:S(2)}, u32[]{:S(2)}) %collective-permute-start.24) | collective-permute-done | bytes 524320 | tf_op jit(solution)/shard_map/ppermute | solution.py:214
  215.3 6.3 %collective-permute-done.22 = bf16[128,2048]{1,0:T(8,128)(2,1)S(1)} collective-permute-done((bf16[128,2048]{1,0:T(8,128)(2,1)S(1)}, bf16[128,2048]{1,0:T(8,128)(2,1)S(1)}, u32[]{:S(2)}, u32[]{:S(2)}) %collective-permute-start.22) | collective-permute-done | bytes 524320 | tf_op jit(solution)/shard_map/ppermute | solution.py:214
  222.8 1.8 collective-permute-start.36
  225.5 9.9 %collective-permute-done.25 = bf16[128,2048]{1,0:T(8,128)(2,1)S(1)} collective-permute-done((bf16[128,2048]{1,0:T(8,128)(2,1)S(1)}, bf16[128,2048]{1,0:T(8,128)(2,1)S(1)}, u32[]{:S(2)}, u32[]{:S(2)}) %collective-permute-start.25) | collective-permute-done | bytes 524320 | tf_op jit(solution)/shard_map/ppermute | solution.py:214
  235.4 2.6 collective-permute-done.36
  242.3 2.6 fusion
  246.5 10.6 %collective-permute-done.27 = bf16[64,2048]{1,0:T(8,128)(2,1)S(1)} collective-permute-done((bf16[64,2048]{1,0:T(8,128)(2,1)S(1)}, bf16[64,2048]{1,0:T(8,128)(2,1)S(1)}, u32[]{:S(2)}, u32[]{:S(2)}) %collective-permute-start.27) | collective-permute-done | bytes 262176 | tf_op jit(solution)/shard_map/ppermute | solution.py:214
  260.7 2.8 fusion.2
  270.1 2.6 fusion.6
  276.2 2.6 fusion.4
  283.2 6.8 %collective-permute-done.31 = bf16[64,2048]{1,0:T(8,128)(2,1)S(1)} collective-permute-done((bf16[64,2048]{1,0:T(8,128)(2,1)S(1)}, bf16[64,2048]{1,0:T(8,128)(2,1)S(1)}, u32[]{:S(2)}, u32[]{:S(2)}) %collective-permute-start.31) | collective-permute-done | bytes 262176 | tf_op jit(solution)/shard_map/ppermute | solution.py:214
  296.5 8.9 %collective-permute-done.32 = bf16[128,2048]{1,0:T(8,128)(2,1)S(1)} collective-permute-done((bf16[128,2048]{1,0:T(8,128)(2,1)S(1)}, bf16[128,2048]{1,0:T(8,128)(2,1)S(1)}, u32[]{:S(2)}, u32[]{:S(2)}) %collective-permute-start.32) | collective-permute-done | bytes 524320 | tf_op jit(solution)/shard_map/ppermute | solution.py:214
  307.2 8.9 %collective-permute-start.35 = (bf16[128,2048]{1,0:T(8,128)(2,1)}, bf16[128,2048]{1,0:T(8,128)(2,1)}, u32[]{:S(2)}, u32[]{:S(2)}) collective-permute-start(bf16[128,2048]{1,0:T(8,128)(2,1)} %fusion.103), channel_id=1, source_target_pairs={{0,4},{1,5},{2,6},{3,7},{4,0},{5,1},{6,2},{7,3},{8,12},{9,13},{10,... | collective-permute-start | bytes 1572872 | tf_op jit(solution)/shard_map/ppermute | solution.py:214
  320.7 4.8 %collective-permute-done.53 = bf16[64,2048]{1,0:T(8,128)(2,1)S(1)} collective-permute-done((bf16[64,2048]{1,0:T(8,128)(2,1)S(1)}, bf16[64,2048]{1,0:T(8,128)(2,1)S(1)}, u32[]{:S(2)}, u32[]{:S(2)}) %collective-permute-start.53) | collective-permute-done | bytes 262176 | tf_op jit(solution)/shard_map/ppermute | solution.py:214
  329.4 8.8 %collective-permute-done.44 = bf16[128,2048]{1,0:T(8,128)(2,1)S(1)} collective-permute-done((bf16[128,2048]{1,0:T(8,128)(2,1)S(1)}, bf16[128,2048]{1,0:T(8,128)(2,1)S(1)}, u32[]{:S(2)}, u32[]{:S(2)}) %collective-permute-start.44) | collective-permute-done | bytes 524320 | tf_op jit(solution)/shard_map/ppermute | solution.py:214
  341.2 6.5 %collective-permute-done.63 = bf16[64,2048]{1,0:T(8,128)(2,1)S(1)} collective-permute-done((bf16[64,2048]{1,0:T(8,128)(2,1)S(1)}, bf16[64,2048]{1,0:T(8,128)(2,1)S(1)}, u32[]{:S(2)}, u32[]{:S(2)}) %collective-permute-start.63) | collective-permute-done | bytes 262176 | tf_op jit(solution)/shard_map/ppermute | solution.py:214
  348.7 2.2 collective-permute-done.65
  355.4 2.8 collective-permute-start.57
  359.0 2.0 copy.88
  363.8 6.6 %collective-permute-done.57 = bf16[128,2048]{1,0:T(8,128)(2,1)} collective-permute-done((bf16[128,2048]{1,0:T(8,128)(2,1)}, bf16[128,2048]{1,0:T(8,128)(2,1)}, u32[]{:S(2)}, u32[]{:S(2)}) %collective-permute-start.57) | collective-permute-done | bytes 524320 | tf_op jit(solution)/shard_map/ppermute | solution.py:214
  370.3 3.4 fusion.92
  (257 shorter events, 95.2 us)
Async XLA Ops:
  0.6 81.5 %collective-permute-start = (bf16[128,2048]{1,0:T(8,128)(2,1)}, bf16[128,2048]{1,0:T(8,128)(2,1)}, u32[]{:S(2)}, u32[]{:S(2)}) collective-permute-start(bf16[128,2048]{1,0:T(8,128)(2,1)} %tokens.1), channel_id=1, source_target_pairs={{0,2},{1,3},{2,0},{3,1},{4,6},{5,7},{6,4},{7,5},{8,10},{9,11},{10,... | collective-permute-start | bytes 1572872 | tf_op jit(solution)/shard_map/ppermute | solution.py:214
  14.9 24.9 %collective-permute-start.1 = (bf16[2048,256]{1,0:T(8,128)(2,1)}, bf16[2048,256]{1,0:T(8,128)(2,1)}, u32[]{:S(2)}, u32[]{:S(2)}) collective-permute-start(bf16[2048,256]{1,0:T(8,128)(2,1)} %constant_dynamic-slice_fusion.2), channel_id=1, source_target_pairs={{0,1},{1,0},{2,3},{3,2},{4,5},{5,4},{6,7},{7,6},{8,9},{9,8},{10,11... | collective-permute-start | bytes 3145736 | tf_op jit(solution)/shard_map/ppermute | solution.py:214
  17.1 16.7 %collective-permute-start.3 = (bf16[128,256]{1,0:T(8,128)(2,1)}, bf16[128,256]{1,0:T(8,128)(2,1)}, u32[]{:S(2)}, u32[]{:S(2)}) collective-permute-start(bf16[128,256]{1,0:T(8,128)(2,1)} %get-tuple-element.83), channel_id=1, source_target_pairs={{0,2},{1,3},{2,0},{3,1},{4,6},{5,7},{6,4},{7,5},{8,10},{9,11},{10,... | collective-permute-start | bytes 196616 | tf_op jit(solution)/shard_map/ppermute | solution.py:214
  17.5 18.7 %collective-permute-start.4 = (bf16[128,256]{1,0:T(8,128)(2,1)}, bf16[128,256]{1,0:T(8,128)(2,1)}, u32[]{:S(2)}, u32[]{:S(2)}) collective-permute-start(bf16[128,256]{1,0:T(8,128)(2,1)} %get-tuple-element.82), channel_id=1, source_target_pairs={{0,4},{1,5},{2,6},{3,7},{4,0},{5,1},{6,2},{7,3},{8,12},{9,13},{10,... | collective-permute-start | bytes 196616 | tf_op jit(solution)/shard_map/ppermute | solution.py:214
  20.1 16.2 %collective-permute-start.5 = (bf16[128,256]{1,0:T(8,128)(2,1)}, bf16[128,256]{1,0:T(8,128)(2,1)}, u32[]{:S(2)}, u32[]{:S(2)}) collective-permute-start(bf16[128,256]{1,0:T(8,128)(2,1)} %get-tuple-element.81), channel_id=1, source_target_pairs={{0,6},{1,7},{2,4},{3,5},{4,2},{5,3},{6,0},{7,1},{8,14},{9,15},{10,... | collective-permute-start | bytes 196616 | tf_op jit(solution)/shard_map/ppermute | solution.py:214
  33.8 53.3 %collective-permute-start.10 = (bf16[128,2048]{1,0:T(8,128)(2,1)}, bf16[128,2048]{1,0:T(8,128)(2,1)S(1)}, u32[]{:S(2)}, u32[]{:S(2)}) collective-permute-start(bf16[128,2048]{1,0:T(8,128)(2,1)} %tokens.1), channel_id=1, source_target_pairs={{0,6},{1,7},{2,4},{3,5},{4,2},{5,3},{6,0},{7,1},{8,14},{9,15},{10,... | collective-permute-start | bytes 1572872 | tf_op jit(solution)/shard_map/ppermute | solution.py:214
  36.3 51.4 %collective-permute-start.9 = (bf16[128,2048]{1,0:T(8,128)(2,1)}, bf16[128,2048]{1,0:T(8,128)(2,1)S(1)}, u32[]{:S(2)}, u32[]{:S(2)}) collective-permute-start(bf16[128,2048]{1,0:T(8,128)(2,1)} %tokens.1), channel_id=1, source_target_pairs={{0,4},{1,5},{2,6},{3,7},{4,0},{5,1},{6,2},{7,3},{8,12},{9,13},{10,... | collective-permute-start | bytes 1572872 | tf_op jit(solution)/shard_map/ppermute | solution.py:214
  36.3 21.5 %collective-permute-start.16 = (bf16[16,128]{1,0:T(8,128)(2,1)}, bf16[16,128]{1,0:T(8,128)(2,1)S(1)}, u32[]{:S(2)}, u32[]{:S(2)}) collective-permute-start(bf16[16,128]{1,0:T(8,128)(2,1)} %pad_maximum_fusion.16), channel_id=1, source_target_pairs={{0,2},{1,3},{2,0},{3,1},{4,6},{5,7},{6,4},{7,5},{8,10},{9,11},{10,... | collective-permute-start | bytes 12296 | tf_op jit(solution)/shard_map/ppermute | solution.py:214
  39.8 40.4 %collective-permute-start.17 = (bf16[16,128]{1,0:T(8,128)(2,1)}, bf16[16,128]{1,0:T(8,128)(2,1)S(1)}, u32[]{:S(2)}, u32[]{:S(2)}) collective-permute-start(bf16[16,128]{1,0:T(8,128)(2,1)} %pad_maximum_fusion.16), channel_id=1, source_target_pairs={{0,4},{1,5},{2,6},{3,7},{4,0},{5,1},{6,2},{7,3},{8,12},{9,13},{10,... | collective-permute-start | bytes 12296 | tf_op jit(solution)/shard_map/ppermute | solution.py:214
  57.8 23.7 %collective-permute-start.18 = (bf16[16,128]{1,0:T(8,128)(2,1)}, bf16[16,128]{1,0:T(8,128)(2,1)S(1)}, u32[]{:S(2)}, u32[]{:S(2)}) collective-permute-start(bf16[16,128]{1,0:T(8,128)(2,1)} %pad_maximum_fusion.16), channel_id=1, source_target_pairs={{0,6},{1,7},{2,4},{3,5},{4,2},{5,3},{6,0},{7,1},{8,14},{9,15},{10,... | collective-permute-start | bytes 12296 | tf_op jit(solution)/shard_map/ppermute | solution.py:214
  81.5 24.8 %collective-permute-start.11 = (bf16[256,2048]{1,0:T(8,128)(2,1)S(1)}, bf16[256,2048]{1,0:T(8,128)(2,1)S(1)}, u32[]{:S(2)}, u32[]{:S(2)}) collective-permute-start(bf16[256,2048]{1,0:T(8,128)(2,1)S(1)} %constant_dynamic-slice_fusion), channel_id=1, source_target_pairs={{0,1},{1,0},{2,3},{3,2},{4,5},{5,4},{6,7},{7,6},{8,9},{9,8},{10,11... | collective-permute-start | bytes 3145736 | tf_op jit(solution)/shard_map/ppermute | solution.py:214
  82.1 26.9 %collective-permute-start.2 = (bf16[2048,256]{1,0:T(8,128)(2,1)}, bf16[2048,256]{1,0:T(8,128)(2,1)S(1)}, u32[]{:S(2)}, u32[]{:S(2)}) collective-permute-start(bf16[2048,256]{1,0:T(8,128)(2,1)} %collective-permute-done.1), channel_id=1, source_target_pairs={{0,8},{1,9},{2,10},{3,11},{4,12},{5,13},{6,14},{7,15},{8,0},{9,1},... | collective-permute-start | bytes 3145736 | tf_op jit(solution)/shard_map/ppermute | solution.py:214
  85.5 50.6 %collective-permute-start.19 = (bf16[4,16,128]{2,1,0:T(8,128)(2,1)S(1)}, bf16[4,16,128]{2,1,0:T(8,128)(2,1)S(1)}, u32[]{:S(2)}, u32[]{:S(2)}) collective-permute-start(bf16[4,16,128]{2,1,0:T(8,128)(2,1)S(1)} %get-tuple-element.95), channel_id=1, source_target_pairs={{0,1},{1,0},{2,3},{3,2},{4,5},{5,4},{6,7},{7,6},{8,9},{9,8},{10,11... | collective-permute-start | bytes 49160 | tf_op jit(solution)/shard_map/ppermute | solution.py:214
  87.1 25.2 %collective-permute-start.6 = (bf16[4,128,256]{2,1,0:T(8,128)(2,1)S(1)}, bf16[4,128,256]{2,1,0:T(8,128)(2,1)S(1)}, u32[]{:S(2)}, u32[]{:S(2)}) collective-permute-start(bf16[4,128,256]{2,1,0:T(8,128)(2,1)S(1)} %pad_maximum_fusion.12.kv_here), channel_id=1, source_target_pairs={{0,1},{1,0},{2,3},{3,2},{4,5},{5,4},{6,7},{7,6},{8,9},{9,8},{10,11... | collective-permute-start | bytes 786440 | tf_op jit(solution)/shard_map/ppermute | solution.py:214
  87.6 30.3 %collective-permute-start.8 = (bf16[4,128,256]{2,1,0:T(8,128)(2,1)S(1)}, bf16[4,128,256]{2,1,0:T(8,128)(2,1)S(1)}, u32[]{:S(2)}, u32[]{:S(2)}) collective-permute-start(bf16[4,128,256]{2,1,0:T(8,128)(2,1)S(1)} %collective-permute-done.7.kv_before), channel_id=1, source_target_pairs={{0,1},{1,0},{2,3},{3,2},{4,5},{5,4},{6,7},{7,6},{8,9},{9,8},{10,11... | collective-permute-start | bytes 786440 | tf_op jit(solution)/shard_map/ppermute | solution.py:214
  106.3 22.5 %collective-permute-start.12 = (bf16[256,2048]{1,0:T(8,128)(2,1)S(1)}, bf16[256,2048]{1,0:T(8,128)(2,1)S(1)}, u32[]{:S(2)}, u32[]{:S(2)}) collective-permute-start(bf16[256,2048]{1,0:T(8,128)(2,1)S(1)} %collective-permute-done.11), channel_id=1, source_target_pairs={{0,8},{1,9},{2,10},{3,11},{4,12},{5,13},{6,14},{7,15},{8,0},{9,1},... | collective-permute-start | bytes 3145736 | tf_op jit(solution)/shard_map/ppermute | solution.py:214
  130.3 47.8 %collective-permute-start.15 = (bf16[128,2048]{1,0:T(8,128)(2,1)S(1)}, bf16[128,2048]{1,0:T(8,128)(2,1)S(1)}, u32[]{:S(2)}, u32[]{:S(2)}) collective-permute-start(bf16[128,2048]{1,0:T(8,128)(2,1)S(1)} %get-tuple-element.79), channel_id=1, source_target_pairs={{0,6},{1,7},{2,4},{3,5},{4,2},{5,3},{6,0},{7,1},{8,14},{9,15},{10,... | collective-permute-start | bytes 1572872 | tf_op jit(solution)/shard_map/ppermute | solution.py:214
  134.3 26.6 %collective-permute-start.13 = (bf16[128,2048]{1,0:T(8,128)(2,1)S(1)}, bf16[128,2048]{1,0:T(8,128)(2,1)S(1)}, u32[]{:S(2)}, u32[]{:S(2)}) collective-permute-start(bf16[128,2048]{1,0:T(8,128)(2,1)S(1)} %slice.478), channel_id=1, source_target_pairs={{0,2},{1,3},{2,0},{3,1},{4,6},{5,7},{6,4},{7,5},{8,10},{9,11},{10,... | collective-permute-start | bytes 1572872 | tf_op jit(solution)/shard_map/ppermute | solution.py:214
  134.4 43.7 %collective-permute-start.14 = (bf16[128,2048]{1,0:T(8,128)(2,1)S(1)}, bf16[128,2048]{1,0:T(8,128)(2,1)S(1)}, u32[]{:S(2)}, u32[]{:S(2)}) collective-permute-start(bf16[128,2048]{1,0:T(8,128)(2,1)S(1)} %get-tuple-element.78), channel_id=1, source_target_pairs={{0,4},{1,5},{2,6},{3,7},{4,0},{5,1},{6,2},{7,3},{8,12},{9,13},{10,... | collective-permute-start | bytes 1572872 | tf_op jit(solution)/shard_map/ppermute | solution.py:214
  179.6 14.0 %collective-permute-start.23 = (bf16[128,2048]{1,0:T(8,128)(2,1)S(1)}, bf16[128,2048]{1,0:T(8,128)(2,1)S(1)}, u32[]{:S(2)}, u32[]{:S(2)}) collective-permute-start(bf16[128,2048]{1,0:T(8,128)(2,1)S(1)} %fusion.88), channel_id=1, source_target_pairs={{0,1},{1,0},{2,3},{3,2},{4,5},{5,4},{6,7},{7,6},{8,9},{9,8},{10,11... | collective-permute-start | bytes 1572872 | tf_op jit(solution)/shard_map/ppermute | solution.py:214
  179.7 14.0 %collective-permute-start.58 = (bf16[128,2048]{1,0:T(8,128)(2,1)S(1)}, bf16[128,2048]{1,0:T(8,128)(2,1)S(1)}, u32[]{:S(2)}, u32[]{:S(2)}) collective-permute-start(bf16[128,2048]{1,0:T(8,128)(2,1)S(1)} %fusion.88), channel_id=1, source_target_pairs={{0,16},{1,17},{2,18},{3,19},{4,20},{5,21},{6,22},{7,23},{8,24},{9,... | collective-permute-start | bytes 1572872 | tf_op jit(solution)/shard_map/ppermute | solution.py:214
  180.1 15.6 %collective-permute-start.21 = (bf16[128,2048]{1,0:T(8,128)(2,1)S(1)}, bf16[128,2048]{1,0:T(8,128)(2,1)S(1)}, u32[]{:S(2)}, u32[]{:S(2)}) collective-permute-start(bf16[128,2048]{1,0:T(8,128)(2,1)S(1)} %fusion.88), channel_id=1, source_target_pairs={{0,2},{1,3},{2,0},{3,1},{4,6},{5,7},{6,4},{7,5},{8,10},{9,11},{10,... | collective-permute-start | bytes 1572872 | tf_op jit(solution)/shard_map/ppermute | solution.py:214
  195.6 16.9 %collective-permute-start.24 = (bf16[128,2048]{1,0:T(8,128)(2,1)S(1)}, bf16[128,2048]{1,0:T(8,128)(2,1)S(1)}, u32[]{:S(2)}, u32[]{:S(2)}) collective-permute-start(bf16[128,2048]{1,0:T(8,128)(2,1)S(1)} %collective-permute-done.21), channel_id=1, source_target_pairs={{0,1},{1,0},{2,3},{3,2},{4,5},{5,4},{6,7},{7,6},{8,9},{9,8},{10,11... | collective-permute-start | bytes 1572872 | tf_op jit(solution)/shard_map/ppermute | solution.py:214
  196.1 18.3 %collective-permute-start.48 = (bf16[128,2048]{1,0:T(8,128)(2,1)S(1)}, bf16[128,2048]{1,0:T(8,128)(2,1)S(1)}, u32[]{:S(2)}, u32[]{:S(2)}) collective-permute-start(bf16[128,2048]{1,0:T(8,128)(2,1)S(1)} %collective-permute-done.21), channel_id=1, source_target_pairs={{0,16},{1,17},{2,18},{3,19},{4,20},{5,21},{6,22},{7,23},{8,24},{9,... | collective-permute-start | bytes 1572872 | tf_op jit(solution)/shard_map/ppermute | solution.py:214
  198.1 23.5 %collective-permute-start.22 = (bf16[128,2048]{1,0:T(8,128)(2,1)S(1)}, bf16[128,2048]{1,0:T(8,128)(2,1)S(1)}, u32[]{:S(2)}, u32[]{:S(2)}) collective-permute-start(bf16[128,2048]{1,0:T(8,128)(2,1)S(1)} %fusion.88), channel_id=1, source_target_pairs={{0,4},{1,5},{2,6},{3,7},{4,0},{5,1},{6,2},{7,3},{8,12},{9,13},{10,... | collective-permute-start | bytes 1572872 | tf_op jit(solution)/shard_map/ppermute | solution.py:214
  215.2 26.3 %collective-permute-start.61 = (bf16[192,2048]{1,0:T(8,128)(2,1)S(1)}, bf16[192,2048]{1,0:T(8,128)(2,1)S(1)}, u32[]{:S(2)}, u32[]{:S(2)}) collective-permute-start(bf16[192,2048]{1,0:T(8,128)(2,1)S(1)} %bitcast.259), channel_id=1, source_target_pairs={{0,8},{1,9},{2,10},{3,11},{4,12},{5,13},{6,14},{7,15},{8,0},{9,1},... | collective-permute-start | bytes 2359304 | tf_op jit(solution)/shard_map/ppermute | solution.py:214
  221.6 13.8 %collective-permute-start.25 = (bf16[128,2048]{1,0:T(8,128)(2,1)S(1)}, bf16[128,2048]{1,0:T(8,128)(2,1)S(1)}, u32[]{:S(2)}, u32[]{:S(2)}) collective-permute-start(bf16[128,2048]{1,0:T(8,128)(2,1)S(1)} %collective-permute-done.22), channel_id=1, source_target_pairs={{0,1},{1,0},{2,3},{3,2},{4,5},{5,4},{6,7},{7,6},{8,9},{9,8},{10,11... | collective-permute-start | bytes 1572872 | tf_op jit(solution)/shard_map/ppermute | solution.py:214
  222.2 18.6 %collective-permute-start.26 = (bf16[128,2048]{1,0:T(8,128)(2,1)S(1)}, bf16[128,2048]{1,0:T(8,128)(2,1)S(1)}, u32[]{:S(2)}, u32[]{:S(2)}) collective-permute-start(bf16[128,2048]{1,0:T(8,128)(2,1)S(1)} %collective-permute-done.22), channel_id=1, source_target_pairs={{0,16},{1,17},{2,18},{3,19},{4,20},{5,21},{6,22},{7,23},{8,24},{9,... | collective-permute-start | bytes 1572872 | tf_op jit(solution)/shard_map/ppermute | solution.py:214
  222.8 15.2 %collective-permute-start.36 = (bf16[128,2048]{1,0:T(8,128)(2,1)S(1)}, bf16[128,2048]{1,0:T(8,128)(2,1)S(1)}, u32[]{:S(2)}, u32[]{:S(2)}) collective-permute-start(bf16[128,2048]{1,0:T(8,128)(2,1)S(1)} %fusion.88), channel_id=1, source_target_pairs={{0,6},{1,7},{2,4},{3,5},{4,2},{5,3},{6,0},{7,1},{8,14},{9,15},{10,... | collective-permute-start | bytes 1572872 | tf_op jit(solution)/shard_map/ppermute | solution.py:214
  225.4 35.3 %collective-permute-start.51 = (bf16[192,2048]{1,0:T(8,128)(2,1)S(1)}, bf16[192,2048]{1,0:T(8,128)(2,1)S(1)}, u32[]{:S(2)}, u32[]{:S(2)}) collective-permute-start(bf16[192,2048]{1,0:T(8,128)(2,1)S(1)} %bitcast.255), channel_id=1, source_target_pairs={{0,8},{1,9},{2,10},{3,11},{4,12},{5,13},{6,14},{7,15},{8,0},{9,1},... | collective-permute-start | bytes 2359304 | tf_op jit(solution)/shard_map/ppermute | solution.py:214
  238.0 20.3 %collective-permute-start.37 = (bf16[128,2048]{1,0:T(8,128)(2,1)S(1)}, bf16[128,2048]{1,0:T(8,128)(2,1)S(1)}, u32[]{:S(2)}, u32[]{:S(2)}) collective-permute-start(bf16[128,2048]{1,0:T(8,128)(2,1)S(1)} %collective-permute-done.36), channel_id=1, source_target_pairs={{0,1},{1,0},{2,3},{3,2},{4,5},{5,4},{6,7},{7,6},{8,9},{9,8},{10,11... | collective-permute-start | bytes 1572872 | tf_op jit(solution)/shard_map/ppermute | solution.py:214
  239.4 20.5 %collective-permute-start.38 = (bf16[128,2048]{1,0:T(8,128)(2,1)S(1)}, bf16[128,2048]{1,0:T(8,128)(2,1)S(1)}, u32[]{:S(2)}, u32[]{:S(2)}) collective-permute-start(bf16[128,2048]{1,0:T(8,128)(2,1)S(1)} %collective-permute-done.36), channel_id=1, source_target_pairs={{0,16},{1,17},{2,18},{3,19},{4,20},{5,21},{6,22},{7,23},{8,24},{9,... | collective-permute-start | bytes 1572872 | tf_op jit(solution)/shard_map/ppermute | solution.py:214
  240.8 16.2 %collective-permute-start.27 = (bf16[64,2048]{1,0:T(8,128)(2,1)S(1)}, bf16[64,2048]{1,0:T(8,128)(2,1)S(1)}, u32[]{:S(2)}, u32[]{:S(2)}) collective-permute-start(bf16[64,2048]{1,0:T(8,128)(2,1)S(1)} %slice.483), channel_id=1, source_target_pairs={{0,16},{1,17},{2,18},{3,19},{4,20},{5,21},{6,22},{7,23},{8,24},{9,... | collective-permute-start | bytes 786440 | tf_op jit(solution)/shard_map/ppermute | solution.py:214
  241.5 15.5 %collective-permute-start.28 = (bf16[64,2048]{1,0:T(8,128)(2,1)S(1)}, bf16[64,2048]{1,0:T(8,128)(2,1)S(1)}, u32[]{:S(2)}, u32[]{:S(2)}) collective-permute-start(bf16[64,2048]{1,0:T(8,128)(2,1)S(1)} %slice.484), channel_id=1, source_target_pairs={{0,1},{1,0},{2,3},{3,2},{4,5},{5,4},{6,7},{7,6},{8,9},{9,8},{10,11... | collective-permute-start | bytes 786440 | tf_op jit(solution)/shard_map/ppermute | solution.py:214
  257.1 11.7 %collective-permute-start.62 = (bf16[192,2048]{1,0:T(8,128)(2,1)S(1)}, bf16[192,2048]{1,0:T(8,128)(2,1)S(1)}, u32[]{:S(2)}, u32[]{:S(2)}) collective-permute-start(bf16[192,2048]{1,0:T(8,128)(2,1)S(1)} %get-tuple-element.75), channel_id=1, source_target_pairs={{0,8},{1,9},{2,10},{3,11},{4,12},{5,13},{6,14},{7,15},{8,0},{9,1},... | collective-permute-start | bytes 2359304 | tf_op jit(solution)/shard_map/ppermute | solution.py:214
  257.8 12.3 %collective-permute-start.29 = (bf16[192,2048]{1,0:T(8,128)(2,1)S(1)}, bf16[192,2048]{1,0:T(8,128)(2,1)S(1)}, u32[]{:S(2)}, u32[]{:S(2)}) collective-permute-start(bf16[192,2048]{1,0:T(8,128)(2,1)S(1)} %bitcast.258), channel_id=1, source_target_pairs={{0,8},{1,9},{2,10},{3,11},{4,12},{5,13},{6,14},{7,15},{8,0},{9,1},... | collective-permute-start | bytes 2359304 | tf_op jit(solution)/shard_map/ppermute | solution.py:214
  290.5 14.9 %collective-permute-start.32 = (bf16[128,2048]{1,0:T(8,128)(2,1)S(1)}, bf16[128,2048]{1,0:T(8,128)(2,1)S(1)}, u32[]{:S(2)}, u32[]{:S(2)}) collective-permute-start(bf16[128,2048]{1,0:T(8,128)(2,1)S(1)} %pad_maximum_fusion.4), channel_id=1, source_target_pairs={{0,1},{1,0},{2,3},{3,2},{4,5},{5,4},{6,7},{7,6},{8,9},{9,8},{10,11... | collective-permute-start | bytes 1572872 | tf_op jit(solution)/shard_map/ppermute | solution.py:214
  291.3 14.9 %collective-permute-start.34 = (bf16[128,2048]{1,0:T(8,128)(2,1)S(1)}, bf16[128,2048]{1,0:T(8,128)(2,1)S(1)}, u32[]{:S(2)}, u32[]{:S(2)}) collective-permute-start(bf16[128,2048]{1,0:T(8,128)(2,1)S(1)} %pad_maximum_fusion.5), channel_id=1, source_target_pairs={{0,16},{1,17},{2,18},{3,19},{4,20},{5,21},{6,22},{7,23},{8,24},{9,... | collective-permute-start | bytes 1572872 | tf_op jit(solution)/shard_map/ppermute | solution.py:214
  294.5 24.6 %collective-permute-start.43 = (bf16[64,2048]{1,0:T(8,128)(2,1)S(1)}, bf16[64,2048]{1,0:T(8,128)(2,1)S(1)}, u32[]{:S(2)}, u32[]{:S(2)}) collective-permute-start(bf16[64,2048]{1,0:T(8,128)(2,1)S(1)} %get-tuple-element.46), channel_id=1, source_target_pairs={{0,16},{1,17},{2,18},{3,19},{4,20},{5,21},{6,22},{7,23},{8,24},{9,... | collective-permute-start | bytes 786440 | tf_op jit(solution)/shard_map/ppermute | solution.py:214
  295.1 21.0 %collective-permute-start.45 = (bf16[64,2048]{1,0:T(8,128)(2,1)S(1)}, bf16[64,2048]{1,0:T(8,128)(2,1)S(1)}, u32[]{:S(2)}, u32[]{:S(2)}) collective-permute-start(bf16[64,2048]{1,0:T(8,128)(2,1)S(1)} %get-tuple-element.47), channel_id=1, source_target_pairs={{0,1},{1,0},{2,3},{3,2},{4,5},{5,4},{6,7},{7,6},{8,9},{9,8},{10,11... | collective-permute-start | bytes 786440 | tf_op jit(solution)/shard_map/ppermute | solution.py:214
  307.2 56.0 %collective-permute-start.35 = (bf16[128,2048]{1,0:T(8,128)(2,1)}, bf16[128,2048]{1,0:T(8,128)(2,1)}, u32[]{:S(2)}, u32[]{:S(2)}) collective-permute-start(bf16[128,2048]{1,0:T(8,128)(2,1)} %fusion.103), channel_id=1, source_target_pairs={{0,4},{1,5},{2,6},{3,7},{4,0},{5,1},{6,2},{7,3},{8,12},{9,13},{10,... | collective-permute-start | bytes 1572872 | tf_op jit(solution)/shard_map/ppermute | solution.py:214
  319.3 18.9 %collective-permute-start.44 = (bf16[128,2048]{1,0:T(8,128)(2,1)S(1)}, bf16[128,2048]{1,0:T(8,128)(2,1)S(1)}, u32[]{:S(2)}, u32[]{:S(2)}) collective-permute-start(bf16[128,2048]{1,0:T(8,128)(2,1)S(1)} %pad_maximum_fusion.6), channel_id=1, source_target_pairs={{0,1},{1,0},{2,3},{3,2},{4,5},{5,4},{6,7},{7,6},{8,9},{9,8},{10,11... | collective-permute-start | bytes 1572872 | tf_op jit(solution)/shard_map/ppermute | solution.py:214
  320.1 18.8 %collective-permute-start.46 = (bf16[128,2048]{1,0:T(8,128)(2,1)S(1)}, bf16[128,2048]{1,0:T(8,128)(2,1)S(1)}, u32[]{:S(2)}, u32[]{:S(2)}) collective-permute-start(bf16[128,2048]{1,0:T(8,128)(2,1)S(1)} %pad_maximum_fusion.7), channel_id=1, source_target_pairs={{0,16},{1,17},{2,18},{3,19},{4,20},{5,21},{6,22},{7,23},{8,24},{9,... | collective-permute-start | bytes 1572872 | tf_op jit(solution)/shard_map/ppermute | solution.py:214
  327.2 27.1 %collective-permute-start.54 = (bf16[128,2048]{1,0:T(8,128)(2,1)S(1)}, bf16[128,2048]{1,0:T(8,128)(2,1)S(1)}, u32[]{:S(2)}, u32[]{:S(2)}) collective-permute-start(bf16[128,2048]{1,0:T(8,128)(2,1)S(1)} %pad_maximum_fusion.8), channel_id=1, source_target_pairs={{0,1},{1,0},{2,3},{3,2},{4,5},{5,4},{6,7},{7,6},{8,9},{9,8},{10,11... | collective-permute-start | bytes 1572872 | tf_op jit(solution)/shard_map/ppermute | solution.py:214
  328.6 25.7 %collective-permute-start.56 = (bf16[128,2048]{1,0:T(8,128)(2,1)S(1)}, bf16[128,2048]{1,0:T(8,128)(2,1)S(1)}, u32[]{:S(2)}, u32[]{:S(2)}) collective-permute-start(bf16[128,2048]{1,0:T(8,128)(2,1)S(1)} %pad_maximum_fusion.9), channel_id=1, source_target_pairs={{0,16},{1,17},{2,18},{3,19},{4,20},{5,21},{6,22},{7,23},{8,24},{9,... | collective-permute-start | bytes 1572872 | tf_op jit(solution)/shard_map/ppermute | solution.py:214
  338.8 12.0 %collective-permute-start.65 = (bf16[64,2048]{1,0:T(8,128)(2,1)S(1)}, bf16[64,2048]{1,0:T(8,128)(2,1)S(1)}, u32[]{:S(2)}, u32[]{:S(2)}) collective-permute-start(bf16[64,2048]{1,0:T(8,128)(2,1)S(1)} %get-tuple-element.59), channel_id=1, source_target_pairs={{0,1},{1,0},{2,3},{3,2},{4,5},{5,4},{6,7},{7,6},{8,9},{9,8},{10,11... | collective-permute-start | bytes 786440 | tf_op jit(solution)/shard_map/ppermute | solution.py:214
  347.7 15.5 %collective-permute-start.47 = (bf16[128,2048]{1,0:T(8,128)(2,1)}, bf16[128,2048]{1,0:T(8,128)(2,1)}, u32[]{:S(2)}, u32[]{:S(2)}) collective-permute-start(bf16[128,2048]{1,0:T(8,128)(2,1)} %fusion.101), channel_id=1, source_target_pairs={{0,6},{1,7},{2,4},{3,5},{4,2},{5,3},{6,0},{7,1},{8,14},{9,15},{10,... | collective-permute-start | bytes 1572872 | tf_op jit(solution)/shard_map/ppermute | solution.py:214
  355.4 14.9 %collective-permute-start.57 = (bf16[128,2048]{1,0:T(8,128)(2,1)}, bf16[128,2048]{1,0:T(8,128)(2,1)}, u32[]{:S(2)}, u32[]{:S(2)}) collective-permute-start(bf16[128,2048]{1,0:T(8,128)(2,1)} %fusion.99), channel_id=1, source_target_pairs={{0,2},{1,3},{2,0},{3,1},{4,6},{5,7},{6,4},{7,5},{8,10},{9,11},{10,... | collective-permute-start | bytes 1572872 | tf_op jit(solution)/shard_map/ppermute | solution.py:214
  (43 other events, 818.7 us)

commit v3 on v2

--- a/solution.py
+++ b/solution.py
@@ -230,6 +230,10 @@
     return moved(block, lambda y, core, z, x: (y, core, z ^ k, x))
 
 
+def sum_of(a, b):
+    return (a.astype(jnp.float32) + b.astype(jnp.float32)).astype(jnp.bfloat16)
+
+
 def after(value, earlier):
     return lax.optimization_barrier((value, earlier))[0]
 
@@ -251,8 +255,8 @@
                 at = jnp.bitwise_xor(z, k) * 2
                 for source, shift in ((near, x), (far, 1 - x)):
                     row = pl.multiple_of((first + at + shift) * rows, rows)
-                    keys[pl.ds(row, rows), :] = source[k, :, :head]
-                    values[:, pl.ds(row, rows)] = source[k, :, head:].astype(jnp.float32).T.astype(jnp.bfloat16)
+                    keys[pl.ds(row, rows), :] = source[k, :rows, :head]
+                    values[:, pl.ds(row, rows)] = source[k, :rows, head:].astype(jnp.float32).T.astype(jnp.bfloat16)
 
     turned = []
     for h in range(heads):
@@ -364,15 +368,15 @@
             whole(rows, width),
             whole(1, width),
             whole(head, 1),
-            whole(1, head // 2, rows),
-            whole(1, head // 2, rows),
+            pl.BlockSpec((1, head // 2, rows), lambda h: (0, 0, 0)),
+            pl.BlockSpec((1, head // 2, rows), lambda h: (0, 0, 0)),
             pl.BlockSpec((width, head), lambda h: (0, h)),
             pl.BlockSpec((width, head), lambda h: (0, heads + h)),
         ],
         out_specs=pl.BlockSpec((1, rows, 2 * head), lambda h: (h, 0, 0)),
         out_shape=jax.ShapeDtypeStruct((heads, rows, 2 * head), jnp.bfloat16),
         scratch_shapes=[pltpu.VMEM((rows, width), jnp.bfloat16)],
-        compiler_params=pltpu.CompilerParams(vmem_limit_bytes=32 * 2**20),
+        compiler_params=pltpu.CompilerParams(vmem_limit_bytes=60 * 2**20),
         cost_estimate=pl.CostEstimate(
             flops=2 * rows * width * w_keyval.shape[1], bytes_accessed=5 * 2**20, transcendentals=0
         ),
@@ -406,39 +410,47 @@
     group_start = rep * group_rows
     slots = range(4)
 
-    raw = [tokens] + [other_z(tokens, k) for k in (1, 2, 3)]
-
-    slot_z = jnp.stack([z ^ k for k in slots])
-    slot_position = group_start + ((slot_z * 2 + x) * rows)[:, None] + jnp.arange(rows, dtype=jnp.int32)
+    slot_start = [group_start + ((z ^ k) * 2 + x) * rows for k in slots]
+    slot_position = jnp.stack([at + jnp.arange(rows, dtype=jnp.int32) for at in slot_start])
     frequency = jnp.exp(
         jnp.arange(head // 2, dtype=jnp.float32) * (-2.0 * math.log(1000000.0) / head)
     )
     angles = frequency[None, :, None] * slot_position.astype(jnp.float32)[:, None, :]
     cosine, sine = jnp.cos(angles), jnp.sin(angles)
 
-    by_head = keyval_by_head(tokens, attn_gain, key_norm_gain, cosine[:1], sine[:1], w_keyval)
-    pick = lambda h: lax.dynamic_index_in_dim(by_head, h, 0, keepdims=False)
-    kv_here = jnp.stack([pick(z)] + [other_z(pick(z ^ k), k) for k in (1, 2, 3)])
-    kv_before = passed_along(kv_here, "rep", 1)
-    kv_side = other_x(kv_here)
-    kv_before_side = other_x(kv_before)
-
-    half_heads = w_query.shape[1] // 2
-    query_half = other_x(
-        lax.dynamic_slice_in_dim(after(w_query, by_head), core * half_heads, half_heads, 1)
-    )
-    query_rest = other_core(query_half)
-    out_half = other_x(
-        lax.dynamic_slice_in_dim(after(w_out, query_half), core * half_heads, half_heads, 0)
-    )
-    out_rest = other_core(out_half)
+    by_head = keyval_by_head(tokens, attn_gain, key_norm_gain, cosine, sine, w_keyval)
+    part = w_query.shape[1] // 4
+    quarter = y * 2 + core
+    query_x = other_x(lax.dynamic_slice_in_dim(w_query, quarter * part, part, 1))
+    by_head, query_x = lax.optimization_barrier((by_head, query_x))
+    query_y = other_y(query_x)
 
     top = expert_ids.shape[1]
     routes = jnp.concatenate([expert_ids.T.astype(jnp.bfloat16), gates.T], axis=0)
-    routes = after(routes, by_head)
-    routes = jnp.stack([routes] + [other_z(routes, k) for k in (1, 2, 3)])
-    routes = jnp.stack([routes, other_x(routes)], axis=1)
-    routes = jnp.concatenate([routes, other_y(routes)], axis=1).reshape(16, 2, top, rows)
+    routes = jnp.pad(routes, ((0, 0), (0, 2 * head - rows)))
+    pick = lambda h: jnp.concatenate(
+        [lax.dynamic_index_in_dim(by_head, h, 0, keepdims=False), routes], axis=0
+    )
+    kv_here = jnp.stack([pick(z)] + [other_z(pick(z ^ k), k) for k in (1, 2, 3)])
+    far = other_z(tokens, 2)
+    kv_here, query_y, far, w_query, w_out = lax.optimization_barrier(
+        (kv_here, query_y, far, w_query, w_out)
+    )
+    kv_before, kv_side = passed_along(kv_here, "rep", 1), other_x(kv_here)
+    farther = other_z(far, 1)
+    query_two = jnp.concatenate([query_x, query_y], axis=1)
+    query_far = other_core(query_two)
+    out_x = other_x(lax.dynamic_slice_in_dim(w_out, quarter * part, part, 0))
+    kv_side, query_far = lax.optimization_barrier((kv_side, query_far))
+    kv_before_side = passed_along(kv_side, "rep", 1)
+    w_query_wide = jnp.concatenate([w_query, query_two, query_far], axis=1)
+    kv_before, kv_before_side, out_x, farther = lax.optimization_barrier(
+        (kv_before, kv_before_side, out_x, farther)
+    )
+    near = other_z(after(tokens, farther), 1)
+    out_two = jnp.concatenate([out_x, other_y(out_x)], axis=0)
+    w_out_wide = jnp.concatenate([w_out, out_two, other_core(out_two)], axis=0)
+    raw = [tokens, near, far, farther]
 
     pages = page_table.shape[0]
     stored = jnp.transpose(by_head.reshape(kv_heads, rows, 2, head), (1, 2, 0, 3))
@@ -446,18 +458,20 @@
     cache = jnp.dot(placing, stored.reshape(pages, -1), preferred_element_type=jnp.float32)
     cache = cache.astype(jnp.bfloat16).reshape(pages, rows // pages, 2 * kv_width)
 
-    slot_seg = jnp.take(seg_ids, slot_position.reshape(-1), axis=0)
+    slot_seg = jnp.concatenate(
+        [lax.dynamic_slice_in_dim(seg_ids, at, rows, 0) for at in slot_start]
+    )
     starts = jnp.sum((seg_ids[None, :] < slot_seg[:, None]).astype(jnp.int32), axis=1)
     starts = (starts - (group_start - group_rows)).reshape(4, 1, rows)
     low = starts[:, 0, 0] // KEY_BLOCK
-    w_query_wide = jnp.concatenate([w_query, query_half, query_rest], axis=1)
-    w_out_wide = jnp.concatenate([w_out, out_half, out_rest], axis=0)
-
-    def attended(first):
+
+    def projection(first):
+        lines = jnp.concatenate(raw[first : first + 2], axis=0).astype(jnp.float32)
+        lines = root_mean_norm(lines, attn_gain).astype(jnp.bfloat16)
+        return jnp.dot(lines, w_query_wide, preferred_element_type=jnp.float32)
+
+    def attended(first, projected):
         two = slice(first, first + 2)
-        lines = jnp.concatenate(raw[two], axis=0).astype(jnp.float32)
-        lines = root_mean_norm(lines, attn_gain).astype(jnp.bfloat16)
-        projected = jnp.dot(lines, w_query_wide, preferred_element_type=jnp.float32)
         return attend_slots(
             jnp.stack([z, x, jnp.int32(first)]),
             low[two],
@@ -473,33 +487,41 @@
         term = jnp.dot(part, w_out_wide, preferred_element_type=jnp.float32).astype(jnp.bfloat16)
         return term[:rows], term[rows:]
 
-    early = attended(0)
-    term_2, term_3 = term_of(attended(2))
-    far = [other_z(term_2, 2), other_z(term_3, 3)]
-    term_0, term_1 = term_of(after(early, term_3))
-    mixed_sum = term_0.astype(jnp.float32)
-    for part in [other_z(term_1, 1)] + far:
-        mixed_sum = mixed_sum + part.astype(jnp.float32)
+    term_2, term_3 = term_of(attended(2, projection(2)))
+    far_3 = other_z(term_3, 1)
+    far = other_z(sum_of(term_2, far_3), 2)
+    term_0, term_1 = term_of(attended(0, after(projection(0), term_3)))
+    near = other_z(term_1, 1)
+    mixed_sum = term_0.astype(jnp.float32) + near.astype(jnp.float32) + far.astype(jnp.float32)
     residual = (tokens.astype(jnp.float32) + mixed_sum).astype(jnp.bfloat16)
     normed_moe = root_mean_norm(residual.astype(jnp.float32), moe_gain).astype(jnp.bfloat16)
 
+    turned = (False, True, False, True)
+    routes = kv_here[:, rows:, :rows]
+    over_x, over_y = kv_side[:, rows:, :rows], other_y(routes)
+    routes = jnp.stack(
+        [jnp.stack([routes[k], (over_y if turned[k] else over_x)[k]]) for k in slots]
+    ).reshape(4, 2, 2, top, rows)
     capacity = max(2, 3 * rows * top // (2 * 32))
-    experts = jnp.stack([rep * 8 + tp, (rep ^ 1) * 8 + tp])
-    hits = routes[:, 0][:, None] == experts.astype(jnp.bfloat16)[None, :, None, None]
-    weight = jnp.sum(jnp.where(hits, routes[:, 1][:, None].astype(jnp.float32), 0.0), axis=2)
-    hit = jnp.any(hits, axis=2)
+    mine = [rep * 8 + tp, (rep ^ 1) * 8 + tp]
+    experts = jnp.stack(
+        [jnp.stack(mine + [e ^ 1 if turned[k] else e ^ 16 for e in mine]) for k in slots]
+    ).astype(jnp.bfloat16)
+    hits = routes[:, :, 0][:, :, None] == experts[:, None, :, None, None]
+    weight = jnp.sum(jnp.where(hits, routes[:, :, 1][:, :, None].astype(jnp.float32), 0.0), axis=3)
+    hit = jnp.any(hits, axis=3)
     earlier = jnp.arange(rows)[:, None] < jnp.arange(rows)[None, :]
     place = jnp.dot(
         hit.reshape(-1, rows).astype(jnp.bfloat16),
         earlier.astype(jnp.bfloat16),
         preferred_element_type=jnp.float32,
-    ).reshape(16, 2, rows)
+    ).reshape(4, 2, 4, rows)
     chosen = (
-        place[:, :, None, :].astype(jnp.int32) == jnp.arange(capacity, dtype=jnp.int32)[None, None, :, None]
-    ) & hit[:, :, None, :]
-    weighted = jnp.where(chosen, weight[:, :, None, :], 0.0).astype(jnp.bfloat16)
-    weighted = weighted.reshape(4, 4, 2, capacity, rows)
-    chosen = chosen.astype(jnp.bfloat16).reshape(4, 4, 2 * capacity, rows)
+        place[..., None, :].astype(jnp.int32) == jnp.arange(capacity, dtype=jnp.int32)[:, None]
+    ) & hit[..., None, :]
+    weighted = jnp.where(chosen, weight[..., None, :], 0.0).astype(jnp.bfloat16)
+    weighted = weighted.reshape(4, 2, 4 * capacity, rows)
+    chosen = chosen.astype(jnp.bfloat16).reshape(4, 2, 4 * capacity, rows)
 
     def experts_of(slot_rows_in):
         gate_up = jnp.dot(slot_rows_in, w_gate_up[0], preferred_element_type=jnp.float32)
@@ -507,48 +529,70 @@
         act = (jax.nn.silu(gate_up[:, :hidden]) * gate_up[:, hidden:]).astype(jnp.bfloat16)
         return jnp.dot(act, w_down[0], preferred_element_type=jnp.float32).astype(jnp.bfloat16)
 
-    half = rows // 2
-    arrived = [normed_moe, other_z(normed_moe, 1)]
-    arrived.append(other_z(after(normed_moe, arrived[1]), 2))
-    arrived.append(other_z(after(normed_moe, arrived[2]), 3))
-    partial = []
-    turn = normed_moe
-    for k in slots:
-        block, turn = lax.optimization_barrier((arrived[k], turn))
-        side_x, side_y = other_x(block), other_y(block)
-        turn = side_x
-        corner = jnp.concatenate([other_y(side_x[:half]), other_x(side_y[half:])], axis=0)
-        blocks = jnp.stack([block, side_x, side_y, corner])
+    pair = 2 * capacity
+    together = lambda *values: lax.optimization_barrier(values)
+
+    def picks(k, block, side):
         picked = lax.dot_general(
-            chosen[k], blocks, (((2,), (1,)), ((0,), (0,))), preferred_element_type=jnp.float32
+            chosen[k], jnp.stack([block, side]), (((2,), (1,)), ((0,), (0,))), preferred_element_type=jnp.float32
         ).astype(jnp.bfloat16)
+        return picked[:, :pair], picked[:, pair:]
+
+    def routed(mine, theirs):
+        picked = jnp.concatenate([mine, theirs], axis=0)
         kept = picked[:, :capacity].reshape(-1, width)
-        traded = other_core(picked[:, capacity:].reshape(-1, width))
-        result = experts_of(jnp.concatenate([kept, traded], axis=0))
-        back = other_core(result[4 * capacity :])
-        both = jnp.stack([result[: 4 * capacity], back]).reshape(2, 4, capacity, width)
-        partial.append(
-            lax.dot_general(
-                weighted[k],
-                jnp.transpose(both, (1, 0, 2, 3)),
-                (((1, 2), (1, 2)), ((0,), (0,))),
-                preferred_element_type=jnp.float32,
-            ).astype(jnp.bfloat16)
-        )
+        return jnp.concatenate([kept, other_core(picked[:, capacity:].reshape(-1, width))], axis=0)
+
+    near, far = other_z(normed_moe, 1), other_z(normed_moe, 2)
+    mine_0, theirs_0 = picks(0, normed_moe, other_x(normed_moe))
+    theirs_0 = other_y(theirs_0)
+    near, far, mine_0 = together(near, far, mine_0)
+    side_1, side_2, farther = other_y(near), other_x(far), other_z(far, 1)
+    side_2, farther, theirs_0 = together(side_2, farther, theirs_0)
+    mine_2, theirs_2 = picks(2, far, side_2)
+    side_3 = other_y(farther)
+    side_1, mine_2, theirs_2 = together(side_1, mine_2, theirs_2)
+    mine_1, theirs_1 = picks(1, near, side_1)
+    theirs_1 = other_x(theirs_1)
+    result_0 = experts_of(routed(mine_0, theirs_0))
+    side_3, theirs_2, result_0 = together(side_3, theirs_2, result_0)
+    mine_3, theirs_3 = picks(3, farther, side_3)
+    theirs_2, theirs_3 = other_y(theirs_2), other_x(theirs_3)
+    result_1 = experts_of(routed(mine_1, after(theirs_1, side_3)))
+    theirs_2, result_1 = together(theirs_2, result_1)
+    result_2 = experts_of(routed(mine_2, theirs_2))
+    result_3 = experts_of(after(routed(mine_3, theirs_3), result_2))
+
+    def back(result):
+        traded = other_core(result[4 * capacity :])
+        both = jnp.stack([result[: 4 * capacity], traded]).reshape(2, 4, capacity, width)
+        both = jnp.transpose(both, (1, 0, 2, 3)).reshape(4, pair, width)
+        return both[:2], both[2:]
+
+    def summed(k, here, there):
+        total = lax.dot_general(
+            weighted[k],
+            jnp.concatenate([here, there], axis=1),
+            (((1,), (1,)), ((0,), (0,))),
+            preferred_element_type=jnp.float32,
+        ).astype(jnp.bfloat16)
+        return total[0], total[1]
+
+    (here_0, there_0), (here_1, there_1) = back(result_0), back(result_1)
+    (here_2, there_2), (here_3, there_3) = back(result_2), back(result_3)
+    there_2, there_3 = together(other_y(there_2), other_x(there_3))
+    (own_2, side_2), (own_3, side_3) = summed(2, here_2, there_2), summed(3, here_3, there_3)
+    side_2, side_3, there_0, there_1 = together(other_x(side_2), other_y(side_3), there_0, there_1)
+    far_3 = other_z(sum_of(own_3, side_3), 1)
+    there_0, there_1 = together(other_y(there_0), other_x(there_1))
+    (own_0, side_0), (own_1, side_1) = summed(0, here_0, there_0), summed(1, here_1, there_1)
+    far = own_2.astype(jnp.float32) + side_2.astype(jnp.float32) + far_3.astype(jnp.float32)
+    far = other_z(far.astype(jnp.bfloat16), 2)
+    side_0, side_1 = together(other_x(side_0), other_y(side_1))
+    near = other_z(sum_of(own_1, side_1), 1)
     combined = residual.astype(jnp.float32)
-    add = lambda a, b: (a.astype(jnp.float32) + b.astype(jnp.float32)).astype(jnp.bfloat16)
-    turn = partial[2]
-    for k in (2, 3, 1, 0):
-        partial_k, turn = lax.optimization_barrier((partial[k], turn))
-        here, to_x, to_y, to_corner = (partial_k[v] for v in range(4))
-        by_y, by_x = other_y(to_corner[:half]), other_x(to_corner[half:])
-        turn = by_x
-        from_x = other_x(jnp.concatenate([add(to_x[:half], by_y), to_x[half:]], axis=0))
-        from_y = other_y(jnp.concatenate([to_y[:half], add(to_y[half:], by_x)], axis=0))
-        total = here.astype(jnp.float32) + from_x.astype(jnp.float32) + from_y.astype(jnp.float32)
-        if k:
-            total = other_z(total.astype(jnp.bfloat16), k).astype(jnp.float32)
-        combined = combined + total
+    for value in (far, near, own_0, side_0):
+        combined = combined + value.astype(jnp.float32)
     return (combined.astype(jnp.bfloat16), cache)
 
 

time: 382 us -> 311 us (0.81); the launches traced: 374 us -> 311 us
  starting transfers between devices: 82.2 us -> 52.1 us
  waiting for transfers between devices: 202 us -> 184 us
  local copies, waits for them, and re-layouts: 28.3 us -> 16.3 us
    ppermute x66 -> x47, starting transfers between devices: 80.9 us -> 49.5 us  [moved(): return lax.ppermute(block, ('rep', 'tp'), route)]
    ppermute x66 -> x47, waiting for transfers between devices: 202 us -> 184 us  [moved(): return lax.ppermute(block, ('rep', 'tp'), route)]
    unnamed x53 -> x39, local copies, waits for them, and re-layouts: 11.8 us -> 3.27 us
  transfers between devices with their start and end apart: 67 -> 49, of which waited for: 30 -> 30; matrix products, arithmetic and copies ran while one was open for 17% -> 17% of each run, Pallas kernels for 3% -> 5%
where the time goes in v3:
time: 311 us
  waiting for transfers between devices  184 us (59%)
  starting transfers between devices  52.1 us (17%)
  matrix products  27.1 us (9%)
  local copies, waits for them, and re-layouts  16.3 us (5%)
  other arithmetic  15.3 us (5%)
  Pallas kernels  14.8 us (5%)
    ppermute x47, waiting for transfers between devices, moved(): return lax.ppermute(block, ('rep', 'tp'), route)  184 us
    ppermute x47, starting transfers between devices, moved(): return lax.ppermute(block, ('rep', 'tp'), route)  49.5 us
    dot_general x4, matrix products, experts_of(): jnp.dot(slot_rows_in, w_gate_up[0], preferred_element_type=jnp.float32)  10.5 us
    pallas_call x2, Pallas kernels, attend_slots(): pl.pallas_call(attention_kernel, grid_spec=pltpu.PrefetchScalarGridSpec(n...  9.5 us
  transfers between devices with their start and end apart: 49, of which 30 were waited for; matrix products, arithmetic and copies ran while one was open for 17% of the time, Pallas kernels for 5%

profile of v3, /device:TPU:0, one launch (start us, length us, event | category | flops | bytes accessed | tf_op | source)
XLA Modules:
  0.0 311.1 jit_solution(7660931364347957422)
XLA Ops:
  0.7 2.0 constant_dynamic-slice_fusion.1
  2.7 2.9 collective-permute-start
  5.6 2.6 collective-permute-start.5
  16.0 5.3 %keyval.1 = bf16[4,128,256]{2,1,0:T(8,128)(2,1)} custom-call(bf16[128,2048]{1,0:T(8,128)(2,1)} %tokens.1, f32[1,2048]{1,0:T(1,128)} %bitcast.225, f32[128,1]{1,0:T(8,128)} %copy.54.key_gain, f32[4,64,128]{2,1,0:T(8,128)} %get-tuple-element.161.cosine, f32[4,64,128]{2,1,0:T(8,128)} %get-tuple-element.160.sine, bf16[2048,1024]{1,0:T(8,128)(2,1)} %w_value.1, ...), custom_call_target="tpu_custom_call" | custom-call | flops 536870912 | bytes 5242880 | tf_op jit(solution)/shard_map/keyval/pallas_call | solution.py:364
  28.6 2.1 collective-permute-done.3
  30.7 7.0 %collective-permute-done.2 = bf16[144,256]{1,0:T(8,128)(2,1)S(1)} collective-permute-done((bf16[144,256]{1,0:T(8,128)(2,1)S(1)}, bf16[144,256]{1,0:T(8,128)(2,1)S(1)}, u32[]{:S(2)}, u32[]{:S(2)}) %collective-permute-start.2) | collective-permute-done | bytes 73760 | tf_op jit(solution)/shard_map/ppermute | solution.py:214
  42.7 2.4 collective-permute-start.8
  47.0 1.9 collective-permute-done.18
  51.2 8.3 %collective-permute-done.10 = bf16[128,2048]{1,0:T(8,128)(2,1)S(1)} collective-permute-done((bf16[128,2048]{1,0:T(8,128)(2,1)S(1)}, bf16[128,2048]{1,0:T(8,128)(2,1)S(1)}, u32[]{:S(2)}, u32[]{:S(2)}) %collective-permute-start.10) | collective-permute-done | bytes 524320 | tf_op jit(solution)/shard_map/ppermute | solution.py:214
  59.5 2.4 collective-permute-done.11
  64.7 9.0 %collective-permute-done.13 = bf16[128,2048]{1,0:T(8,128)(2,1)S(1)} collective-permute-done((bf16[128,2048]{1,0:T(8,128)(2,1)S(1)}, bf16[128,2048]{1,0:T(8,128)(2,1)S(1)}, u32[]{:S(2)}, u32[]{:S(2)}) %collective-permute-start.13) | collective-permute-done | bytes 524320 | tf_op jit(solution)/shard_map/ppermute | solution.py:214
  73.8 2.4 fusion.66.projected
  76.2 5.3 %attention.2 = bf16[256,1024]{1,0:T(8,128)(2,1)S(1)} custom-call(s32[3]{0:T(128)S(1)} %get-tuple-element.167.place, s32[2]{0:T(128)S(1)} %get-tuple-element.165.low, f32[256,1024]{1,0:T(8,128)S(1)} %fusion.66.projected, f32[128,1]{1,0:T(8,128)S(1)} %copy.55.gain, f32[2,64,128]{2,1,0:T(8,128)S(1)} %get-tuple-element.147.cosine, ...), custom_call_target="tpu_custom_call" | custom-call | flops 536870912 | bytes 8388608 | tf_op jit(solution)/shard_map/attention/pallas_call | solution.py:308
  85.5 4.2 %attention.3 = bf16[256,1024]{1,0:T(8,128)(2,1)S(1)} custom-call(s32[3]{0:T(128)S(1)} %get-tuple-element.166.place, s32[2]{0:T(128)S(1)} %get-tuple-element.164.low, f32[256,1024]{1,0:T(8,128)S(1)} %fusion.68.projected, f32[128,1]{1,0:T(8,128)S(1)} %copy.55.gain, f32[2,64,128]{2,1,0:T(8,128)S(1)} %get-tuple-element.146.cosine, ...), custom_call_target="tpu_custom_call" | custom-call | flops 536870912 | bytes 8388608 | tf_op jit(solution)/shard_map/attention/pallas_call | solution.py:308
  92.5 5.8 %collective-permute-done.16 = bf16[128,2048]{1,0:T(8,128)(2,1)S(1)} collective-permute-done((bf16[128,2048]{1,0:T(8,128)(2,1)S(1)}, bf16[128,2048]{1,0:T(8,128)(2,1)S(1)}, u32[]{:S(2)}, u32[]{:S(2)}) %collective-permute-start.16) | collective-permute-done | bytes 524320 | tf_op jit(solution)/shard_map/ppermute | solution.py:214
  100.0 18.1 %collective-permute-done.15 = bf16[128,2048]{1,0:T(8,128)(2,1)S(1)} collective-permute-done((bf16[128,2048]{1,0:T(8,128)(2,1)S(1)}, bf16[128,2048]{1,0:T(8,128)(2,1)S(1)}, u32[]{:S(2)}, u32[]{:S(2)}) %collective-permute-start.15) | collective-permute-done | bytes 524320 | tf_op jit(solution)/shard_map/ppermute | solution.py:214
  118.1 5.7 %collective-permute-done.17 = bf16[128,2048]{1,0:T(8,128)(2,1)S(1)} collective-permute-done((bf16[128,2048]{1,0:T(8,128)(2,1)S(1)}, bf16[128,2048]{1,0:T(8,128)(2,1)S(1)}, u32[]{:S(2)}, u32[]{:S(2)}) %collective-permute-start.17) | collective-permute-done | bytes 524320 | tf_op jit(solution)/shard_map/ppermute | solution.py:214
  125.4 3.4 %collective-permute-start.20 = (bf16[128,2048]{1,0:T(8,128)(2,1)S(1)}, bf16[128,2048]{1,0:T(8,128)(2,1)S(1)}, u32[]{:S(2)}, u32[]{:S(2)}) collective-permute-start(bf16[128,2048]{1,0:T(8,128)(2,1)S(1)} %fusion.61), channel_id=1, source_target_pairs={{0,4},{1,5},{2,6},{3,7},{4,0},{5,1},{6,2},{7,3},{8,12},{9,13},{10,... | collective-permute-start | bytes 1572872 | tf_op jit(solution)/shard_map/ppermute | solution.py:214
  129.0 7.8 %collective-permute-done.21 = bf16[128,2048]{1,0:T(8,128)(2,1)S(1)} collective-permute-done((bf16[128,2048]{1,0:T(8,128)(2,1)S(1)}, bf16[128,2048]{1,0:T(8,128)(2,1)S(1)}, u32[]{:S(2)}, u32[]{:S(2)}) %collective-permute-start.21) | collective-permute-done | bytes 524320 | tf_op jit(solution)/shard_map/ppermute | solution.py:214
  138.6 9.4 %collective-permute-done.19 = bf16[128,2048]{1,0:T(8,128)(2,1)S(1)} collective-permute-done((bf16[128,2048]{1,0:T(8,128)(2,1)S(1)}, bf16[128,2048]{1,0:T(8,128)(2,1)S(1)}, u32[]{:S(2)}, u32[]{:S(2)}) %collective-permute-start.19) | collective-permute-done | bytes 524320 | tf_op jit(solution)/shard_map/ppermute | solution.py:214
  147.9 3.3 %collective-permute-done.20 = bf16[128,2048]{1,0:T(8,128)(2,1)S(1)} collective-permute-done((bf16[128,2048]{1,0:T(8,128)(2,1)S(1)}, bf16[128,2048]{1,0:T(8,128)(2,1)S(1)}, u32[]{:S(2)}, u32[]{:S(2)}) %collective-permute-start.20) | collective-permute-done | bytes 524320 | tf_op jit(solution)/shard_map/ppermute | solution.py:214
  151.3 1.7 collective-permute-start.23
  153.8 6.6 %collective-permute-done.23 = bf16[128,2048]{1,0:T(8,128)(2,1)S(1)} collective-permute-done((bf16[128,2048]{1,0:T(8,128)(2,1)S(1)}, bf16[128,2048]{1,0:T(8,128)(2,1)S(1)}, u32[]{:S(2)}, u32[]{:S(2)}) %collective-permute-start.23) | collective-permute-done | bytes 524320 | tf_op jit(solution)/shard_map/ppermute | solution.py:214
  160.4 3.5 %collective-permute-done.24 = bf16[128,2048]{1,0:T(8,128)(2,1)S(1)} collective-permute-done((bf16[128,2048]{1,0:T(8,128)(2,1)S(1)}, bf16[128,2048]{1,0:T(8,128)(2,1)S(1)}, u32[]{:S(2)}, u32[]{:S(2)}) %collective-permute-start.24) | collective-permute-done | bytes 524320 | tf_op jit(solution)/shard_map/ppermute | solution.py:214
  167.4 2.6 fusion.6
  171.5 7.9 %collective-permute-done.26 = bf16[128,2048]{1,0:T(8,128)(2,1)S(1)} collective-permute-done((bf16[128,2048]{1,0:T(8,128)(2,1)S(1)}, bf16[128,2048]{1,0:T(8,128)(2,1)S(1)}, u32[]{:S(2)}, u32[]{:S(2)}) %collective-permute-start.26) | collective-permute-done | bytes 524320 | tf_op jit(solution)/shard_map/ppermute | solution.py:214
  179.4 6.4 %collective-permute-done.29 = bf16[2,96,2048]{2,1,0:T(8,128)(2,1)S(1)} collective-permute-done((bf16[2,96,2048]{2,1,0:T(8,128)(2,1)S(1)}, bf16[2,96,2048]{2,1,0:T(8,128)(2,1)S(1)}, u32[]{:S(2)}, u32[]{:S(2)}) %collective-permute-start.29) | collective-permute-done | bytes 786464 | tf_op jit(solution)/shard_map/ppermute | solution.py:214
  186.0 1.8 collective-permute-start.28
  188.8 2.6 fusion.4
  192.9 13.1 %collective-permute-done.28 = bf16[2,96,2048]{2,1,0:T(8,128)(2,1)S(1)} collective-permute-done((bf16[2,96,2048]{2,1,0:T(8,128)(2,1)S(1)}, bf16[2,96,2048]{2,1,0:T(8,128)(2,1)S(1)}, u32[]{:S(2)}, u32[]{:S(2)}) %collective-permute-start.28) | collective-permute-done | bytes 786464 | tf_op jit(solution)/shard_map/ppermute | solution.py:214
  208.6 2.6 fusion.2
  213.4 2.6 fusion
  218.3 1.8 collective-permute-start.33
  221.3 16.9 %collective-permute-done.33 = bf16[2,96,2048]{2,1,0:T(8,128)(2,1)S(1)} collective-permute-done((bf16[2,96,2048]{2,1,0:T(8,128)(2,1)S(1)}, bf16[2,96,2048]{2,1,0:T(8,128)(2,1)S(1)}, u32[]{:S(2)}, u32[]{:S(2)}) %collective-permute-start.33) | collective-permute-done | bytes 786464 | tf_op jit(solution)/shard_map/ppermute | solution.py:214
  241.4 1.8 collective-permute-start.39
  243.6 10.0 %collective-permute-done.38 = bf16[128,2048]{1,0:T(8,128)(2,1)S(1)} collective-permute-done((bf16[128,2048]{1,0:T(8,128)(2,1)S(1)}, bf16[128,2048]{1,0:T(8,128)(2,1)S(1)}, u32[]{:S(2)}, u32[]{:S(2)}) %collective-permute-start.38) | collective-permute-done | bytes 524320 | tf_op jit(solution)/shard_map/ppermute | solution.py:214
  254.5 1.7 collective-permute-start.44
  256.3 1.7 collective-permute-start.45
  258.3 1.8 collective-permute-start.42
  260.1 12.3 %collective-permute-done.44 = bf16[2,96,2048]{2,1,0:T(8,128)(2,1)S(1)} collective-permute-done((bf16[2,96,2048]{2,1,0:T(8,128)(2,1)S(1)}, bf16[2,96,2048]{2,1,0:T(8,128)(2,1)S(1)}, u32[]{:S(2)}, u32[]{:S(2)}) %collective-permute-start.44) | collective-permute-done | bytes 786464 | tf_op jit(solution)/shard_map/ppermute | solution.py:214
  274.4 1.8 collective-permute-start.46
  278.1 2.4 collective-permute-start.43
  280.6 4.9 %collective-permute-done.46 = bf16[128,2048]{1,0:T(8,128)(2,1)S(1)} collective-permute-done((bf16[128,2048]{1,0:T(8,128)(2,1)S(1)}, bf16[128,2048]{1,0:T(8,128)(2,1)S(1)}, u32[]{:S(2)}, u32[]{:S(2)}) %collective-permute-start.46) | collective-permute-done | bytes 524320 | tf_op jit(solution)/shard_map/ppermute | solution.py:214
  285.4 2.1 collective-permute-done.47
  290.9 2.0 copy.69
  295.1 6.3 %collective-permute-done.43 = bf16[128,2048]{1,0:T(8,128)(2,1)} collective-permute-done((bf16[128,2048]{1,0:T(8,128)(2,1)}, bf16[128,2048]{1,0:T(8,128)(2,1)}, u32[]{:S(2)}, u32[]{:S(2)}) %collective-permute-start.43) | collective-permute-done | bytes 524320 | tf_op jit(solution)/shard_map/ppermute | solution.py:214
  301.4 6.8 %collective-permute-done.48 = bf16[128,2048]{1,0:T(8,128)(2,1)} collective-permute-done((bf16[128,2048]{1,0:T(8,128)(2,1)}, bf16[128,2048]{1,0:T(8,128)(2,1)}, u32[]{:S(2)}, u32[]{:S(2)}) %collective-permute-start.48) | collective-permute-done | bytes 524320 | tf_op jit(solution)/shard_map/ppermute | solution.py:214
  308.2 2.9 fusion.65
  (216 shorter events, 69.3 us)
Async XLA Ops:
  2.7 18.7 %collective-permute-start = (bf16[2048,128]{1,0:T(8,128)(2,1)}, bf16[2048,128]{1,0:T(8,128)(2,1)}, u32[]{:S(2)}, u32[]{:S(2)}) collective-permute-start(bf16[2048,128]{1,0:T(8,128)(2,1)} %constant_dynamic-slice_fusion.1), channel_id=1, source_target_pairs={{0,1},{1,0},{2,3},{3,2},{4,5},{5,4},{6,7},{7,6},{8,9},{9,8},{10,11... | collective-permute-start | bytes 1572872 | tf_op jit(solution)/shard_map/ppermute | solution.py:214
  5.6 32.1 %collective-permute-start.5 = (bf16[128,2048]{1,0:T(8,128)(2,1)}, bf16[128,2048]{1,0:T(8,128)(2,1)}, u32[]{:S(2)}, u32[]{:S(2)}) collective-permute-start(bf16[128,2048]{1,0:T(8,128)(2,1)} %tokens.1), channel_id=1, source_target_pairs={{0,4},{1,5},{2,6},{3,7},{4,0},{5,1},{6,2},{7,3},{8,12},{9,13},{10,... | collective-permute-start | bytes 1572872 | tf_op jit(solution)/shard_map/ppermute | solution.py:214
  21.4 16.3 %collective-permute-start.4 = (bf16[2048,128]{1,0:T(8,128)(2,1)}, bf16[2048,128]{1,0:T(8,128)(2,1)S(1)}, u32[]{:S(2)}, u32[]{:S(2)}) collective-permute-start(bf16[2048,128]{1,0:T(8,128)(2,1)} %collective-permute-done), channel_id=1, source_target_pairs={{0,16},{1,17},{2,18},{3,19},{4,20},{5,21},{6,22},{7,23},{8,24},{9,... | collective-permute-start | bytes 1572872 | tf_op jit(solution)/shard_map/ppermute | solution.py:214
  24.0 6.7 %collective-permute-start.3 = (bf16[144,256]{1,0:T(8,128)(2,1)S(1)}, bf16[144,256]{1,0:T(8,128)(2,1)S(1)}, u32[]{:S(2)}, u32[]{:S(2)}) collective-permute-start(bf16[144,256]{1,0:T(8,128)(2,1)S(1)} %get-tuple-element.159), channel_id=1, source_target_pairs={{0,6},{1,7},{2,4},{3,5},{4,2},{5,3},{6,0},{7,1},{8,14},{9,15},{10,... | collective-permute-start | bytes 221192 | tf_op jit(solution)/shard_map/ppermute | solution.py:214
  25.5 12.2 %collective-permute-start.2 = (bf16[144,256]{1,0:T(8,128)(2,1)S(1)}, bf16[144,256]{1,0:T(8,128)(2,1)S(1)}, u32[]{:S(2)}, u32[]{:S(2)}) collective-permute-start(bf16[144,256]{1,0:T(8,128)(2,1)S(1)} %get-tuple-element.158), channel_id=1, source_target_pairs={{0,4},{1,5},{2,6},{3,7},{4,0},{5,1},{6,2},{7,3},{8,12},{9,13},{10,... | collective-permute-start | bytes 221192 | tf_op jit(solution)/shard_map/ppermute | solution.py:214
  27.1 10.5 %collective-permute-start.1 = (bf16[144,256]{1,0:T(8,128)(2,1)S(1)}, bf16[144,256]{1,0:T(8,128)(2,1)S(1)}, u32[]{:S(2)}, u32[]{:S(2)}) collective-permute-start(bf16[144,256]{1,0:T(8,128)(2,1)S(1)} %get-tuple-element.157), channel_id=1, source_target_pairs={{0,2},{1,3},{2,0},{3,1},{4,6},{5,7},{6,4},{7,5},{8,10},{9,11},{10,... | collective-permute-start | bytes 221192 | tf_op jit(solution)/shard_map/ppermute | solution.py:214
  37.8 11.9 %collective-permute-start.7 = (bf16[4,144,256]{2,1,0:T(8,128)(2,1)S(1)}, bf16[4,144,256]{2,1,0:T(8,128)(2,1)S(1)}, u32[]{:S(2)}, u32[]{:S(2)}) collective-permute-start(bf16[4,144,256]{2,1,0:T(8,128)(2,1)S(1)} %pad_maximum_fusion.9.kv_here), channel_id=1, source_target_pairs={{0,1},{1,0},{2,3},{3,2},{4,5},{5,4},{6,7},{7,6},{8,9},{9,8},{10,11... | collective-permute-start | bytes 884744 | tf_op jit(solution)/shard_map/ppermute | solution.py:214
  38.3 12.8 %collective-permute-start.6 = (bf16[4,144,256]{2,1,0:T(8,128)(2,1)S(1)}, bf16[4,144,256]{2,1,0:T(8,128)(2,1)S(1)}, u32[]{:S(2)}, u32[]{:S(2)}) collective-permute-start(bf16[4,144,256]{2,1,0:T(8,128)(2,1)S(1)} %pad_maximum_fusion.9.kv_here), channel_id=1, source_target_pairs={{0,8},{8,16},{16,24},{1,9},{9,17},{17,25},{2,10},{10,18},{18,26},{... | collective-permute-start | bytes 884744 | tf_op jit(solution)/shard_map/ppermute | solution.py:15
  42.7 6.9 %collective-permute-start.8 = (bf16[2048,256]{1,0:T(8,128)(2,1)S(1)}, bf16[2048,256]{1,0:T(8,128)(2,1)S(1)}, u32[]{:S(2)}, u32[]{:S(2)}) collective-permute-start(bf16[2048,256]{1,0:T(8,128)(2,1)S(1)} %pad_maximum_fusion.1), channel_id=1, source_target_pairs={{0,8},{1,9},{2,10},{3,11},{4,12},{5,13},{6,14},{7,15},{8,0},{9,1},... | collective-permute-start | bytes 3145736 | tf_op jit(solution)/shard_map/ppermute | solution.py:214
  45.1 3.8 %collective-permute-start.18 = (bf16[4,16,128]{2,1,0:T(8,128)(2,1)S(1)}, bf16[4,16,128]{2,1,0:T(8,128)(2,1)S(1)}, u32[]{:S(2)}, u32[]{:S(2)}) collective-permute-start(bf16[4,16,128]{2,1,0:T(8,128)(2,1)S(1)} %slice.307), channel_id=1, source_target_pairs={{0,16},{1,17},{2,18},{3,19},{4,20},{5,21},{6,22},{7,23},{8,24},{9,... | collective-permute-start | bytes 49160 | tf_op jit(solution)/shard_map/ppermute | solution.py:214
  45.5 14.0 %collective-permute-start.10 = (bf16[128,2048]{1,0:T(8,128)(2,1)S(1)}, bf16[128,2048]{1,0:T(8,128)(2,1)S(1)}, u32[]{:S(2)}, u32[]{:S(2)}) collective-permute-start(bf16[128,2048]{1,0:T(8,128)(2,1)S(1)} %constant_dynamic-slice_fusion), channel_id=1, source_target_pairs={{0,1},{1,0},{2,3},{3,2},{4,5},{5,4},{6,7},{7,6},{8,9},{9,8},{10,11... | collective-permute-start | bytes 1572872 | tf_op jit(solution)/shard_map/ppermute | solution.py:214
  48.9 12.9 %collective-permute-start.11 = (bf16[128,2048]{1,0:T(8,128)(2,1)}, bf16[128,2048]{1,0:T(8,128)(2,1)S(1)}, u32[]{:S(2)}, u32[]{:S(2)}) collective-permute-start(bf16[128,2048]{1,0:T(8,128)(2,1)} %collective-permute-done.5), channel_id=1, source_target_pairs={{0,2},{1,3},{2,0},{3,1},{4,6},{5,7},{6,4},{7,5},{8,10},{9,11},{10,... | collective-permute-start | bytes 1572872 | tf_op jit(solution)/shard_map/ppermute | solution.py:214
  49.6 12.2 %collective-permute-start.9 = (bf16[4,144,256]{2,1,0:T(8,128)(2,1)S(1)}, bf16[4,144,256]{2,1,0:T(8,128)(2,1)S(1)}, u32[]{:S(2)}, u32[]{:S(2)}) collective-permute-start(bf16[4,144,256]{2,1,0:T(8,128)(2,1)S(1)} %collective-permute-done.7.kv_side), channel_id=1, source_target_pairs={{0,8},{8,16},{16,24},{1,9},{9,17},{17,25},{2,10},{10,18},{18,26},{... | collective-permute-start | bytes 884744 | tf_op jit(solution)/shard_map/ppermute | solution.py:15
  61.9 11.8 %collective-permute-start.13 = (bf16[128,2048]{1,0:T(8,128)(2,1)S(1)}, bf16[128,2048]{1,0:T(8,128)(2,1)S(1)}, u32[]{:S(2)}, u32[]{:S(2)}) collective-permute-start(bf16[128,2048]{1,0:T(8,128)(2,1)S(1)} %collective-permute-done.10), channel_id=1, source_target_pairs={{0,16},{1,17},{2,18},{3,19},{4,20},{5,21},{6,22},{7,23},{8,24},{9,... | collective-permute-start | bytes 1572872 | tf_op jit(solution)/shard_map/ppermute | solution.py:214
  62.6 19.0 %collective-permute-start.12 = (bf16[128,2048]{1,0:T(8,128)(2,1)S(1)}, bf16[128,2048]{1,0:T(8,128)(2,1)S(1)}, u32[]{:S(2)}, u32[]{:S(2)}) collective-permute-start(bf16[128,2048]{1,0:T(8,128)(2,1)S(1)} %copy-done.2), channel_id=1, source_target_pairs={{0,2},{1,3},{2,0},{3,1},{4,6},{5,7},{6,4},{7,5},{8,10},{9,11},{10,... | collective-permute-start | bytes 1572872 | tf_op jit(solution)/shard_map/ppermute | solution.py:214
  73.8 8.2 %collective-permute-start.14 = (bf16[256,2048]{1,0:T(8,128)(2,1)S(1)}, bf16[256,2048]{1,0:T(8,128)(2,1)S(1)}, u32[]{:S(2)}, u32[]{:S(2)}) collective-permute-start(bf16[256,2048]{1,0:T(8,128)(2,1)S(1)} %pad_maximum_fusion.4), channel_id=1, source_target_pairs={{0,8},{1,9},{2,10},{3,11},{4,12},{5,13},{6,14},{7,15},{8,0},{9,1},... | collective-permute-start | bytes 3145736 | tf_op jit(solution)/shard_map/ppermute | solution.py:214
  83.4 14.8 %collective-permute-start.16 = (bf16[128,2048]{1,0:T(8,128)(2,1)S(1)}, bf16[128,2048]{1,0:T(8,128)(2,1)S(1)}, u32[]{:S(2)}, u32[]{:S(2)}) collective-permute-start(bf16[128,2048]{1,0:T(8,128)(2,1)S(1)} %slice.381), channel_id=1, source_target_pairs={{0,2},{1,3},{2,0},{3,1},{4,6},{5,7},{6,4},{7,5},{8,10},{9,11},{10,... | collective-permute-start | bytes 1572872 | tf_op jit(solution)/shard_map/ppermute | solution.py:214
  91.0 27.0 %collective-permute-start.15 = (bf16[128,2048]{1,0:T(8,128)(2,1)S(1)}, bf16[128,2048]{1,0:T(8,128)(2,1)S(1)}, u32[]{:S(2)}, u32[]{:S(2)}) collective-permute-start(bf16[128,2048]{1,0:T(8,128)(2,1)S(1)} %slice.385), channel_id=1, source_target_pairs={{0,2},{1,3},{2,0},{3,1},{4,6},{5,7},{6,4},{7,5},{8,10},{9,11},{10,... | collective-permute-start | bytes 1572872 | tf_op jit(solution)/shard_map/ppermute | solution.py:214
  98.4 25.4 %collective-permute-start.17 = (bf16[128,2048]{1,0:T(8,128)(2,1)S(1)}, bf16[128,2048]{1,0:T(8,128)(2,1)S(1)}, u32[]{:S(2)}, u32[]{:S(2)}) collective-permute-start(bf16[128,2048]{1,0:T(8,128)(2,1)S(1)} %add_convert_fusion.1), channel_id=1, source_target_pairs={{0,4},{1,5},{2,6},{3,7},{4,0},{5,1},{6,2},{7,3},{8,12},{9,13},{10,... | collective-permute-start | bytes 1572872 | tf_op jit(solution)/shard_map/ppermute | solution.py:214
  124.5 12.3 %collective-permute-start.21 = (bf16[128,2048]{1,0:T(8,128)(2,1)S(1)}, bf16[128,2048]{1,0:T(8,128)(2,1)S(1)}, u32[]{:S(2)}, u32[]{:S(2)}) collective-permute-start(bf16[128,2048]{1,0:T(8,128)(2,1)S(1)} %fusion.61), channel_id=1, source_target_pairs={{0,1},{1,0},{2,3},{3,2},{4,5},{5,4},{6,7},{7,6},{8,9},{9,8},{10,11... | collective-permute-start | bytes 1572872 | tf_op jit(solution)/shard_map/ppermute | solution.py:214
  124.6 23.3 %collective-permute-start.19 = (bf16[128,2048]{1,0:T(8,128)(2,1)S(1)}, bf16[128,2048]{1,0:T(8,128)(2,1)S(1)}, u32[]{:S(2)}, u32[]{:S(2)}) collective-permute-start(bf16[128,2048]{1,0:T(8,128)(2,1)S(1)} %fusion.61), channel_id=1, source_target_pairs={{0,2},{1,3},{2,0},{3,1},{4,6},{5,7},{6,4},{7,5},{8,10},{9,11},{10,... | collective-permute-start | bytes 1572872 | tf_op jit(solution)/shard_map/ppermute | solution.py:214
  125.4 25.9 %collective-permute-start.20 = (bf16[128,2048]{1,0:T(8,128)(2,1)S(1)}, bf16[128,2048]{1,0:T(8,128)(2,1)S(1)}, u32[]{:S(2)}, u32[]{:S(2)}) collective-permute-start(bf16[128,2048]{1,0:T(8,128)(2,1)S(1)} %fusion.61), channel_id=1, source_target_pairs={{0,4},{1,5},{2,6},{3,7},{4,0},{5,1},{6,2},{7,3},{8,12},{9,13},{10,... | collective-permute-start | bytes 1572872 | tf_op jit(solution)/shard_map/ppermute | solution.py:214
  137.5 26.4 %collective-permute-start.25 = (bf16[2,96,2048]{2,1,0:T(8,128)(2,1)S(1)}, bf16[2,96,2048]{2,1,0:T(8,128)(2,1)S(1)}, u32[]{:S(2)}, u32[]{:S(2)}) collective-permute-start(bf16[2,96,2048]{2,1,0:T(8,128)(2,1)S(1)} %get-tuple-element.124), channel_id=1, source_target_pairs={{0,16},{1,17},{2,18},{3,19},{4,20},{5,21},{6,22},{7,23},{8,24},{9,... | collective-permute-start | bytes 2359304 | tf_op jit(solution)/shard_map/ppermute | solution.py:214
  151.3 9.2 %collective-permute-start.23 = (bf16[128,2048]{1,0:T(8,128)(2,1)S(1)}, bf16[128,2048]{1,0:T(8,128)(2,1)S(1)}, u32[]{:S(2)}, u32[]{:S(2)}) collective-permute-start(bf16[128,2048]{1,0:T(8,128)(2,1)S(1)} %collective-permute-done.20), channel_id=1, source_target_pairs={{0,1},{1,0},{2,3},{3,2},{4,5},{5,4},{6,7},{7,6},{8,9},{9,8},{10,11... | collective-permute-start | bytes 1572872 | tf_op jit(solution)/shard_map/ppermute | solution.py:214
  153.0 11.0 %collective-permute-start.24 = (bf16[128,2048]{1,0:T(8,128)(2,1)S(1)}, bf16[128,2048]{1,0:T(8,128)(2,1)S(1)}, u32[]{:S(2)}, u32[]{:S(2)}) collective-permute-start(bf16[128,2048]{1,0:T(8,128)(2,1)S(1)} %collective-permute-done.20), channel_id=1, source_target_pairs={{0,2},{1,3},{2,0},{3,1},{4,6},{5,7},{6,4},{7,5},{8,10},{9,11},{10,... | collective-permute-start | bytes 1572872 | tf_op jit(solution)/shard_map/ppermute | solution.py:214
  153.7 12.2 %collective-permute-start.22 = (bf16[128,2048]{1,0:T(8,128)(2,1)S(1)}, bf16[128,2048]{1,0:T(8,128)(2,1)S(1)}, u32[]{:S(2)}, u32[]{:S(2)}) collective-permute-start(bf16[128,2048]{1,0:T(8,128)(2,1)S(1)} %collective-permute-done.19), channel_id=1, source_target_pairs={{0,16},{1,17},{2,18},{3,19},{4,20},{5,21},{6,22},{7,23},{8,24},{9,... | collective-permute-start | bytes 1572872 | tf_op jit(solution)/shard_map/ppermute | solution.py:214
  164.2 3.2 %collective-permute-start.27 = (bf16[192,2048]{1,0:T(8,128)(2,1)S(1)}, bf16[192,2048]{1,0:T(8,128)(2,1)S(1)}, u32[]{:S(2)}, u32[]{:S(2)}) collective-permute-start(bf16[192,2048]{1,0:T(8,128)(2,1)S(1)} %bitcast.200), channel_id=1, source_target_pairs={{0,8},{1,9},{2,10},{3,11},{4,12},{5,13},{6,14},{7,15},{8,0},{9,1},... | collective-permute-start | bytes 2359304 | tf_op jit(solution)/shard_map/ppermute | solution.py:214
  165.8 13.5 %collective-permute-start.26 = (bf16[128,2048]{1,0:T(8,128)(2,1)S(1)}, bf16[128,2048]{1,0:T(8,128)(2,1)S(1)}, u32[]{:S(2)}, u32[]{:S(2)}) collective-permute-start(bf16[128,2048]{1,0:T(8,128)(2,1)S(1)} %collective-permute-done.24), channel_id=1, source_target_pairs={{0,16},{1,17},{2,18},{3,19},{4,20},{5,21},{6,22},{7,23},{8,24},{9,... | collective-permute-start | bytes 1572872 | tf_op jit(solution)/shard_map/ppermute | solution.py:214
  166.8 18.9 %collective-permute-start.29 = (bf16[2,96,2048]{2,1,0:T(8,128)(2,1)S(1)}, bf16[2,96,2048]{2,1,0:T(8,128)(2,1)S(1)}, u32[]{:S(2)}, u32[]{:S(2)}) collective-permute-start(bf16[2,96,2048]{2,1,0:T(8,128)(2,1)S(1)} %get-tuple-element.119), channel_id=1, source_target_pairs={{0,1},{1,0},{2,3},{3,2},{4,5},{5,4},{6,7},{7,6},{8,9},{9,8},{10,11... | collective-permute-start | bytes 2359304 | tf_op jit(solution)/shard_map/ppermute | solution.py:214
  185.9 3.0 collective-permute-start.30
  186.0 20.0 %collective-permute-start.28 = (bf16[2,96,2048]{2,1,0:T(8,128)(2,1)S(1)}, bf16[2,96,2048]{2,1,0:T(8,128)(2,1)S(1)}, u32[]{:S(2)}, u32[]{:S(2)}) collective-permute-start(bf16[2,96,2048]{2,1,0:T(8,128)(2,1)S(1)} %get-tuple-element.66), channel_id=1, source_target_pairs={{0,16},{1,17},{2,18},{3,19},{4,20},{5,21},{6,22},{7,23},{8,24},{9,... | collective-permute-start | bytes 2359304 | tf_op jit(solution)/shard_map/ppermute | solution.py:214
  188.5 19.7 %collective-permute-start.34 = (bf16[2,96,2048]{2,1,0:T(8,128)(2,1)S(1)}, bf16[2,96,2048]{2,1,0:T(8,128)(2,1)S(1)}, u32[]{:S(2)}, u32[]{:S(2)}) collective-permute-start(bf16[2,96,2048]{2,1,0:T(8,128)(2,1)S(1)} %get-tuple-element.111), channel_id=1, source_target_pairs={{0,1},{1,0},{2,3},{3,2},{4,5},{5,4},{6,7},{7,6},{8,9},{9,8},{10,11... | collective-permute-start | bytes 2359304 | tf_op jit(solution)/shard_map/ppermute | solution.py:214
  206.7 11.1 %collective-permute-start.40 = (bf16[192,2048]{1,0:T(8,128)(2,1)S(1)}, bf16[192,2048]{1,0:T(8,128)(2,1)S(1)}, u32[]{:S(2)}, u32[]{:S(2)}) collective-permute-start(bf16[192,2048]{1,0:T(8,128)(2,1)S(1)} %get-tuple-element.101), channel_id=1, source_target_pairs={{0,8},{1,9},{2,10},{3,11},{4,12},{5,13},{6,14},{7,15},{8,0},{9,1},... | collective-permute-start | bytes 2359304 | tf_op jit(solution)/shard_map/ppermute | solution.py:214
  208.4 4.9 %collective-permute-start.35 = (bf16[192,2048]{1,0:T(8,128)(2,1)S(1)}, bf16[192,2048]{1,0:T(8,128)(2,1)S(1)}, u32[]{:S(2)}, u32[]{:S(2)}) collective-permute-start(bf16[192,2048]{1,0:T(8,128)(2,1)S(1)} %bitcast.206), channel_id=1, source_target_pairs={{0,8},{1,9},{2,10},{3,11},{4,12},{5,13},{6,14},{7,15},{8,0},{9,1},... | collective-permute-start | bytes 2359304 | tf_op jit(solution)/shard_map/ppermute | solution.py:214
  212.8 5.2 %collective-permute-start.32 = (bf16[192,2048]{1,0:T(8,128)(2,1)S(1)}, bf16[192,2048]{1,0:T(8,128)(2,1)S(1)}, u32[]{:S(2)}, u32[]{:S(2)}) collective-permute-start(bf16[192,2048]{1,0:T(8,128)(2,1)S(1)} %get-tuple-element.113), channel_id=1, source_target_pairs={{0,8},{1,9},{2,10},{3,11},{4,12},{5,13},{6,14},{7,15},{8,0},{9,1},... | collective-permute-start | bytes 2359304 | tf_op jit(solution)/shard_map/ppermute | solution.py:214
  217.6 2.5 collective-permute-start.36
  218.3 19.9 %collective-permute-start.33 = (bf16[2,96,2048]{2,1,0:T(8,128)(2,1)S(1)}, bf16[2,96,2048]{2,1,0:T(8,128)(2,1)S(1)}, u32[]{:S(2)}, u32[]{:S(2)}) collective-permute-start(bf16[2,96,2048]{2,1,0:T(8,128)(2,1)S(1)} %bitcast.189), channel_id=1, source_target_pairs={{0,16},{1,17},{2,18},{3,19},{4,20},{5,21},{6,22},{7,23},{8,24},{9,... | collective-permute-start | bytes 2359304 | tf_op jit(solution)/shard_map/ppermute | solution.py:214
  220.5 19.5 %collective-permute-start.37 = (bf16[2,96,2048]{2,1,0:T(8,128)(2,1)S(1)}, bf16[2,96,2048]{2,1,0:T(8,128)(2,1)S(1)}, u32[]{:S(2)}, u32[]{:S(2)}) collective-permute-start(bf16[2,96,2048]{2,1,0:T(8,128)(2,1)S(1)} %bitcast.191), channel_id=1, source_target_pairs={{0,1},{1,0},{2,3},{3,2},{4,5},{5,4},{6,7},{7,6},{8,9},{9,8},{10,11... | collective-permute-start | bytes 2359304 | tf_op jit(solution)/shard_map/ppermute | solution.py:214
  221.1 22.1 %collective-permute-start.41 = (bf16[192,2048]{1,0:T(8,128)(2,1)S(1)}, bf16[192,2048]{1,0:T(8,128)(2,1)S(1)}, u32[]{:S(2)}, u32[]{:S(2)}) collective-permute-start(bf16[192,2048]{1,0:T(8,128)(2,1)S(1)} %get-tuple-element.99), channel_id=1, source_target_pairs={{0,8},{1,9},{2,10},{3,11},{4,12},{5,13},{6,14},{7,15},{8,0},{9,1},... | collective-permute-start | bytes 2359304 | tf_op jit(solution)/shard_map/ppermute | solution.py:214
  240.5 13.0 %collective-permute-start.38 = (bf16[128,2048]{1,0:T(8,128)(2,1)S(1)}, bf16[128,2048]{1,0:T(8,128)(2,1)S(1)}, u32[]{:S(2)}, u32[]{:S(2)}) collective-permute-start(bf16[128,2048]{1,0:T(8,128)(2,1)S(1)} %slice_bitcast_fusion.6), channel_id=1, source_target_pairs={{0,1},{1,0},{2,3},{3,2},{4,5},{5,4},{6,7},{7,6},{8,9},{9,8},{10,11... | collective-permute-start | bytes 1572872 | tf_op jit(solution)/shard_map/ppermute | solution.py:214
  241.4 13.2 %collective-permute-start.39 = (bf16[128,2048]{1,0:T(8,128)(2,1)S(1)}, bf16[128,2048]{1,0:T(8,128)(2,1)S(1)}, u32[]{:S(2)}, u32[]{:S(2)}) collective-permute-start(bf16[128,2048]{1,0:T(8,128)(2,1)S(1)} %slice_bitcast_fusion.5), channel_id=1, source_target_pairs={{0,16},{1,17},{2,18},{3,19},{4,20},{5,21},{6,22},{7,23},{8,24},{9,... | collective-permute-start | bytes 1572872 | tf_op jit(solution)/shard_map/ppermute | solution.py:214
  254.5 17.8 %collective-permute-start.44 = (bf16[2,96,2048]{2,1,0:T(8,128)(2,1)S(1)}, bf16[2,96,2048]{2,1,0:T(8,128)(2,1)S(1)}, u32[]{:S(2)}, u32[]{:S(2)}) collective-permute-start(bf16[2,96,2048]{2,1,0:T(8,128)(2,1)S(1)} %bitcast.188), channel_id=1, source_target_pairs={{0,16},{1,17},{2,18},{3,19},{4,20},{5,21},{6,22},{7,23},{8,24},{9,... | collective-permute-start | bytes 2359304 | tf_op jit(solution)/shard_map/ppermute | solution.py:214
  256.3 17.5 %collective-permute-start.45 = (bf16[2,96,2048]{2,1,0:T(8,128)(2,1)S(1)}, bf16[2,96,2048]{2,1,0:T(8,128)(2,1)S(1)}, u32[]{:S(2)}, u32[]{:S(2)}) collective-permute-start(bf16[2,96,2048]{2,1,0:T(8,128)(2,1)S(1)} %bitcast.190), channel_id=1, source_target_pairs={{0,1},{1,0},{2,3},{3,2},{4,5},{5,4},{6,7},{7,6},{8,9},{9,8},{10,11... | collective-permute-start | bytes 2359304 | tf_op jit(solution)/shard_map/ppermute | solution.py:214
  258.3 18.8 %collective-permute-start.42 = (bf16[128,2048]{1,0:T(8,128)(2,1)S(1)}, bf16[128,2048]{1,0:T(8,128)(2,1)S(1)}, u32[]{:S(2)}, u32[]{:S(2)}) collective-permute-start(bf16[128,2048]{1,0:T(8,128)(2,1)S(1)} %fusion.83), channel_id=1, source_target_pairs={{0,2},{1,3},{2,0},{3,1},{4,6},{5,7},{6,4},{7,5},{8,10},{9,11},{10,... | collective-permute-start | bytes 1572872 | tf_op jit(solution)/shard_map/ppermute | solution.py:214
  274.4 11.0 %collective-permute-start.46 = (bf16[128,2048]{1,0:T(8,128)(2,1)S(1)}, bf16[128,2048]{1,0:T(8,128)(2,1)S(1)}, u32[]{:S(2)}, u32[]{:S(2)}) collective-permute-start(bf16[128,2048]{1,0:T(8,128)(2,1)S(1)} %slice_bitcast_fusion.2), channel_id=1, source_target_pairs={{0,1},{1,0},{2,3},{3,2},{4,5},{5,4},{6,7},{7,6},{8,9},{9,8},{10,11... | collective-permute-start | bytes 1572872 | tf_op jit(solution)/shard_map/ppermute | solution.py:214
  276.7 10.8 %collective-permute-start.47 = (bf16[128,2048]{1,0:T(8,128)(2,1)S(1)}, bf16[128,2048]{1,0:T(8,128)(2,1)S(1)}, u32[]{:S(2)}, u32[]{:S(2)}) collective-permute-start(bf16[128,2048]{1,0:T(8,128)(2,1)S(1)} %slice_bitcast_fusion.1), channel_id=1, source_target_pairs={{0,16},{1,17},{2,18},{3,19},{4,20},{5,21},{6,22},{7,23},{8,24},{9,... | collective-permute-start | bytes 1572872 | tf_op jit(solution)/shard_map/ppermute | solution.py:214
  278.1 23.3 %collective-permute-start.43 = (bf16[128,2048]{1,0:T(8,128)(2,1)}, bf16[128,2048]{1,0:T(8,128)(2,1)}, u32[]{:S(2)}, u32[]{:S(2)}) collective-permute-start(bf16[128,2048]{1,0:T(8,128)(2,1)} %fusion.85), channel_id=1, source_target_pairs={{0,4},{1,5},{2,6},{3,7},{4,0},{5,1},{6,2},{7,3},{8,12},{9,13},{10,... | collective-permute-start | bytes 1572872 | tf_op jit(solution)/shard_map/ppermute | solution.py:214
  288.4 19.8 %collective-permute-start.48 = (bf16[128,2048]{1,0:T(8,128)(2,1)}, bf16[128,2048]{1,0:T(8,128)(2,1)}, u32[]{:S(2)}, u32[]{:S(2)}) collective-permute-start(bf16[128,2048]{1,0:T(8,128)(2,1)} %fusion.82), channel_id=1, source_target_pairs={{0,2},{1,3},{2,0},{3,1},{4,6},{5,7},{6,4},{7,5},{8,10},{9,11},{10,... | collective-permute-start | bytes 1572872 | tf_op jit(solution)/shard_map/ppermute | solution.py:214
  (16 other events, 332.2 us)

commit v4 on v3

--- a/solution.py
+++ b/solution.py
@@ -226,6 +226,12 @@
     return moved(block, lambda y, core, z, x: (y, 1 - core, z, x))
 
 
+def across(block, over_y):
+    if over_y:
+        return moved(block, lambda y, core, z, x: (1 - y, 1 - core, z, x))
+    return moved(block, lambda y, core, z, x: (y, 1 - core, z, 1 - x))
+
+
 def other_z(block, k):
     return moved(block, lambda y, core, z, x: (y, core, z ^ k, x))
 
@@ -244,7 +250,7 @@
 ):
     z, x, slot = place[0], place[1], place[2] + pl.program_id(0)
     rows = projected.shape[0]
-    head = gain.shape[0]
+    head = gain.shape[1]
     heads = projected.shape[1] // head
     half = head // 2
 
@@ -258,10 +264,11 @@
                     keys[pl.ds(row, rows), :] = source[k, :rows, :head]
                     values[:, pl.ds(row, rows)] = source[k, :rows, head:].astype(jnp.float32).T.astype(jnp.bfloat16)
 
+    gain_column = jnp.broadcast_to(gain[...], (rows, head)).T
     turned = []
     for h in range(heads):
         q = projected[:, h * head : (h + 1) * head].T
-        q = q * lax.rsqrt(jnp.mean(q * q, axis=0, keepdims=True) + 1e-06) * gain[...]
+        q = q * lax.rsqrt(jnp.mean(q * q, axis=0, keepdims=True) + 1e-06) * gain_column
         first, second = q[:half], q[half:]
         turned.append(
             jnp.concatenate(
@@ -312,7 +319,7 @@
             grid=(slots,),
             in_specs=[
                 pl.BlockSpec((rows, width), lambda s, *_: (s, 0)),
-                whole(head, 1),
+                whole(1, head),
                 pl.BlockSpec((1, head // 2, rows), lambda s, *_: (s, 0, 0)),
                 pl.BlockSpec((1, head // 2, rows), lambda s, *_: (s, 0, 0)),
                 pl.BlockSpec((1, 1, rows), lambda s, *_: (s, 0, 0)),
@@ -335,7 +342,7 @@
             transcendentals=slots * width * rows,
         ),
         name="attention",
-    )(place, low, projected, q_gain.reshape(head, 1), cosine, sine, start, *kv)
+    )(place, low, projected, q_gain.reshape(1, head), cosine, sine, start, *kv)
 
 
 def keyval_kernel(tokens, gain, key_gain, cosine, sine, w_key, w_value, out, normed):
@@ -343,10 +350,11 @@
     def _():
         normed[...] = root_mean_norm(tokens[...].astype(jnp.float32), gain[...]).astype(jnp.bfloat16)
 
-    head = key_gain.shape[0]
+    head = key_gain.shape[1]
     half = head // 2
     k = jnp.dot(normed[...], w_key[...], preferred_element_type=jnp.float32).T
-    k = k * lax.rsqrt(jnp.mean(k * k, axis=0, keepdims=True) + 1e-06) * key_gain[...]
+    k = k * lax.rsqrt(jnp.mean(k * k, axis=0, keepdims=True) + 1e-06)
+    k = k * jnp.broadcast_to(key_gain[...], (normed.shape[0], head)).T
     first, second = k[:half], k[half:]
     k = jnp.concatenate(
         [first * cosine[0] - second * sine[0], second * cosine[0] + first * sine[0]], axis=0
@@ -367,7 +375,7 @@
         in_specs=[
             whole(rows, width),
             whole(1, width),
-            whole(head, 1),
+            whole(1, head),
             pl.BlockSpec((1, head // 2, rows), lambda h: (0, 0, 0)),
             pl.BlockSpec((1, head // 2, rows), lambda h: (0, 0, 0)),
             pl.BlockSpec((width, head), lambda h: (0, h)),
@@ -381,7 +389,7 @@
             flops=2 * rows * width * w_keyval.shape[1], bytes_accessed=5 * 2**20, transcendentals=0
         ),
         name="keyval",
-    )(tokens, attn_gain.reshape(1, width), key_norm_gain.reshape(head, 1), cosine, sine, w_keyval, w_keyval)
+    )(tokens, attn_gain.reshape(1, width), key_norm_gain.reshape(1, head), cosine, sine, w_keyval, w_keyval)
 
 
 def grid_body(
@@ -421,9 +429,10 @@
     by_head = keyval_by_head(tokens, attn_gain, key_norm_gain, cosine, sine, w_keyval)
     part = w_query.shape[1] // 4
     quarter = y * 2 + core
+    far = other_z(tokens, 2)
     query_x = other_x(lax.dynamic_slice_in_dim(w_query, quarter * part, part, 1))
-    by_head, query_x = lax.optimization_barrier((by_head, query_x))
-    query_y = other_y(query_x)
+    by_head, late_segs, query_x, w_out = lax.optimization_barrier((by_head, seg_ids, query_x, w_out))
+    out_x = other_x(lax.dynamic_slice_in_dim(w_out, quarter * part, part, 0))
 
     top = expert_ids.shape[1]
     routes = jnp.concatenate([expert_ids.T.astype(jnp.bfloat16), gates.T], axis=0)
@@ -431,24 +440,22 @@
     pick = lambda h: jnp.concatenate(
         [lax.dynamic_index_in_dim(by_head, h, 0, keepdims=False), routes], axis=0
     )
-    kv_here = jnp.stack([pick(z)] + [other_z(pick(z ^ k), k) for k in (1, 2, 3)])
-    far = other_z(tokens, 2)
-    kv_here, query_y, far, w_query, w_out = lax.optimization_barrier(
-        (kv_here, query_y, far, w_query, w_out)
-    )
+    kv_parts = [other_z(pick(z ^ k), k) for k in (1, 2, 3)]
+    query_y = other_y(after(query_x, kv_parts[0]))
+    kv_here = jnp.stack([pick(z)] + kv_parts)
+    kv_here, out_x, far, w_query, w_out = lax.optimization_barrier((kv_here, out_x, far, w_query, w_out))
     kv_before, kv_side = passed_along(kv_here, "rep", 1), other_x(kv_here)
-    farther = other_z(far, 1)
+    farther, out_y = other_z(far, 1), other_y(out_x)
+    kv_side, query_y = lax.optimization_barrier((kv_side, query_y))
+    kv_before_side = passed_along(kv_side, "rep", 1)
     query_two = jnp.concatenate([query_x, query_y], axis=1)
     query_far = other_core(query_two)
-    out_x = other_x(lax.dynamic_slice_in_dim(w_out, quarter * part, part, 0))
-    kv_side, query_far = lax.optimization_barrier((kv_side, query_far))
-    kv_before_side = passed_along(kv_side, "rep", 1)
+    kv_before, kv_before_side, query_far, farther, out_y = lax.optimization_barrier(
+        (kv_before, kv_before_side, query_far, farther, out_y)
+    )
     w_query_wide = jnp.concatenate([w_query, query_two, query_far], axis=1)
-    kv_before, kv_before_side, out_x, farther = lax.optimization_barrier(
-        (kv_before, kv_before_side, out_x, farther)
-    )
+    out_two = jnp.concatenate([out_x, out_y], axis=0)
     near = other_z(after(tokens, farther), 1)
-    out_two = jnp.concatenate([out_x, other_y(out_x)], axis=0)
     w_out_wide = jnp.concatenate([w_out, out_two, other_core(out_two)], axis=0)
     raw = [tokens, near, far, farther]
 
@@ -459,9 +466,9 @@
     cache = cache.astype(jnp.bfloat16).reshape(pages, rows // pages, 2 * kv_width)
 
     slot_seg = jnp.concatenate(
-        [lax.dynamic_slice_in_dim(seg_ids, at, rows, 0) for at in slot_start]
-    )
-    starts = jnp.sum((seg_ids[None, :] < slot_seg[:, None]).astype(jnp.int32), axis=1)
+        [lax.dynamic_slice_in_dim(late_segs, at, rows, 0) for at in slot_start]
+    )
+    starts = jnp.sum((late_segs[None, :] < slot_seg[:, None]).astype(jnp.int32), axis=1)
     starts = (starts - (group_start - group_rows)).reshape(4, 1, rows)
     low = starts[:, 0, 0] // KEY_BLOCK
 
@@ -487,7 +494,9 @@
         term = jnp.dot(part, w_out_wide, preferred_element_type=jnp.float32).astype(jnp.bfloat16)
         return term[:rows], term[rows:]
 
-    term_2, term_3 = term_of(attended(2, projection(2)))
+    attended_far = attended(2, projection(2))
+    raw[1] = after(near, attended_far)
+    term_2, term_3 = term_of(attended_far)
     far_3 = other_z(term_3, 1)
     far = other_z(sum_of(term_2, far_3), 2)
     term_0, term_1 = term_of(attended(0, after(projection(0), term_3)))
@@ -497,7 +506,7 @@
     normed_moe = root_mean_norm(residual.astype(jnp.float32), moe_gain).astype(jnp.bfloat16)
 
     turned = (False, True, False, True)
-    routes = kv_here[:, rows:, :rows]
+    routes = after(kv_here[:, rows:, :rows], term_3)
     over_x, over_y = kv_side[:, rows:, :rows], other_y(routes)
     routes = jnp.stack(
         [jnp.stack([routes[k], (over_y if turned[k] else over_x)[k]]) for k in slots]
@@ -543,6 +552,7 @@
         kept = picked[:, :capacity].reshape(-1, width)
         return jnp.concatenate([kept, other_core(picked[:, capacity:].reshape(-1, width))], axis=0)
 
+    half = rows // 2
     near, far = other_z(normed_moe, 1), other_z(normed_moe, 2)
     mine_0, theirs_0 = picks(0, normed_moe, other_x(normed_moe))
     theirs_0 = other_y(theirs_0)
@@ -554,14 +564,31 @@
     side_1, mine_2, theirs_2 = together(side_1, mine_2, theirs_2)
     mine_1, theirs_1 = picks(1, near, side_1)
     theirs_1 = other_x(theirs_1)
+
+    def over_second(to_y, to_y_across, to_x, to_x_across):
+        return together(
+            other_y(to_y), across(to_y_across, True), other_x(to_x), across(to_x_across, False)
+        )
+
+    def experts_on(*parts):
+        return experts_of(jnp.concatenate(parts, axis=0).reshape(-1, width)).reshape(-1, capacity, width)
+
+    kept = lambda *parts: jnp.concatenate([part[:, :capacity] for part in parts], axis=0)
+    traded = lambda *parts: other_core(jnp.concatenate([part[:, capacity:] for part in parts], axis=0))
     result_0 = experts_of(routed(mine_0, theirs_0))
-    side_3, theirs_2, result_0 = together(side_3, theirs_2, result_0)
+    result_12 = experts_on(kept(mine_1, mine_2), traded(mine_1, mine_2))
+    side_3, theirs_2, result_0, result_12, theirs_1 = together(side_3, theirs_2, result_0, result_12, theirs_1)
     mine_3, theirs_3 = picks(3, farther, side_3)
-    theirs_2, theirs_3 = other_y(theirs_2), other_x(theirs_3)
-    result_1 = experts_of(routed(mine_1, after(theirs_1, side_3)))
-    theirs_2, result_1 = together(theirs_2, result_1)
-    result_2 = experts_of(routed(mine_2, theirs_2))
-    result_3 = experts_of(after(routed(mine_3, theirs_3), result_2))
+    late = traded(mine_3, theirs_1)
+    got = over_second(
+        theirs_2[:, :capacity], theirs_2[:, capacity:], theirs_3[:, :capacity], theirs_3[:, capacity:]
+    )
+    *got, late = together(*got, late)
+    got, late = together(experts_on(*got), late)
+    result_31 = experts_on(kept(mine_3, theirs_1), late)
+    both = lambda result: jnp.concatenate([result[:4], other_core(result[4:])], axis=1)
+    here_1, here_2 = jnp.split(both(result_12), 2)
+    here_3, there_1 = jnp.split(both(result_31), 2)
 
     def back(result):
         traded = other_core(result[4 * capacity :])
@@ -578,9 +605,9 @@
         ).astype(jnp.bfloat16)
         return total[0], total[1]
 
-    (here_0, there_0), (here_1, there_1) = back(result_0), back(result_1)
-    (here_2, there_2), (here_3, there_3) = back(result_2), back(result_3)
-    there_2, there_3 = together(other_y(there_2), other_x(there_3))
+    here_0, there_0 = back(result_0)
+    there = over_second(got[:2], got[2:4], got[4:6], got[6:])
+    there_2, there_3 = jnp.concatenate(there[:2], axis=1), jnp.concatenate(there[2:], axis=1)
     (own_2, side_2), (own_3, side_3) = summed(2, here_2, there_2), summed(3, here_3, there_3)
     side_2, side_3, there_0, there_1 = together(other_x(side_2), other_y(side_3), there_0, there_1)
     far_3 = other_z(sum_of(own_3, side_3), 1)
@@ -588,8 +615,11 @@
     (own_0, side_0), (own_1, side_1) = summed(0, here_0, there_0), summed(1, here_1, there_1)
     far = own_2.astype(jnp.float32) + side_2.astype(jnp.float32) + far_3.astype(jnp.float32)
     far = other_z(far.astype(jnp.bfloat16), 2)
-    side_0, side_1 = together(other_x(side_0), other_y(side_1))
-    near = other_z(sum_of(own_1, side_1), 1)
+    side_0 = other_x(side_0)
+    near = [
+        other_z(sum_of(own_1[part], other_y(side_1[part])), 1) for part in (slice(0, half), slice(half, rows))
+    ]
+    near = jnp.concatenate(near, axis=0)
     combined = residual.astype(jnp.float32)
     for value in (far, near, own_0, side_0):
         combined = combined + value.astype(jnp.float32)

time: 311 us -> 302 us (0.971)
  waiting for transfers between devices: 184 us -> 169 us
  starting transfers between devices: 52.1 us -> 59.4 us
    ppermute x47 -> x51, waiting for transfers between devices: 184 us -> 169 us  [moved(): return lax.ppermute(block, ('rep', 'tp'), route)]
    ppermute x47 -> x51, starting transfers between devices: 49.5 us -> 55.6 us  [moved(): return lax.ppermute(block, ('rep', 'tp'), route)]
  transfers between devices with their start and end apart: 49 -> 53, of which waited for: 30 -> 33; matrix products, arithmetic and copies ran while one was open for 17% -> 15% of each run, Pallas kernels for 5% -> 5%
where the time goes in v4:
time: 302 us; the launch traced here: 301 us
  waiting for transfers between devices  169 us (56%)
  starting transfers between devices  59.4 us (20%)
  matrix products  27 us (9%)
  local copies, waits for them, and re-layouts  14.7 us (5%)
  other arithmetic  14.5 us (5%)
  Pallas kernels  14.1 us (5%)
    ppermute x51, waiting for transfers between devices, moved(): return lax.ppermute(block, ('rep', 'tp'), route)  169 us
    ppermute x51, starting transfers between devices, moved(): return lax.ppermute(block, ('rep', 'tp'), route)  55.6 us
    dot_general x4, matrix products, experts_of(): jnp.dot(slot_rows_in, w_gate_up[0], preferred_element_type=jnp.float32)  10.5 us
    pallas_call x2, Pallas kernels, attend_slots(): pl.pallas_call(attention_kernel, grid_spec=pltpu.PrefetchScalarGridSpec(n...  8.77 us
  transfers between devices with their start and end apart: 53, of which 33 were waited for; matrix products, arithmetic and copies ran while one was open for 15% of the time, Pallas kernels for 5%

profile of v4, /device:TPU:0, one launch (start us, length us, event | category | flops | bytes accessed | tf_op | source)
XLA Modules:
  0.0 300.7 jit_solution(1286336895958145416)
XLA Ops:
  0.7 2.0 constant_dynamic-slice_fusion.1
  2.7 2.9 collective-permute-start
  5.6 2.6 collective-permute-start.5
  11.2 5.3 %keyval.1 = bf16[4,128,256]{2,1,0:T(8,128)(2,1)} custom-call(bf16[128,2048]{1,0:T(8,128)(2,1)} %tokens.1, f32[1,2048]{1,0:T(1,128)} %bitcast.208, f32[1,128]{1,0:T(1,128)} %bitcast.210, f32[4,64,128]{2,1,0:T(8,128)} %get-tuple-element.195.cosine, f32[4,64,128]{2,1,0:T(8,128)} %get-tuple-element.194.sine, bf16[2048,1024]{1,0:T(8,128)(2,1)} %w_value.1, ...), custom_call_target="tpu_custom_call" | custom-call | flops 536870912 | bytes 5242880 | tf_op jit(solution)/shard_map/keyval/pallas_call | solution.py:372
  20.1 1.8 collective-permute-start.4
  24.5 2.6 collective-permute-start.2
  27.5 3.0 %collective-permute-done.1 = bf16[144,256]{1,0:T(8,128)(2,1)S(1)} collective-permute-done((bf16[144,256]{1,0:T(8,128)(2,1)S(1)}, bf16[144,256]{1,0:T(8,128)(2,1)S(1)}, u32[]{:S(2)}, u32[]{:S(2)}) %collective-permute-start.1) | collective-permute-done | bytes 73760 | tf_op jit(solution)/shard_map/ppermute | solution.py:214
  32.1 4.9 %collective-permute-done.2 = bf16[144,256]{1,0:T(8,128)(2,1)S(1)} collective-permute-done((bf16[144,256]{1,0:T(8,128)(2,1)S(1)}, bf16[144,256]{1,0:T(8,128)(2,1)S(1)}, u32[]{:S(2)}, u32[]{:S(2)}) %collective-permute-start.2) | collective-permute-done | bytes 73760 | tf_op jit(solution)/shard_map/ppermute | solution.py:214
  39.0 1.9 collective-permute-start.11
  47.5 2.5 collective-permute-start.9
  50.2 2.5 collective-permute-done.11
  52.7 3.1 %collective-permute-done.12 = bf16[128,2048]{1,0:T(8,128)(2,1)S(1)} collective-permute-done((bf16[128,2048]{1,0:T(8,128)(2,1)S(1)}, bf16[128,2048]{1,0:T(8,128)(2,1)S(1)}, u32[]{:S(2)}, u32[]{:S(2)}) %collective-permute-start.12) | collective-permute-done | bytes 524320 | tf_op jit(solution)/shard_map/ppermute | solution.py:214
  57.4 5.6 %collective-permute-start.14 = (bf16[256,2048]{1,0:T(8,128)(2,1)S(1)}, bf16[256,2048]{1,0:T(8,128)(2,1)S(1)}, u32[]{:S(2)}, u32[]{:S(2)}) collective-permute-start(bf16[256,2048]{1,0:T(8,128)(2,1)S(1)} %pad_maximum_fusion.7), channel_id=1, source_target_pairs={{0,8},{1,9},{2,10},{3,11},{4,12},{5,13},{6,14},{7,15},{8,0},{9,1},... | collective-permute-start | bytes 3145736 | tf_op jit(solution)/shard_map/ppermute | solution.py:214
  63.1 2.3 fusion.67.projected
  65.4 5.3 %attention.2 = bf16[256,1024]{1,0:T(8,128)(2,1)S(1)} custom-call(s32[3]{0:T(128)S(1)} %pad_add_fusion.3.place, s32[2]{0:T(128)S(1)} %get-tuple-element.199.low, f32[256,1024]{1,0:T(8,128)S(1)} %fusion.67.projected, f32[1,128]{1,0:T(1,128)S(1)} %bitcast.173, f32[2,64,128]{2,1,0:T(8,128)S(1)} %get-tuple-element.177.cosine, ...), custom_call_target="tpu_custom_call" | custom-call | flops 536870912 | bytes 8388608 | tf_op jit(solution)/shard_map/attention/pallas_call | solution.py:315
  75.7 3.3 %collective-permute-start.18 = (bf16[4,16,128]{2,1,0:T(8,128)(2,1)S(1)}, bf16[4,16,128]{2,1,0:T(8,128)(2,1)S(1)}, u32[]{:S(2)}, u32[]{:S(2)}) collective-permute-start(bf16[4,16,128]{2,1,0:T(8,128)(2,1)S(1)} %slice.314), channel_id=1, source_target_pairs={{0,16},{1,17},{2,18},{3,19},{4,20},{5,21},{6,22},{7,23},{8,24},{9,... | collective-permute-start | bytes 49160 | tf_op jit(solution)/shard_map/ppermute | solution.py:214
  79.0 3.4 %attention.3 = bf16[256,1024]{1,0:T(8,128)(2,1)S(1)} custom-call(s32[3]{0:T(128)S(1)} %pad_add_fusion.1.place, s32[2]{0:T(128)S(1)} %get-tuple-element.198.low, f32[256,1024]{1,0:T(8,128)S(1)} %fusion.65.projected, f32[1,128]{1,0:T(1,128)S(1)} %bitcast.174, f32[2,64,128]{2,1,0:T(8,128)S(1)} %get-tuple-element.176.cosine, ...), custom_call_target="tpu_custom_call" | custom-call | flops 536870912 | bytes 8388608 | tf_op jit(solution)/shard_map/attention/pallas_call | solution.py:315
  85.6 2.5 collective-permute-done.16
  88.3 1.9 collective-permute-start.17
  90.6 16.7 %collective-permute-done.15 = bf16[128,2048]{1,0:T(8,128)(2,1)S(1)} collective-permute-done((bf16[128,2048]{1,0:T(8,128)(2,1)S(1)}, bf16[128,2048]{1,0:T(8,128)(2,1)S(1)}, u32[]{:S(2)}, u32[]{:S(2)}) %collective-permute-start.15) | collective-permute-done | bytes 524320 | tf_op jit(solution)/shard_map/ppermute | solution.py:214
  107.4 7.7 %collective-permute-done.17 = bf16[128,2048]{1,0:T(8,128)(2,1)S(1)} collective-permute-done((bf16[128,2048]{1,0:T(8,128)(2,1)S(1)}, bf16[128,2048]{1,0:T(8,128)(2,1)S(1)}, u32[]{:S(2)}, u32[]{:S(2)}) %collective-permute-start.17) | collective-permute-done | bytes 524320 | tf_op jit(solution)/shard_map/ppermute | solution.py:214
  115.9 2.4 collective-permute-start.20
  118.5 11.3 %collective-permute-done.21 = bf16[128,2048]{1,0:T(8,128)(2,1)S(1)} collective-permute-done((bf16[128,2048]{1,0:T(8,128)(2,1)S(1)}, bf16[128,2048]{1,0:T(8,128)(2,1)S(1)}, u32[]{:S(2)}, u32[]{:S(2)}) %collective-permute-start.21) | collective-permute-done | bytes 524320 | tf_op jit(solution)/shard_map/ppermute | solution.py:214
  130.5 1.9 collective-permute-start.24
  132.3 7.3 %collective-permute-done.19 = bf16[128,2048]{1,0:T(8,128)(2,1)S(1)} collective-permute-done((bf16[128,2048]{1,0:T(8,128)(2,1)S(1)}, bf16[128,2048]{1,0:T(8,128)(2,1)S(1)}, u32[]{:S(2)}, u32[]{:S(2)}) %collective-permute-start.19) | collective-permute-done | bytes 524320 | tf_op jit(solution)/shard_map/ppermute | solution.py:214
  139.7 2.4 collective-permute-done.20
  144.3 10.9 %collective-permute-done.22 = bf16[128,2048]{1,0:T(8,128)(2,1)S(1)} collective-permute-done((bf16[128,2048]{1,0:T(8,128)(2,1)S(1)}, bf16[128,2048]{1,0:T(8,128)(2,1)S(1)}, u32[]{:S(2)}, u32[]{:S(2)}) %collective-permute-start.22) | collective-permute-done | bytes 524320 | tf_op jit(solution)/shard_map/ppermute | solution.py:214
  157.1 3.4 %collective-permute-done.26 = bf16[128,2048]{1,0:T(8,128)(2,1)S(1)} collective-permute-done((bf16[128,2048]{1,0:T(8,128)(2,1)S(1)}, bf16[128,2048]{1,0:T(8,128)(2,1)S(1)}, u32[]{:S(2)}, u32[]{:S(2)}) %collective-permute-start.26) | collective-permute-done | bytes 524320 | tf_op jit(solution)/shard_map/ppermute | solution.py:214
  164.1 2.7 fusion.4
  166.8 2.6 fusion.6
  172.3 4.4 %collective-permute-done.25 = bf16[128,2048]{1,0:T(8,128)(2,1)S(1)} collective-permute-done((bf16[128,2048]{1,0:T(8,128)(2,1)S(1)}, bf16[128,2048]{1,0:T(8,128)(2,1)S(1)}, u32[]{:S(2)}, u32[]{:S(2)}) %collective-permute-start.25) | collective-permute-done | bytes 524320 | tf_op jit(solution)/shard_map/ppermute | solution.py:214
  176.8 4.7 %collective-permute-done.29 = bf16[2,96,2048]{2,1,0:T(8,128)(2,1)S(1)} collective-permute-done((bf16[2,96,2048]{2,1,0:T(8,128)(2,1)S(1)}, bf16[2,96,2048]{2,1,0:T(8,128)(2,1)S(1)}, u32[]{:S(2)}, u32[]{:S(2)}) %collective-permute-start.29) | collective-permute-done | bytes 786464 | tf_op jit(solution)/shard_map/ppermute | solution.py:214
  186.4 8.0 %collective-permute-done.33 = bf16[2,48,2048]{2,1,0:T(8,128)(2,1)S(1)} collective-permute-done((bf16[2,48,2048]{2,1,0:T(8,128)(2,1)S(1)}, bf16[2,48,2048]{2,1,0:T(8,128)(2,1)S(1)}, u32[]{:S(2)}, u32[]{:S(2)}) %collective-permute-start.33) | collective-permute-done | bytes 393248 | tf_op jit(solution)/shard_map/ppermute | solution.py:214
  194.4 7.5 %collective-permute-done.34 = bf16[2,48,2048]{2,1,0:T(8,128)(2,1)S(1)} collective-permute-done((bf16[2,48,2048]{2,1,0:T(8,128)(2,1)S(1)}, bf16[2,48,2048]{2,1,0:T(8,128)(2,1)S(1)}, u32[]{:S(2)}, u32[]{:S(2)}) %collective-permute-start.34) | collective-permute-done | bytes 393248 | tf_op jit(solution)/shard_map/ppermute | solution.py:214
  203.9 2.6 fusion.2
  208.1 2.6 fusion
  216.6 6.3 %collective-permute-done.36 = bf16[2,48,2048]{2,1,0:T(8,128)(2,1)S(1)} collective-permute-done((bf16[2,48,2048]{2,1,0:T(8,128)(2,1)S(1)}, bf16[2,48,2048]{2,1,0:T(8,128)(2,1)S(1)}, u32[]{:S(2)}, u32[]{:S(2)}) %collective-permute-start.36) | collective-permute-done | bytes 393248 | tf_op jit(solution)/shard_map/ppermute | solution.py:214
  222.9 7.3 %collective-permute-done.37 = bf16[2,48,2048]{2,1,0:T(8,128)(2,1)S(1)} collective-permute-done((bf16[2,48,2048]{2,1,0:T(8,128)(2,1)S(1)}, bf16[2,48,2048]{2,1,0:T(8,128)(2,1)S(1)}, u32[]{:S(2)}, u32[]{:S(2)}) %collective-permute-start.37) | collective-permute-done | bytes 393248 | tf_op jit(solution)/shard_map/ppermute | solution.py:214
  230.2 1.9 collective-permute-done.39
  234.6 12.2 %collective-permute-done.40 = bf16[128,2048]{1,0:T(8,128)(2,1)S(1)} collective-permute-done((bf16[128,2048]{1,0:T(8,128)(2,1)S(1)}, bf16[128,2048]{1,0:T(8,128)(2,1)S(1)}, u32[]{:S(2)}, u32[]{:S(2)}) %collective-permute-start.40) | collective-permute-done | bytes 524320 | tf_op jit(solution)/shard_map/ppermute | solution.py:214
  249.9 11.1 %collective-permute-done.44 = bf16[128,2048]{1,0:T(8,128)(2,1)S(1)} collective-permute-done((bf16[128,2048]{1,0:T(8,128)(2,1)S(1)}, bf16[128,2048]{1,0:T(8,128)(2,1)S(1)}, u32[]{:S(2)}, u32[]{:S(2)}) %collective-permute-start.44) | collective-permute-done | bytes 524320 | tf_op jit(solution)/shard_map/ppermute | solution.py:214
  262.1 4.6 %collective-permute-done.46 = bf16[2,96,2048]{2,1,0:T(8,128)(2,1)S(1)} collective-permute-done((bf16[2,96,2048]{2,1,0:T(8,128)(2,1)S(1)}, bf16[2,96,2048]{2,1,0:T(8,128)(2,1)S(1)}, u32[]{:S(2)}, u32[]{:S(2)}) %collective-permute-start.46) | collective-permute-done | bytes 786464 | tf_op jit(solution)/shard_map/ppermute | solution.py:214
  272.4 4.3 %collective-permute-done.48 = bf16[64,2048]{1,0:T(8,128)(2,1)S(1)} collective-permute-done((bf16[64,2048]{1,0:T(8,128)(2,1)S(1)}, bf16[64,2048]{1,0:T(8,128)(2,1)S(1)}, u32[]{:S(2)}, u32[]{:S(2)}) %collective-permute-start.48) | collective-permute-done | bytes 262176 | tf_op jit(solution)/shard_map/ppermute | solution.py:214
  276.6 2.8 collective-permute-done.50
  283.2 2.0 copy.33
  287.4 4.9 %collective-permute-done.49 = bf16[64,2048]{1,0:T(8,128)(2,1)} collective-permute-done((bf16[64,2048]{1,0:T(8,128)(2,1)}, bf16[64,2048]{1,0:T(8,128)(2,1)}, u32[]{:S(2)}, u32[]{:S(2)}) %collective-permute-start.49) | collective-permute-done | bytes 262176 | tf_op jit(solution)/shard_map/ppermute | solution.py:214
  292.3 5.5 %collective-permute-done.51 = bf16[64,2048]{1,0:T(8,128)(2,1)} collective-permute-done((bf16[64,2048]{1,0:T(8,128)(2,1)}, bf16[64,2048]{1,0:T(8,128)(2,1)}, u32[]{:S(2)}, u32[]{:S(2)}) %collective-permute-start.51) | collective-permute-done | bytes 262176 | tf_op jit(solution)/shard_map/ppermute | solution.py:214
  297.8 2.9 fusion.64
  (218 shorter events, 74.3 us)
Async XLA Ops:
  2.7 15.2 %collective-permute-start = (bf16[2048,128]{1,0:T(8,128)(2,1)}, bf16[2048,128]{1,0:T(8,128)(2,1)}, u32[]{:S(2)}, u32[]{:S(2)}) collective-permute-start(bf16[2048,128]{1,0:T(8,128)(2,1)} %constant_dynamic-slice_fusion.1), channel_id=1, source_target_pairs={{0,1},{1,0},{2,3},{3,2},{4,5},{5,4},{6,7},{7,6},{8,9},{9,8},{10,11... | collective-permute-start | bytes 1572872 | tf_op jit(solution)/shard_map/ppermute | solution.py:214
  5.6 31.4 %collective-permute-start.5 = (bf16[128,2048]{1,0:T(8,128)(2,1)}, bf16[128,2048]{1,0:T(8,128)(2,1)}, u32[]{:S(2)}, u32[]{:S(2)}) collective-permute-start(bf16[128,2048]{1,0:T(8,128)(2,1)} %tokens.1), channel_id=1, source_target_pairs={{0,4},{1,5},{2,6},{3,7},{4,0},{5,1},{6,2},{7,3},{8,12},{9,13},{10,... | collective-permute-start | bytes 1572872 | tf_op jit(solution)/shard_map/ppermute | solution.py:214
  20.1 16.9 %collective-permute-start.4 = (bf16[128,2048]{1,0:T(8,128)(2,1)S(1)}, bf16[128,2048]{1,0:T(8,128)(2,1)S(1)}, u32[]{:S(2)}, u32[]{:S(2)}) collective-permute-start(bf16[128,2048]{1,0:T(8,128)(2,1)S(1)} %constant_dynamic-slice_fusion), channel_id=1, source_target_pairs={{0,1},{1,0},{2,3},{3,2},{4,5},{5,4},{6,7},{7,6},{8,9},{9,8},{10,11... | collective-permute-start | bytes 1572872 | tf_op jit(solution)/shard_map/ppermute | solution.py:214
  24.5 12.4 %collective-permute-start.2 = (bf16[144,256]{1,0:T(8,128)(2,1)S(1)}, bf16[144,256]{1,0:T(8,128)(2,1)S(1)}, u32[]{:S(2)}, u32[]{:S(2)}) collective-permute-start(bf16[144,256]{1,0:T(8,128)(2,1)S(1)} %get-tuple-element.192), channel_id=1, source_target_pairs={{0,4},{1,5},{2,6},{3,7},{4,0},{5,1},{6,2},{7,3},{8,12},{9,13},{10,... | collective-permute-start | bytes 221192 | tf_op jit(solution)/shard_map/ppermute | solution.py:214
  27.1 9.9 %collective-permute-start.3 = (bf16[144,256]{1,0:T(8,128)(2,1)S(1)}, bf16[144,256]{1,0:T(8,128)(2,1)S(1)}, u32[]{:S(2)}, u32[]{:S(2)}) collective-permute-start(bf16[144,256]{1,0:T(8,128)(2,1)S(1)} %get-tuple-element.193), channel_id=1, source_target_pairs={{0,6},{1,7},{2,4},{3,5},{4,2},{5,3},{6,0},{7,1},{8,14},{9,15},{10,... | collective-permute-start | bytes 221192 | tf_op jit(solution)/shard_map/ppermute | solution.py:214
  30.5 14.1 %collective-permute-start.8 = (bf16[2048,128]{1,0:T(8,128)(2,1)}, bf16[2048,128]{1,0:T(8,128)(2,1)S(1)}, u32[]{:S(2)}, u32[]{:S(2)}) collective-permute-start(bf16[2048,128]{1,0:T(8,128)(2,1)} %collective-permute-done), channel_id=1, source_target_pairs={{0,16},{1,17},{2,18},{3,19},{4,20},{5,21},{6,22},{7,23},{8,24},{9,... | collective-permute-start | bytes 1572872 | tf_op jit(solution)/shard_map/ppermute | solution.py:214
  37.7 12.6 %collective-permute-start.6 = (bf16[4,144,256]{2,1,0:T(8,128)(2,1)S(1)}, bf16[4,144,256]{2,1,0:T(8,128)(2,1)S(1)}, u32[]{:S(2)}, u32[]{:S(2)}) collective-permute-start(bf16[4,144,256]{2,1,0:T(8,128)(2,1)S(1)} %pad_maximum_fusion.13.kv_here), channel_id=1, source_target_pairs={{0,8},{8,16},{16,24},{1,9},{9,17},{17,25},{2,10},{10,18},{18,26},{... | collective-permute-start | bytes 884744 | tf_op jit(solution)/shard_map/ppermute | solution.py:15
  39.0 13.7 %collective-permute-start.11 = (bf16[128,2048]{1,0:T(8,128)(2,1)}, bf16[128,2048]{1,0:T(8,128)(2,1)S(1)}, u32[]{:S(2)}, u32[]{:S(2)}) collective-permute-start(bf16[128,2048]{1,0:T(8,128)(2,1)} %collective-permute-done.5), channel_id=1, source_target_pairs={{0,2},{1,3},{2,0},{3,1},{4,6},{5,7},{6,4},{7,5},{8,10},{9,11},{10,... | collective-permute-start | bytes 1572872 | tf_op jit(solution)/shard_map/ppermute | solution.py:214
  40.9 14.9 %collective-permute-start.12 = (bf16[128,2048]{1,0:T(8,128)(2,1)S(1)}, bf16[128,2048]{1,0:T(8,128)(2,1)S(1)}, u32[]{:S(2)}, u32[]{:S(2)}) collective-permute-start(bf16[128,2048]{1,0:T(8,128)(2,1)S(1)} %collective-permute-done.4), channel_id=1, source_target_pairs={{0,16},{1,17},{2,18},{3,19},{4,20},{5,21},{6,22},{7,23},{8,24},{9,... | collective-permute-start | bytes 1572872 | tf_op jit(solution)/shard_map/ppermute | solution.py:214
  45.8 10.0 %collective-permute-start.10 = (bf16[2048,256]{1,0:T(8,128)(2,1)S(1)}, bf16[2048,256]{1,0:T(8,128)(2,1)S(1)}, u32[]{:S(2)}, u32[]{:S(2)}) collective-permute-start(bf16[2048,256]{1,0:T(8,128)(2,1)S(1)} %pad_maximum_fusion.4), channel_id=1, source_target_pairs={{0,8},{1,9},{2,10},{3,11},{4,12},{5,13},{6,14},{7,15},{8,0},{9,1},... | collective-permute-start | bytes 3145736 | tf_op jit(solution)/shard_map/ppermute | solution.py:214
  57.2 13.7 %collective-permute-start.13 = (bf16[128,2048]{1,0:T(8,128)(2,1)S(1)}, bf16[128,2048]{1,0:T(8,128)(2,1)S(1)}, u32[]{:S(2)}, u32[]{:S(2)}) collective-permute-start(bf16[128,2048]{1,0:T(8,128)(2,1)S(1)} %copy-done.3), channel_id=1, source_target_pairs={{0,2},{1,3},{2,0},{3,1},{4,6},{5,7},{6,4},{7,5},{8,10},{9,11},{10,... | collective-permute-start | bytes 1572872 | tf_op jit(solution)/shard_map/ppermute | solution.py:214
  57.4 15.1 %collective-permute-start.14 = (bf16[256,2048]{1,0:T(8,128)(2,1)S(1)}, bf16[256,2048]{1,0:T(8,128)(2,1)S(1)}, u32[]{:S(2)}, u32[]{:S(2)}) collective-permute-start(bf16[256,2048]{1,0:T(8,128)(2,1)S(1)} %pad_maximum_fusion.7), channel_id=1, source_target_pairs={{0,8},{1,9},{2,10},{3,11},{4,12},{5,13},{6,14},{7,15},{8,0},{9,1},... | collective-permute-start | bytes 3145736 | tf_op jit(solution)/shard_map/ppermute | solution.py:214
  73.9 14.2 %collective-permute-start.16 = (bf16[128,2048]{1,0:T(8,128)(2,1)S(1)}, bf16[128,2048]{1,0:T(8,128)(2,1)S(1)}, u32[]{:S(2)}, u32[]{:S(2)}) collective-permute-start(bf16[128,2048]{1,0:T(8,128)(2,1)S(1)} %slice.390), channel_id=1, source_target_pairs={{0,2},{1,3},{2,0},{3,1},{4,6},{5,7},{6,4},{7,5},{8,10},{9,11},{10,... | collective-permute-start | bytes 1572872 | tf_op jit(solution)/shard_map/ppermute | solution.py:214
  75.7 9.9 %collective-permute-start.18 = (bf16[4,16,128]{2,1,0:T(8,128)(2,1)S(1)}, bf16[4,16,128]{2,1,0:T(8,128)(2,1)S(1)}, u32[]{:S(2)}, u32[]{:S(2)}) collective-permute-start(bf16[4,16,128]{2,1,0:T(8,128)(2,1)S(1)} %slice.314), channel_id=1, source_target_pairs={{0,16},{1,17},{2,18},{3,19},{4,20},{5,21},{6,22},{7,23},{8,24},{9,... | collective-permute-start | bytes 49160 | tf_op jit(solution)/shard_map/ppermute | solution.py:214
  83.8 23.6 %collective-permute-start.15 = (bf16[128,2048]{1,0:T(8,128)(2,1)S(1)}, bf16[128,2048]{1,0:T(8,128)(2,1)S(1)}, u32[]{:S(2)}, u32[]{:S(2)}) collective-permute-start(bf16[128,2048]{1,0:T(8,128)(2,1)S(1)} %slice.394), channel_id=1, source_target_pairs={{0,2},{1,3},{2,0},{3,1},{4,6},{5,7},{6,4},{7,5},{8,10},{9,11},{10,... | collective-permute-start | bytes 1572872 | tf_op jit(solution)/shard_map/ppermute | solution.py:214
  88.3 26.8 %collective-permute-start.17 = (bf16[128,2048]{1,0:T(8,128)(2,1)S(1)}, bf16[128,2048]{1,0:T(8,128)(2,1)S(1)}, u32[]{:S(2)}, u32[]{:S(2)}) collective-permute-start(bf16[128,2048]{1,0:T(8,128)(2,1)S(1)} %add_convert_fusion.1), channel_id=1, source_target_pairs={{0,4},{1,5},{2,6},{3,7},{4,0},{5,1},{6,2},{7,3},{8,12},{9,13},{10,... | collective-permute-start | bytes 1572872 | tf_op jit(solution)/shard_map/ppermute | solution.py:214
  115.7 14.0 %collective-permute-start.21 = (bf16[128,2048]{1,0:T(8,128)(2,1)S(1)}, bf16[128,2048]{1,0:T(8,128)(2,1)S(1)}, u32[]{:S(2)}, u32[]{:S(2)}) collective-permute-start(bf16[128,2048]{1,0:T(8,128)(2,1)S(1)} %fusion.60), channel_id=1, source_target_pairs={{0,1},{1,0},{2,3},{3,2},{4,5},{5,4},{6,7},{7,6},{8,9},{9,8},{10,11... | collective-permute-start | bytes 1572872 | tf_op jit(solution)/shard_map/ppermute | solution.py:214
  115.8 23.8 %collective-permute-start.19 = (bf16[128,2048]{1,0:T(8,128)(2,1)S(1)}, bf16[128,2048]{1,0:T(8,128)(2,1)S(1)}, u32[]{:S(2)}, u32[]{:S(2)}) collective-permute-start(bf16[128,2048]{1,0:T(8,128)(2,1)S(1)} %fusion.60), channel_id=1, source_target_pairs={{0,2},{1,3},{2,0},{3,1},{4,6},{5,7},{6,4},{7,5},{8,10},{9,11},{10,... | collective-permute-start | bytes 1572872 | tf_op jit(solution)/shard_map/ppermute | solution.py:214
  115.9 26.2 %collective-permute-start.20 = (bf16[128,2048]{1,0:T(8,128)(2,1)S(1)}, bf16[128,2048]{1,0:T(8,128)(2,1)S(1)}, u32[]{:S(2)}, u32[]{:S(2)}) collective-permute-start(bf16[128,2048]{1,0:T(8,128)(2,1)S(1)} %fusion.60), channel_id=1, source_target_pairs={{0,4},{1,5},{2,6},{3,7},{4,0},{5,1},{6,2},{7,3},{8,12},{9,13},{10,... | collective-permute-start | bytes 1572872 | tf_op jit(solution)/shard_map/ppermute | solution.py:214
  130.5 25.9 %collective-permute-start.24 = (bf16[2,96,2048]{2,1,0:T(8,128)(2,1)S(1)}, bf16[2,96,2048]{2,1,0:T(8,128)(2,1)S(1)}, u32[]{:S(2)}, u32[]{:S(2)}) collective-permute-start(bf16[2,96,2048]{2,1,0:T(8,128)(2,1)S(1)} %get-tuple-element.148), channel_id=1, source_target_pairs={{0,16},{1,17},{2,18},{3,19},{4,20},{5,21},{6,22},{7,23},{8,24},{9,... | collective-permute-start | bytes 2359304 | tf_op jit(solution)/shard_map/ppermute | solution.py:214
  142.1 13.1 %collective-permute-start.22 = (bf16[128,2048]{1,0:T(8,128)(2,1)S(1)}, bf16[128,2048]{1,0:T(8,128)(2,1)S(1)}, u32[]{:S(2)}, u32[]{:S(2)}) collective-permute-start(bf16[128,2048]{1,0:T(8,128)(2,1)S(1)} %collective-permute-done.20), channel_id=1, source_target_pairs={{0,1},{1,0},{2,3},{3,2},{4,5},{5,4},{6,7},{7,6},{8,9},{9,8},{10,11... | collective-permute-start | bytes 1572872 | tf_op jit(solution)/shard_map/ppermute | solution.py:214
  143.8 12.6 %collective-permute-start.23 = (bf16[128,2048]{1,0:T(8,128)(2,1)S(1)}, bf16[128,2048]{1,0:T(8,128)(2,1)S(1)}, u32[]{:S(2)}, u32[]{:S(2)}) collective-permute-start(bf16[128,2048]{1,0:T(8,128)(2,1)S(1)} %collective-permute-done.20), channel_id=1, source_target_pairs={{0,2},{1,3},{2,0},{3,1},{4,6},{5,7},{6,4},{7,5},{8,10},{9,11},{10,... | collective-permute-start | bytes 1572872 | tf_op jit(solution)/shard_map/ppermute | solution.py:214
  144.2 16.3 %collective-permute-start.26 = (bf16[128,2048]{1,0:T(8,128)(2,1)S(1)}, bf16[128,2048]{1,0:T(8,128)(2,1)S(1)}, u32[]{:S(2)}, u32[]{:S(2)}) collective-permute-start(bf16[128,2048]{1,0:T(8,128)(2,1)S(1)} %collective-permute-done.19), channel_id=1, source_target_pairs={{0,16},{1,17},{2,18},{3,19},{4,20},{5,21},{6,22},{7,23},{8,24},{9,... | collective-permute-start | bytes 1572872 | tf_op jit(solution)/shard_map/ppermute | solution.py:214
  161.5 20.0 %collective-permute-start.29 = (bf16[2,96,2048]{2,1,0:T(8,128)(2,1)S(1)}, bf16[2,96,2048]{2,1,0:T(8,128)(2,1)S(1)}, u32[]{:S(2)}, u32[]{:S(2)}) collective-permute-start(bf16[2,96,2048]{2,1,0:T(8,128)(2,1)S(1)} %slice.416), channel_id=1, source_target_pairs={{0,1},{1,0},{2,3},{3,2},{4,5},{5,4},{6,7},{7,6},{8,9},{9,8},{10,11... | collective-permute-start | bytes 2359304 | tf_op jit(solution)/shard_map/ppermute | solution.py:214
  162.7 14.1 %collective-permute-start.25 = (bf16[128,2048]{1,0:T(8,128)(2,1)S(1)}, bf16[128,2048]{1,0:T(8,128)(2,1)S(1)}, u32[]{:S(2)}, u32[]{:S(2)}) collective-permute-start(bf16[128,2048]{1,0:T(8,128)(2,1)S(1)} %collective-permute-done.23), channel_id=1, source_target_pairs={{0,16},{1,17},{2,18},{3,19},{4,20},{5,21},{6,22},{7,23},{8,24},{9,... | collective-permute-start | bytes 1572872 | tf_op jit(solution)/shard_map/ppermute | solution.py:214
  182.4 21.3 %collective-permute-start.35 = (bf16[4,48,2048]{2,1,0:T(8,128)(2,1)S(1)}, bf16[4,48,2048]{2,1,0:T(8,128)(2,1)S(1)}, u32[]{:S(2)}, u32[]{:S(2)}) collective-permute-start(bf16[4,48,2048]{2,1,0:T(8,128)(2,1)S(1)} %pad_maximum_fusion.10), channel_id=1, source_target_pairs={{0,8},{1,9},{2,10},{3,11},{4,12},{5,13},{6,14},{7,15},{8,0},{9,1},... | collective-permute-start | bytes 2359304 | tf_op jit(solution)/shard_map/ppermute | solution.py:214
  182.5 12.0 %collective-permute-start.33 = (bf16[2,48,2048]{2,1,0:T(8,128)(2,1)S(1)}, bf16[2,48,2048]{2,1,0:T(8,128)(2,1)S(1)}, u32[]{:S(2)}, u32[]{:S(2)}) collective-permute-start(bf16[2,48,2048]{2,1,0:T(8,128)(2,1)S(1)} %get-tuple-element.135), channel_id=1, source_target_pairs={{0,1},{1,0},{2,3},{3,2},{4,5},{5,4},{6,7},{7,6},{8,9},{9,8},{10,11... | collective-permute-start | bytes 1179656 | tf_op jit(solution)/shard_map/ppermute | solution.py:214
  183.1 18.8 %collective-permute-start.34 = (bf16[2,48,2048]{2,1,0:T(8,128)(2,1)S(1)}, bf16[2,48,2048]{2,1,0:T(8,128)(2,1)S(1)}, u32[]{:S(2)}, u32[]{:S(2)}) collective-permute-start(bf16[2,48,2048]{2,1,0:T(8,128)(2,1)S(1)} %get-tuple-element.134), channel_id=1, source_target_pairs={{0,9},{1,8},{2,11},{3,10},{4,13},{5,12},{6,15},{7,14},{8,1},{9,0},... | collective-permute-start | bytes 1179656 | tf_op jit(solution)/shard_map/ppermute | solution.py:214
  184.4 17.6 %collective-permute-start.31 = (bf16[2,48,2048]{2,1,0:T(8,128)(2,1)S(1)}, bf16[2,48,2048]{2,1,0:T(8,128)(2,1)S(1)}, u32[]{:S(2)}, u32[]{:S(2)}) collective-permute-start(bf16[2,48,2048]{2,1,0:T(8,128)(2,1)S(1)} %get-tuple-element.157), channel_id=1, source_target_pairs={{0,16},{1,17},{2,18},{3,19},{4,20},{5,21},{6,22},{7,23},{8,24},{9,... | collective-permute-start | bytes 1179656 | tf_op jit(solution)/shard_map/ppermute | solution.py:214
  184.7 18.9 %collective-permute-start.32 = (bf16[2,48,2048]{2,1,0:T(8,128)(2,1)S(1)}, bf16[2,48,2048]{2,1,0:T(8,128)(2,1)S(1)}, u32[]{:S(2)}, u32[]{:S(2)}) collective-permute-start(bf16[2,48,2048]{2,1,0:T(8,128)(2,1)S(1)} %get-tuple-element.156), channel_id=1, source_target_pairs={{0,24},{1,25},{2,26},{3,27},{4,28},{5,29},{6,30},{7,31},{8,16},{9,... | collective-permute-start | bytes 1179656 | tf_op jit(solution)/shard_map/ppermute | solution.py:214
  194.4 21.7 %collective-permute-start.30 = (bf16[4,48,2048]{2,1,0:T(8,128)(2,1)S(1)}, bf16[4,48,2048]{2,1,0:T(8,128)(2,1)S(1)}, u32[]{:S(2)}, u32[]{:S(2)}) collective-permute-start(bf16[4,48,2048]{2,1,0:T(8,128)(2,1)S(1)} %get-tuple-element.136), channel_id=1, source_target_pairs={{0,8},{1,9},{2,10},{3,11},{4,12},{5,13},{6,14},{7,15},{8,0},{9,1},... | collective-permute-start | bytes 2359304 | tf_op jit(solution)/shard_map/ppermute | solution.py:214
  210.9 12.0 %collective-permute-start.36 = (bf16[2,48,2048]{2,1,0:T(8,128)(2,1)S(1)}, bf16[2,48,2048]{2,1,0:T(8,128)(2,1)S(1)}, u32[]{:S(2)}, u32[]{:S(2)}) collective-permute-start(bf16[2,48,2048]{2,1,0:T(8,128)(2,1)S(1)} %get-tuple-element.141), channel_id=1, source_target_pairs={{0,16},{1,17},{2,18},{3,19},{4,20},{5,21},{6,22},{7,23},{8,24},{9,... | collective-permute-start | bytes 1179656 | tf_op jit(solution)/shard_map/ppermute | solution.py:214
  211.3 19.0 %collective-permute-start.37 = (bf16[2,48,2048]{2,1,0:T(8,128)(2,1)S(1)}, bf16[2,48,2048]{2,1,0:T(8,128)(2,1)S(1)}, u32[]{:S(2)}, u32[]{:S(2)}) collective-permute-start(bf16[2,48,2048]{2,1,0:T(8,128)(2,1)S(1)} %get-tuple-element.140), channel_id=1, source_target_pairs={{0,24},{1,25},{2,26},{3,27},{4,28},{5,29},{6,30},{7,31},{8,16},{9,... | collective-permute-start | bytes 1179656 | tf_op jit(solution)/shard_map/ppermute | solution.py:214
  212.7 17.5 %collective-permute-start.38 = (bf16[2,48,2048]{2,1,0:T(8,128)(2,1)S(1)}, bf16[2,48,2048]{2,1,0:T(8,128)(2,1)S(1)}, u32[]{:S(2)}, u32[]{:S(2)}) collective-permute-start(bf16[2,48,2048]{2,1,0:T(8,128)(2,1)S(1)} %get-tuple-element.139), channel_id=1, source_target_pairs={{0,1},{1,0},{2,3},{3,2},{4,5},{5,4},{6,7},{7,6},{8,9},{9,8},{10,11... | collective-permute-start | bytes 1179656 | tf_op jit(solution)/shard_map/ppermute | solution.py:214
  213.3 18.8 %collective-permute-start.39 = (bf16[2,48,2048]{2,1,0:T(8,128)(2,1)S(1)}, bf16[2,48,2048]{2,1,0:T(8,128)(2,1)S(1)}, u32[]{:S(2)}, u32[]{:S(2)}) collective-permute-start(bf16[2,48,2048]{2,1,0:T(8,128)(2,1)S(1)} %get-tuple-element.138), channel_id=1, source_target_pairs={{0,9},{1,8},{2,11},{3,10},{4,13},{5,12},{6,15},{7,14},{8,1},{9,0},... | collective-permute-start | bytes 1179656 | tf_op jit(solution)/shard_map/ppermute | solution.py:214
  216.1 17.2 %collective-permute-start.41 = (bf16[4,48,2048]{2,1,0:T(8,128)(2,1)S(1)}, bf16[4,48,2048]{2,1,0:T(8,128)(2,1)S(1)}, u32[]{:S(2)}, u32[]{:S(2)}) collective-permute-start(bf16[4,48,2048]{2,1,0:T(8,128)(2,1)S(1)} %bitcast.187), channel_id=1, source_target_pairs={{0,8},{1,9},{2,10},{3,11},{4,12},{5,13},{6,14},{7,15},{8,0},{9,1},... | collective-permute-start | bytes 2359304 | tf_op jit(solution)/shard_map/ppermute | solution.py:214
  222.9 11.4 %collective-permute-start.43 = (bf16[192,2048]{1,0:T(8,128)(2,1)S(1)}, bf16[192,2048]{1,0:T(8,128)(2,1)S(1)}, u32[]{:S(2)}, u32[]{:S(2)}) collective-permute-start(bf16[192,2048]{1,0:T(8,128)(2,1)S(1)} %get-tuple-element.129), channel_id=1, source_target_pairs={{0,8},{1,9},{2,10},{3,11},{4,12},{5,13},{6,14},{7,15},{8,0},{9,1},... | collective-permute-start | bytes 2359304 | tf_op jit(solution)/shard_map/ppermute | solution.py:214
  232.6 14.2 %collective-permute-start.40 = (bf16[128,2048]{1,0:T(8,128)(2,1)S(1)}, bf16[128,2048]{1,0:T(8,128)(2,1)S(1)}, u32[]{:S(2)}, u32[]{:S(2)}) collective-permute-start(bf16[128,2048]{1,0:T(8,128)(2,1)S(1)} %slice_bitcast_fusion.4), channel_id=1, source_target_pairs={{0,1},{1,0},{2,3},{3,2},{4,5},{5,4},{6,7},{7,6},{8,9},{9,8},{10,11... | collective-permute-start | bytes 1572872 | tf_op jit(solution)/shard_map/ppermute | solution.py:214
  234.0 13.9 %collective-permute-start.42 = (bf16[128,2048]{1,0:T(8,128)(2,1)S(1)}, bf16[128,2048]{1,0:T(8,128)(2,1)S(1)}, u32[]{:S(2)}, u32[]{:S(2)}) collective-permute-start(bf16[128,2048]{1,0:T(8,128)(2,1)S(1)} %slice_bitcast_fusion.3), channel_id=1, source_target_pairs={{0,16},{1,17},{2,18},{3,19},{4,20},{5,21},{6,22},{7,23},{8,24},{9,... | collective-permute-start | bytes 1572872 | tf_op jit(solution)/shard_map/ppermute | solution.py:214
  248.0 13.0 %collective-permute-start.44 = (bf16[128,2048]{1,0:T(8,128)(2,1)S(1)}, bf16[128,2048]{1,0:T(8,128)(2,1)S(1)}, u32[]{:S(2)}, u32[]{:S(2)}) collective-permute-start(bf16[128,2048]{1,0:T(8,128)(2,1)S(1)} %fusion.81), channel_id=1, source_target_pairs={{0,2},{1,3},{2,0},{3,1},{4,6},{5,7},{6,4},{7,5},{8,10},{9,11},{10,... | collective-permute-start | bytes 1572872 | tf_op jit(solution)/shard_map/ppermute | solution.py:214
  248.1 18.7 %collective-permute-start.46 = (bf16[2,96,2048]{2,1,0:T(8,128)(2,1)S(1)}, bf16[2,96,2048]{2,1,0:T(8,128)(2,1)S(1)}, u32[]{:S(2)}, u32[]{:S(2)}) collective-permute-start(bf16[2,96,2048]{2,1,0:T(8,128)(2,1)S(1)} %bitcast.185), channel_id=1, source_target_pairs={{0,16},{1,17},{2,18},{3,19},{4,20},{5,21},{6,22},{7,23},{8,24},{9,... | collective-permute-start | bytes 2359304 | tf_op jit(solution)/shard_map/ppermute | solution.py:214
  248.4 18.4 %collective-permute-start.47 = (bf16[2,96,2048]{2,1,0:T(8,128)(2,1)S(1)}, bf16[2,96,2048]{2,1,0:T(8,128)(2,1)S(1)}, u32[]{:S(2)}, u32[]{:S(2)}) collective-permute-start(bf16[2,96,2048]{2,1,0:T(8,128)(2,1)S(1)} %get-tuple-element.111), channel_id=1, source_target_pairs={{0,1},{1,0},{2,3},{3,2},{4,5},{5,4},{6,7},{7,6},{8,9},{9,8},{10,11... | collective-permute-start | bytes 2359304 | tf_op jit(solution)/shard_map/ppermute | solution.py:214
  262.1 25.3 %collective-permute-start.45 = (bf16[128,2048]{1,0:T(8,128)(2,1)}, bf16[128,2048]{1,0:T(8,128)(2,1)}, u32[]{:S(2)}, u32[]{:S(2)}) collective-permute-start(bf16[128,2048]{1,0:T(8,128)(2,1)} %fusion.83), channel_id=1, source_target_pairs={{0,4},{1,5},{2,6},{3,7},{4,0},{5,1},{6,2},{7,3},{8,12},{9,13},{10,... | collective-permute-start | bytes 1572872 | tf_op jit(solution)/shard_map/ppermute | solution.py:214
  267.4 9.2 %collective-permute-start.48 = (bf16[64,2048]{1,0:T(8,128)(2,1)S(1)}, bf16[64,2048]{1,0:T(8,128)(2,1)S(1)}, u32[]{:S(2)}, u32[]{:S(2)}) collective-permute-start(bf16[64,2048]{1,0:T(8,128)(2,1)S(1)} %get-tuple-element.152), channel_id=1, source_target_pairs={{0,16},{1,17},{2,18},{3,19},{4,20},{5,21},{6,22},{7,23},{8,24},{9,... | collective-permute-start | bytes 786440 | tf_op jit(solution)/shard_map/ppermute | solution.py:214
  269.1 10.3 %collective-permute-start.50 = (bf16[64,2048]{1,0:T(8,128)(2,1)S(1)}, bf16[64,2048]{1,0:T(8,128)(2,1)S(1)}, u32[]{:S(2)}, u32[]{:S(2)}) collective-permute-start(bf16[64,2048]{1,0:T(8,128)(2,1)S(1)} %get-tuple-element.153), channel_id=1, source_target_pairs={{0,16},{1,17},{2,18},{3,19},{4,20},{5,21},{6,22},{7,23},{8,24},{9,... | collective-permute-start | bytes 786440 | tf_op jit(solution)/shard_map/ppermute | solution.py:214
  270.9 26.9 %collective-permute-start.52 = (bf16[128,2048]{1,0:T(8,128)(2,1)}, bf16[128,2048]{1,0:T(8,128)(2,1)}, u32[]{:S(2)}, u32[]{:S(2)}) collective-permute-start(bf16[128,2048]{1,0:T(8,128)(2,1)} %slice_bitcast_fusion), channel_id=1, source_target_pairs={{0,1},{1,0},{2,3},{3,2},{4,5},{5,4},{6,7},{7,6},{8,9},{9,8},{10,11... | collective-permute-start | bytes 1572872 | tf_op jit(solution)/shard_map/ppermute | solution.py:214
  280.4 11.9 %collective-permute-start.49 = (bf16[64,2048]{1,0:T(8,128)(2,1)}, bf16[64,2048]{1,0:T(8,128)(2,1)}, u32[]{:S(2)}, u32[]{:S(2)}) collective-permute-start(bf16[64,2048]{1,0:T(8,128)(2,1)} %get-tuple-element.150), channel_id=1, source_target_pairs={{0,2},{1,3},{2,0},{3,1},{4,6},{5,7},{6,4},{7,5},{8,10},{9,11},{10,... | collective-permute-start | bytes 786440 | tf_op jit(solution)/shard_map/ppermute | solution.py:214
  281.8 16.1 %collective-permute-start.51 = (bf16[64,2048]{1,0:T(8,128)(2,1)}, bf16[64,2048]{1,0:T(8,128)(2,1)}, u32[]{:S(2)}, u32[]{:S(2)}) collective-permute-start(bf16[64,2048]{1,0:T(8,128)(2,1)} %get-tuple-element.151), channel_id=1, source_target_pairs={{0,2},{1,3},{2,0},{3,1},{4,6},{5,7},{6,4},{7,5},{8,10},{9,11},{10,... | collective-permute-start | bytes 786440 | tf_op jit(solution)/shard_map/ppermute | solution.py:214
  (21 other events, 354.5 us)
